TPU v7x, 128 devices: a whole 4x4x4 slice. The times are simulated.
128 devices in a mesh: section: 2 (over core), tensor: 4 (over x), dp: 16 (over z, y).
Axes of the slice: x: 4, y: 4, z: 4, core: 2. Of those that a mesh axis runs over, the one named last changes fastest.
Arguments:
- layer_inputs: bfloat16 [2, 2, 2048, 768], P('section', None, 'dp'), may hold values from -6 to 6
- cotangent: bfloat16 [2, 2048, 768], P(None, 'dp'), may hold values from -6 to 6
- doc_groups: int32 [2, 16], replicated, may hold values from 0 to 16, as said below
- retrieved_at: int32 [2, 16, 256], P(None, 'dp'), may hold values from 0 to 2047, as said below
- sa_qkv: bfloat16 [2, 768, 3, 768], P('section', None, None, 'tensor'), may hold values from -0.21875 to 0.21875
- sa_out: bfloat16 [2, 768, 768], P('section', 'tensor'), may hold values from -0.4375 to 0.4375
- ffn_in: bfloat16 [2, 768, 3072], P('section', None, 'tensor'), may hold values from -0.21875 to 0.21875
- ffn_out: bfloat16 [2, 3072, 768], P('section', 'tensor'), may hold values from -0.109375 to 0.109375
- norm_gain: float32 [2, 2, 768], P('section'), may hold values from 0.5 to 1.5
- norm_bias: float32 [2, 2, 768], P('section'), may hold values from -1.25 to 1.25
- cross_q: bfloat16 [768, 768], P(None, 'tensor'), may hold values from -0.21875 to 0.21875
- cross_kv: bfloat16 [768, 2, 768], P(None, None, 'tensor'), may hold values from -0.21875 to 0.21875
- cross_out: bfloat16 [768, 768], P('tensor'), may hold values from -0.4375 to 0.4375
- cross_gain: float32 [768], replicated, may hold values from 0.5 to 1.5
- cross_bias: float32 [768], replicated, may hold values from -1.25 to 1.25
Outputs:
- block_out: bfloat16 [2, 2, 2048, 768], P('section', None, 'dp')
- input_grad: float32 [2, 2, 2048, 768], P('section', None, 'dp')
- grad_sa_qkv: float32 [2, 768, 3, 768], P('section', None, None, 'tensor')
- grad_sa_out: float32 [2, 768, 768], P('section', 'tensor')
- grad_ffn_in: float32 [2, 768, 3072], P('section', None, 'tensor')
- grad_ffn_out: float32 [2, 3072, 768], P('section', 'tensor')
- grad_norm_gain: float32 [2, 2, 768], P('section')
- grad_norm_bias: float32 [2, 2, 768], P('section')
- grad_cross_q: float32 [768, 768], P(None, 'tensor')
- grad_cross_kv: float32 [768, 2, 768], P(None, None, 'tensor')
- grad_cross_out: float32 [768, 768], P('tensor')
- grad_cross_gain: float32 [768], replicated
- grad_cross_bias: float32 [768], replicated
Inputs may be any that keep to these rules, and one draw needn't show every extreme that they name: `doc_groups`: group 0 starts a document; the documents of a micro-batch tile its 16 groups in order, each covering at least 256 tokens; in one micro-batch a single document covers all groups. `retrieved_at`: each entry is below the length in tokens of the document that its group belongs to; the 256 entries of one block are distinct and rising.
All inputs are finite; a program needn't handle non-finite values.
Results may differ from a plain program's by a relative error of at most 0.033.
Values may be sent and summed in bfloat16 or wider, within the bound.
A program may use at most 128 MiB of HBM per device.

v0:
```python
import jax
import jax.numpy as jnp
from jax import lax
from jax.sharding import PartitionSpec as P

HEAD = 64


epsilon = 1e-05


def from_behind(array, axis, by):
    length = lax.axis_size(axis)
    pairs = [(i, i + by) for i in range(length) if 0 <= i + by < length]
    return lax.ppermute(array, axis, pairs)


def matmul(lhs_mat, rhs_mat):
    return jnp.dot(lhs_mat, rhs_mat, preferred_element_type=jnp.float32)


def matmul_tn(lhs_mat, rhs_mat):
    return lax.dot_general(
        lhs_mat, rhs_mat, (((0,), (0,)), ((), ())), preferred_element_type=jnp.float32
    )


def matmul_nt(lhs_mat, rhs_mat):
    return lax.dot_general(
        lhs_mat, rhs_mat, (((1,), (1,)), ((), ())), preferred_element_type=jnp.float32
    )


def head_total(partial_sum):
    return lax.psum(partial_sum.astype(jnp.bfloat16), "tensor").astype(jnp.float32)


def norm_forward(residual, gain_row, bias_row):
    center = residual - jnp.mean(residual, axis=-1, keepdims=True)
    spread = lax.rsqrt(jnp.mean(center * center, axis=-1, keepdims=True) + epsilon)
    return center * spread * gain_row + bias_row


def norm_backward(residual, gain_row, upstream):
    center = residual - jnp.mean(residual, axis=-1, keepdims=True)
    spread = lax.rsqrt(jnp.mean(center * center, axis=-1, keepdims=True) + epsilon)
    normed = center * spread
    scaled = upstream * gain_row
    d_resid = spread * (
        scaled
        - jnp.mean(scaled, axis=-1, keepdims=True)
        - normed * jnp.mean(scaled * normed, axis=-1, keepdims=True)
    )
    return (d_resid, jnp.sum(upstream * normed, axis=0), jnp.sum(upstream, axis=0))


def gelu_slope(hidden):
    return (
        0.5 * (1.0 + lax.erf(hidden * 0.7071067811865476))
        + hidden * jnp.exp(-0.5 * hidden * hidden) * 0.3989422804014327
    )


def head_split(rows_block):
    return rows_block.reshape(rows_block.shape[0], -1, HEAD)


def attend(queries, key_rows, key_mask):
    scores = jnp.einsum(
        "qhe,khe->hqk", queries, key_rows, preferred_element_type=jnp.float32
    ) * HEAD ** (-0.5)
    scores = jnp.where(key_mask[None], scores, -1000000000.0)
    row_max = jnp.max(scores, axis=-1, keepdims=True)
    exponent = jnp.exp(scores - row_max)
    return exponent / jnp.sum(exponent, axis=-1, keepdims=True)


def attend_forward(queries, key_rows, value_rows, key_mask):
    attn_probs = attend(queries, key_rows, key_mask)
    attended = jnp.einsum(
        "hqk,khe->qhe",
        attn_probs.astype(jnp.bfloat16),
        value_rows,
        preferred_element_type=jnp.float32,
    )
    return attended.reshape(attended.shape[0], -1).astype(jnp.bfloat16)


def attend_backward(queries, key_rows, value_rows, key_mask, d_attended):
    attn_probs = attend(queries, key_rows, key_mask)
    d_heads = head_split(d_attended)
    d_values = jnp.einsum(
        "hqk,qhe->khe", attn_probs.astype(jnp.bfloat16), d_heads, preferred_element_type=jnp.float32
    )
    d_probs = jnp.einsum("qhe,khe->hqk", d_heads, value_rows, preferred_element_type=jnp.float32)
    d_scores = (
        attn_probs * (d_probs - jnp.sum(d_probs * attn_probs, axis=-1, keepdims=True))
    ).astype(jnp.bfloat16)
    d_queries = jnp.einsum(
        "hqk,khe->qhe", d_scores, key_rows, preferred_element_type=jnp.float32
    ) * HEAD ** (-0.5)
    d_keys = jnp.einsum(
        "hqk,qhe->khe", d_scores, queries, preferred_element_type=jnp.float32
    ) * HEAD ** (-0.5)
    return (
        d_queries.reshape(d_queries.shape[0], -1),
        d_keys.reshape(d_keys.shape[0], -1),
        d_values.reshape(d_values.shape[0], -1),
    )


def self_forward(inputs, w_qkv, w_out, gain_row, bias_row, key_mask):
    head_cols = w_out.shape[0]
    low_in = inputs.astype(jnp.bfloat16)
    packed = matmul(low_in, w_qkv.reshape(w_qkv.shape[0], -1)).astype(jnp.bfloat16)
    attended = attend_forward(
        head_split(packed[:, :head_cols]),
        head_split(packed[:, head_cols : 2 * head_cols]),
        head_split(packed[:, 2 * head_cols :]),
        key_mask,
    )
    residual = inputs + head_total(matmul(attended, w_out))
    return (norm_forward(residual, gain_row, bias_row), (low_in, packed, attended, residual))


def self_backward(stored, w_qkv, w_out, gain_row, key_mask, upstream):
    low_in, packed, attended, residual = stored
    head_cols = w_out.shape[0]
    d_resid, d_gain, d_bias = norm_backward(residual, gain_row, upstream)
    d_branch = d_resid.astype(jnp.bfloat16)
    d_w_out = matmul_tn(attended, d_branch)
    d_attended = matmul_nt(d_branch, w_out).astype(jnp.bfloat16)
    d_q, d_k, d_v = attend_backward(
        head_split(packed[:, :head_cols]),
        head_split(packed[:, head_cols : 2 * head_cols]),
        head_split(packed[:, 2 * head_cols :]),
        key_mask,
        d_attended,
    )
    d_packed = jnp.concatenate([d_q, d_k, d_v], axis=1).astype(jnp.bfloat16)
    flat_qkv = w_qkv.reshape(w_qkv.shape[0], -1)
    d_w_qkv = matmul_tn(low_in, d_packed).reshape(w_qkv.shape)
    d_inputs = d_resid + head_total(matmul_nt(d_packed, flat_qkv))
    return (d_inputs, (d_w_qkv, d_w_out, d_gain, d_bias))


def ffn_forward(inputs, w_in, w_out, gain_row, bias_row):
    low_in = inputs.astype(jnp.bfloat16)
    hidden = matmul(low_in, w_in)
    active = jax.nn.gelu(hidden, approximate=False).astype(jnp.bfloat16)
    residual = inputs + head_total(matmul(active, w_out))
    return (norm_forward(residual, gain_row, bias_row), (low_in, hidden, active, residual))


def ffn_backward(stored, w_in, w_out, gain_row, upstream):
    low_in, hidden, active, residual = stored
    d_resid, d_gain, d_bias = norm_backward(residual, gain_row, upstream)
    d_branch = d_resid.astype(jnp.bfloat16)
    d_w_out = matmul_tn(active, d_branch)
    d_hidden = (matmul_nt(d_branch, w_out) * gelu_slope(hidden)).astype(jnp.bfloat16)
    d_w_in = matmul_tn(low_in, d_hidden)
    d_inputs = d_resid + head_total(matmul_nt(d_hidden, w_in))
    return (d_inputs, (d_w_in, d_w_out, d_gain, d_bias))


def cross_forward(
    inputs,
    encoder_state_lookup,
    row_picks,
    w_query,
    pair_weight,
    w_out,
    gain_row,
    bias_row,
    decoder,
):
    head_cols = w_query.shape[1]
    low_in = inputs.astype(jnp.bfloat16)
    queries = matmul(low_in, w_query).astype(jnp.bfloat16)
    gathered_rows = jnp.take(encoder_state_lookup, row_picks, axis=0)
    paired_row_block = matmul(gathered_rows, pair_weight.reshape(pair_weight.shape[0], -1)).astype(
        jnp.bfloat16
    )
    key_mask = jnp.ones((inputs.shape[0], row_picks.shape[0]), bool)
    attended = attend_forward(
        head_split(queries),
        head_split(paired_row_block[:, :head_cols]),
        head_split(paired_row_block[:, head_cols:]),
        key_mask,
    )
    residual = inputs + head_total(matmul(attended, w_out))
    result = jnp.where(decoder, norm_forward(residual, gain_row, bias_row), inputs)
    return (result, (low_in, queries, gathered_rows, paired_row_block, attended, residual))


def cross_backward(stored, w_query, pair_weight, w_out, gain_row, decoder, upstream):
    low_in, queries, gathered_rows, paired_row_block, attended, residual = stored
    head_cols = w_query.shape[1]
    dec_share = decoder.astype(jnp.float32)
    d_resid, d_gain, d_bias = norm_backward(residual, gain_row, upstream)
    d_resid = d_resid * dec_share
    d_branch = d_resid.astype(jnp.bfloat16)
    d_w_out = matmul_tn(attended, d_branch)
    d_attended = matmul_nt(d_branch, w_out).astype(jnp.bfloat16)
    key_mask = jnp.ones((queries.shape[0], paired_row_block.shape[0]), bool)
    d_q, d_k, d_v = attend_backward(
        head_split(queries),
        head_split(paired_row_block[:, :head_cols]),
        head_split(paired_row_block[:, head_cols:]),
        key_mask,
        d_attended,
    )
    d_queries = d_q.astype(jnp.bfloat16)
    d_pair = jnp.concatenate([d_k, d_v], axis=1).astype(jnp.bfloat16)
    d_w_query = matmul_tn(low_in, d_queries)
    d_inputs = jnp.where(decoder, d_resid + head_total(matmul_nt(d_queries, w_query)), upstream)
    d_w_pair = matmul_tn(gathered_rows, d_pair).reshape(pair_weight.shape)
    d_rows = matmul_nt(d_pair, pair_weight.reshape(pair_weight.shape[0], -1))
    return (
        d_inputs,
        d_rows,
        (d_w_query, d_w_pair, d_w_out, d_gain * dec_share, d_bias * dec_share),
    )


def add_tree(running, addend):
    if running is None:
        return addend
    return jax.tree.map(jnp.add, running, addend)


def body(
    layer_inputs,
    cotangent,
    doc_groups,
    retrieved_at,
    sa_qkv,
    sa_out,
    ffn_in,
    ffn_out,
    norm_gain,
    norm_bias,
    cross_q,
    cross_kv,
    cross_out,
    cross_gain,
    cross_bias,
):
    section_id = lax.axis_index("section")
    decoder = section_id == 1
    micro_count = layer_inputs.shape[1]
    tokens = layer_inputs.shape[2]
    model_width = layer_inputs.shape[3]
    group_place = lax.axis_index("dp")
    group_ids = jnp.arange(doc_groups.shape[1], dtype=jnp.int32)
    doc_first = jnp.max(
        jnp.where((doc_groups > 0) & (group_ids <= group_place)[None, :], group_ids[None, :], 0),
        axis=1,
    )
    positions = doc_first[:, None] * tokens + retrieved_at[:, 0, :]
    token_identifiers = jnp.arange(tokens, dtype=jnp.int32)
    self_mask = (token_identifiers[None, :] <= token_identifiers[:, None]) | jnp.logical_not(
        decoder
    )
    w_qkv = sa_qkv[0]
    w_sa_out = sa_out[0]
    w_in = ffn_in[0]
    w_ff_out = ffn_out[0]
    gains = norm_gain[0]
    biases = norm_bias[0]

    def micro_of(tick_id):
        wanted = tick_id - section_id
        is_live = (wanted >= 0) & (wanted < micro_count)
        return (jnp.clip(wanted, 0, micro_count - 1), is_live)

    def forward_tick(tick_id, encoder_state_lookup):
        micro_at, is_live = micro_of(tick_id)
        inputs = lax.dynamic_index_in_dim(layer_inputs[0], micro_at, 0, keepdims=False).astype(
            jnp.float32
        )
        middle, stored_self = self_forward(inputs, w_qkv, w_sa_out, gains[0], biases[0], self_mask)
        row_picks = lax.dynamic_index_in_dim(positions, micro_at, 0, keepdims=False)
        crossed, stored_cross = cross_forward(
            middle,
            encoder_state_lookup,
            row_picks,
            cross_q,
            cross_kv,
            cross_out,
            cross_gain,
            cross_bias,
            decoder,
        )
        result, stored_ffn = ffn_forward(crossed, w_in, w_ff_out, gains[1], biases[1])
        return (result, (stored_self, stored_cross, stored_ffn))

    tables = [jnp.zeros((tokens * lax.axis_size("dp"), model_width), jnp.bfloat16)]
    out_buf = jnp.zeros((micro_count, tokens, model_width), jnp.bfloat16)
    for tick_id in range(micro_count + 1):
        micro_at, is_live = micro_of(tick_id)
        result, stored = forward_tick(tick_id, tables[tick_id])
        state_rows = result.astype(jnp.bfloat16)
        current = lax.dynamic_index_in_dim(out_buf, micro_at, 0, keepdims=False)
        out_buf = lax.dynamic_update_index_in_dim(
            out_buf, jnp.where(is_live, state_rows, current), micro_at, 0
        )
        if tick_id < micro_count:
            arrived = from_behind(state_rows, "section", 1)
            tables.append(lax.all_gather(arrived, "dp", axis=0, tiled=True))
    arriving = jnp.zeros((tokens, model_width), jnp.float32)
    in_grads = jnp.zeros((micro_count, tokens, model_width), jnp.float32)
    grads_self = None
    grads_ffn = None
    grads_cross = None
    for step_id in range(micro_count + 1):
        tick_id = micro_count - step_id
        micro_at, is_live = micro_of(tick_id)
        from_decoder = arriving
        target = lax.dynamic_index_in_dim(cotangent, micro_at, 0, keepdims=False).astype(
            jnp.float32
        )
        upstream = jnp.where(decoder, target, from_decoder) * is_live.astype(jnp.float32)
        unused, (stored_self, stored_cross, stored_ffn) = forward_tick(tick_id, tables[tick_id])
        d_crossed, part_ffn = ffn_backward(stored_ffn, w_in, w_ff_out, gains[1], upstream)
        d_middle, d_rows, part_cross = cross_backward(
            stored_cross, cross_q, cross_kv, cross_out, cross_gain, decoder, d_crossed
        )
        d_inputs, part_self = self_backward(
            stored_self, w_qkv, w_sa_out, gains[0], self_mask, d_middle
        )
        current = lax.dynamic_index_in_dim(in_grads, micro_at, 0, keepdims=False)
        in_grads = lax.dynamic_update_index_in_dim(
            in_grads, jnp.where(is_live, d_inputs, current), micro_at, 0
        )
        grads_self = add_tree(grads_self, part_self)
        grads_ffn = add_tree(grads_ffn, part_ffn)
        grads_cross = add_tree(grads_cross, part_cross)
        if step_id < micro_count:
            row_picks = lax.dynamic_index_in_dim(positions, micro_at, 0, keepdims=False)
            scattered = (
                jnp.zeros((tables[0].shape[0], model_width), jnp.float32).at[row_picks].add(d_rows)
            )
            share_rows = lax.psum_scatter(
                scattered.astype(jnp.bfloat16), "dp", scatter_dimension=0, tiled=True
            ).astype(jnp.float32)
            share_rows = head_total(share_rows)
            arriving = from_behind(share_rows.astype(jnp.bfloat16), "section", -1).astype(
                share_rows.dtype
            )
    gain_stack = jnp.stack([grads_self[2], grads_ffn[2]])
    bias_stack = jnp.stack([grads_self[3], grads_ffn[3]])
    pair_total = grads_cross[1]
    summed_stacked = (
        lax.psum(grads_self[0].astype(jnp.bfloat16), "dp").astype(jnp.float32),
        lax.psum(grads_self[1].astype(jnp.bfloat16), "dp").astype(jnp.float32),
        lax.psum(grads_ffn[0].astype(jnp.bfloat16), "dp").astype(jnp.float32),
        lax.psum(grads_ffn[1].astype(jnp.bfloat16), "dp").astype(jnp.float32),
        lax.psum(gain_stack.astype(jnp.bfloat16), "dp").astype(jnp.float32),
        lax.psum(bias_stack.astype(jnp.bfloat16), "dp").astype(jnp.float32),
        lax.psum(grads_cross[0].astype(jnp.bfloat16), "dp").astype(jnp.float32),
        lax.psum(pair_total.astype(jnp.bfloat16), "dp").astype(jnp.float32),
        lax.psum(grads_cross[2].astype(jnp.bfloat16), "dp").astype(jnp.float32),
        lax.psum(grads_cross[3].astype(jnp.bfloat16), "dp").astype(jnp.float32),
        lax.psum(grads_cross[4].astype(jnp.bfloat16), "dp").astype(jnp.float32),
    )
    summed_shared = (
        lax.psum(summed_stacked[6].astype(jnp.bfloat16), "section").astype(jnp.float32),
        lax.psum(summed_stacked[7].astype(jnp.bfloat16), "section").astype(jnp.float32),
        lax.psum(summed_stacked[8].astype(jnp.bfloat16), "section").astype(jnp.float32),
        lax.psum(summed_stacked[9].astype(jnp.bfloat16), "section").astype(jnp.float32),
        lax.psum(summed_stacked[10].astype(jnp.bfloat16), "section").astype(jnp.float32),
    )
    return (
        out_buf[None],
        in_grads[None],
        summed_stacked[0][None],
        summed_stacked[1][None],
        summed_stacked[2][None],
        summed_stacked[3][None],
        summed_stacked[4][None],
        summed_stacked[5][None],
        summed_shared[0],
        summed_shared[1],
        summed_shared[2],
        summed_shared[3],
        summed_shared[4],
    )


def solution(mesh):
    placed = (
        P("section", None, "dp", None),
        P(None, "dp", None),
        P(),
        P(None, "dp", None),
        P("section", None, None, "tensor"),
        P("section", "tensor", None),
        P("section", None, "tensor"),
        P("section", "tensor", None),
        P("section", None, None),
        P("section", None, None),
        P(None, "tensor"),
        P(None, None, "tensor"),
        P("tensor", None),
        P(),
        P(),
    )
    return jax.shard_map(
        body,
        mesh=mesh,
        in_specs=placed,
        out_specs=(
            P("section", None, "dp", None),
            P("section", None, "dp", None),
            P("section", None, None, "tensor"),
            P("section", "tensor", None),
            P("section", None, "tensor"),
            P("section", "tensor", None),
            P("section", None, None),
            P("section", None, None),
            P(None, "tensor"),
            P(None, None, "tensor"),
            P("tensor", None),
            P(),
            P(),
        ),
        check_vma=False,
    )
```

profile of v0, /device:TPU:0, one launch (start us, length us, event | category | flops | bytes accessed | tf_op | source)
XLA Modules:
  0.0 1194.3 jit_solution(11890570540454989456)
XLA Ops:
  19.8 3.8 gather_fusion
  26.3 36.9 %all-reduce.52.cloned.1.call-done = (bf16[128,768]{1,0:T(8,128)(2,1)}, bf16[128,768]{1,0:T(8,128)(2,1)}, bf16[128,768]{1,0:T(8,128)(2,1)}) async-done(((bf16[128,768]{1,0:T(8,128)(2,1)}, bf16[128,768]{1,0:T(8,128)(2,1)}, bf16[128,768]{1,0:T(8,128)(2,1)}), (bf16[128,768]{1,0:T(8,128)(2,1)}, bf16[128,768]{1,0:T(8,128)(2,1)}, bf16[128,768]{1,0:T(8,128)(2,1)})) %all-reduce.52.cloned.1.call-update) | async-done | bytes 589840 | tf_op jit(solution)/shard_map/psum | solution.py:35
  68.6 42.2 %all-reduce.24.cloned.1.call-done = bf16[128,768]{1,0:T(8,128)(2,1)} async-done(((bf16[128,768]{1,0:T(8,128)(2,1)}), bf16[128,768]{1,0:T(8,128)(2,1)}) %all-reduce.24.cloned.1.call-update) | async-done | bytes 196624 | tf_op jit(solution)/shard_map/psum | solution.py:35
  117.8 42.0 %all-reduce.26.cloned.1.call-done = bf16[128,768]{1,0:T(8,128)(2,1)} async-done(((bf16[128,768]{1,0:T(8,128)(2,1)}), bf16[128,768]{1,0:T(8,128)(2,1)}) %all-reduce.26.cloned.1.call-update) | async-done | bytes 196624 | tf_op jit(solution)/shard_map/psum | solution.py:35
  169.4 1.9 convolution_convert_fusion.37
  171.3 43.2 %all-gather.3.cloned.1.call-done = bf16[2048,768]{1,0:T(8,128)(2,1)} async-done(((bf16[128,768]{1,0:T(8,128)(2,1)}), bf16[2048,768]{1,0:T(8,128)(2,1)}) %all-gather.3.cloned.1.call-update) | async-done | bytes 3145744 | tf_op jit(solution)/shard_map/all_gather | solution.py:310
  214.5 3.8 gather_fusion.1
  224.0 2.0 fusion.288
  229.0 39.8 %all-reduce.28.cloned.1.call-done = bf16[128,768]{1,0:T(8,128)(2,1)} async-done(((bf16[128,768]{1,0:T(8,128)(2,1)}), bf16[128,768]{1,0:T(8,128)(2,1)}) %all-reduce.28.cloned.1.call-update) | async-done | bytes 196624 | tf_op jit(solution)/shard_map/psum | solution.py:35
  277.5 40.3 %all-reduce.30.cloned.1.call-done = bf16[128,768]{1,0:T(8,128)(2,1)} async-done(((bf16[128,768]{1,0:T(8,128)(2,1)}), bf16[128,768]{1,0:T(8,128)(2,1)}) %all-reduce.30.cloned.1.call-update) | async-done | bytes 196624 | tf_op jit(solution)/shard_map/psum | solution.py:35
  320.8 2.0 collective-permute-start.1
  327.0 2.0 convolution_convert_fusion.36
  329.0 43.0 %all-gather.5.cloned.1.call-done = bf16[2048,768]{1,0:T(8,128)(2,1)} async-done(((bf16[128,768]{1,0:T(8,128)(2,1)}), bf16[2048,768]{1,0:T(8,128)(2,1)}) %all-gather.5.cloned.1.call-update) | async-done | bytes 3145744 | tf_op jit(solution)/shard_map/all_gather | solution.py:310
  372.0 4.6 gather_fusion.2
  382.3 2.6 fusion.289
  384.9 2.1 convolution_convert_fusion.24
  388.8 40.2 %all-reduce.32.cloned.1.call-done = bf16[128,768]{1,0:T(8,128)(2,1)} async-done(((bf16[128,768]{1,0:T(8,128)(2,1)}), bf16[128,768]{1,0:T(8,128)(2,1)}) %all-reduce.32.cloned.1.call-update) | async-done | bytes 196624 | tf_op jit(solution)/shard_map/psum | solution.py:35
  435.4 42.0 %all-reduce.34.cloned.1.call-done = bf16[128,768]{1,0:T(8,128)(2,1)} async-done(((bf16[128,768]{1,0:T(8,128)(2,1)}), bf16[128,768]{1,0:T(8,128)(2,1)}) %all-reduce.34.cloned.1.call-update) | async-done | bytes 196624 | tf_op jit(solution)/shard_map/psum | solution.py:35
  483.5 41.8 %all-reduce.36.cloned.1.call-done = bf16[128,768]{1,0:T(8,128)(2,1)} async-done(((bf16[128,768]{1,0:T(8,128)(2,1)}), bf16[128,768]{1,0:T(8,128)(2,1)}) %all-reduce.36.cloned.1.call-update) | async-done | bytes 196624 | tf_op jit(solution)/shard_map/psum | solution.py:35
  525.2 2.3 multiply_reduce_fusion.2
  529.2 2.1 convolution_convert_fusion.20
  534.6 5.8 scatter_custom_fusion
  540.4 4.8 convert_element_type.627
  545.3 76.6 %reduce-scatter.3.cloned.1.call-done = bf16[128,768]{1,0:T(8,128)(2,1)} async-done(((bf16[2048,768]{1,0:T(8,128)(2,1)}), bf16[128,768]{1,0:T(8,128)(2,1)}) %reduce-scatter.3.cloned.1.call-update) | async-done | bytes 196624 | tf_op jit(solution)/shard_map/reduce_scatter | solution.py:344
  621.9 42.8 %all-reduce.38.cloned.1.call-done = bf16[128,768]{1,0:T(8,128)(2,1)} async-done(((bf16[128,768]{1,0:T(8,128)(2,1)}), bf16[128,768]{1,0:T(8,128)(2,1)}) %all-reduce.38.cloned.1.call-update) | async-done | bytes 196624 | tf_op jit(solution)/shard_map/psum | solution.py:35
  666.0 2.4 collective-permute-done.2
  668.4 2.0 multiply_reduce_fusion.4
  674.5 41.9 %all-reduce.40.cloned.1.call-done = bf16[128,768]{1,0:T(8,128)(2,1)} async-done(((bf16[128,768]{1,0:T(8,128)(2,1)}), bf16[128,768]{1,0:T(8,128)(2,1)}) %all-reduce.40.cloned.1.call-update) | async-done | bytes 196624 | tf_op jit(solution)/shard_map/psum | solution.py:35
  720.8 2.1 convolution_convert_fusion.19
  726.1 5.8 scatter_custom_fusion.1
  731.9 4.8 convert_element_type.649
  737.1 3.0 fusion.203
  740.2 2.0 fusion.200
  744.8 1.9 fusion.194
  751.6 61.8 %reduce-scatter.5.cloned.1.call-done = bf16[128,768]{1,0:T(8,128)(2,1)} async-done(((bf16[2048,768]{1,0:T(8,128)(2,1)}), bf16[128,768]{1,0:T(8,128)(2,1)}) %reduce-scatter.5.cloned.1.call-update) | async-done | bytes 196624 | tf_op jit(solution)/shard_map/reduce_scatter | solution.py:344
  813.5 2.2 convolution_add_fusion.4
  815.7 40.5 %all-reduce.42.cloned.1.call-done = bf16[128,768]{1,0:T(8,128)(2,1)} async-done(((bf16[128,768]{1,0:T(8,128)(2,1)}), bf16[128,768]{1,0:T(8,128)(2,1)}) %all-reduce.42.cloned.1.call-update) | async-done | bytes 196624 | tf_op jit(solution)/shard_map/psum | solution.py:35
  865.8 5.1 fusion.12
  872.4 35.7 %all-reduce.44.cloned.1.call-done = bf16[128,768]{1,0:T(8,128)(2,1)} async-done(((bf16[128,768]{1,0:T(8,128)(2,1)}), bf16[128,768]{1,0:T(8,128)(2,1)}) %all-reduce.44.cloned.1.call-update) | async-done | bytes 196624 | tf_op jit(solution)/shard_map/psum | solution.py:35
  908.1 1.9 multiply_reduce_fusion
  913.9 2.2 fusion.19
  922.5 39.6 %all-reduce.50.cloned.1.call-done = (bf16[128,768]{1,0:T(8,128)(2,1)}, bf16[128,768]{1,0:T(8,128)(2,1)}, bf16[128,768]{1,0:T(8,128)(2,1)}) async-done(((bf16[128,768]{1,0:T(8,128)(2,1)}, bf16[128,768]{1,0:T(8,128)(2,1)}, bf16[128,768]{1,0:T(8,128)(2,1)}), (bf16[128,768]{1,0:T(8,128)(2,1)}, bf16[128,768]{1,0:T(8,128)(2,1)}, bf16[128,768]{1,0:T(8,128)(2,1)})) %all-reduce.50.cloned.1.call-update) | async-done | bytes 589840 | tf_op jit(solution)/shard_map/psum | solution.py:35
  962.1 4.3 multiply_reduce_fusion.5
  979.5 1.9 convolution_convert_fusion.21
  993.3 103.8 %all-reduce.46.cloned.1.call-done = (bf16[1,768,3,192]{1,3,2,0:T(8,128)(2,1)}, bf16[1,192,768]{2,1,0:T(8,128)(2,1)}, bf16[1,768,768]{2,1,0:T(8,128)(2,1)}, bf16[...) async-done(((bf16[1,768,3,192]{1,3,2,0:T(8,128)(2,1)}, bf16[1,192,768]{2,1,0:T(8,128)(2,1)}, ...) | async-done | bytes 4718608 | tf_op jit(solution)/shard_map/psum | solution.py:355
  1097.3 72.3 %all-reduce = (bf16[1,2,768]{2,1,0:T(2,128)(2,1)S(1)}, bf16[1,2,768]{2,1,0:T(2,128)(2,1)S(1)}, bf16[768]{0:T(1024)(128)(2,1)S(1)}, bf16[768]{0:T(1024)(128)(2,1)S(1)}) all-reduce(bf16[1,2,768]{2,1,0:T(2,128)(2,1)S(1)} %maximum_bitcast_fusion, ...), channel_id=1, replica_groups=mesh['section'=2,'tensor'=4,'dp'=16] {'dp'}, use_global_device_ids=true, to_apply=%region_89.91 | all-reduce | flops 4608 | bytes 18432 | tf_op jit(solution)/shard_map/psum | solution.py:359
  1169.6 2.4 all-reduce.5
  1183.1 2.2 convert_element_type.677
  (773 shorter events, 163.9 us)
Async XLA Ops:
  7.2 107.5 %copy-start = (bf16[1,768,768]{2,1,0:T(8,128)(2,1)S(1)}, bf16[1,768,768]{2,1,0:T(8,128)(2,1)}, u32[]{:S(2)}) copy-start(bf16[1,768,768]{2,1,0:T(8,128)(2,1)} %param.23) | copy-start | bytes 3538948
  7.2 56.0 %all-reduce.52.cloned.1.call-start = ((), (), s32[]{:S(2)}) async-start(), calls=%async_computation.20 | async-start | bytes 1179648 | tf_op jit(solution)/shard_map/psum | solution.py:35
  9.2 6.6 copy-start.183
  17.1 93.7 %all-reduce.24.cloned.1.call-start = ((), (), s32[]{:S(2)}) async-start(), calls=%async_computation.2 | async-start | bytes 393216 | tf_op jit(solution)/shard_map/psum | solution.py:35
  17.4 6.2 copy-start.247
  67.6 45.5 %copy-start.102 = (f32[768]{0:T(1024)S(1)}, f32[768]{0:T(1024)}, u32[]{:S(2)}) copy-start(f32[768]{0:T(1024)} %param.30) | copy-start | bytes 9220
  68.6 91.2 %all-reduce.26.cloned.1.call-start = ((), (), s32[]{:S(2)}) async-start(), calls=%async_computation.3 | async-start | bytes 393216 | tf_op jit(solution)/shard_map/psum | solution.py:35
  117.8 43.9 %copy-start.151 = (f32[768]{0:T(1024)S(1)}, f32[768]{0:T(1024)}, u32[]{:S(2)}) copy-start(f32[768]{0:T(1024)} %get-tuple-element.61) | copy-start | bytes 9220
  117.8 96.7 %all-gather.3.cloned.1.call-start = ((), (), s32[]{:S(2)}) async-start(), calls=%async_computation.4 | async-start | bytes 3342336 | tf_op jit(solution)/shard_map/all_gather | solution.py:310
  162.6 2.3 collective-permute-start
  165.7 103.1 %all-reduce.28.cloned.1.call-start = ((), (), s32[]{:S(2)}) async-start(), calls=%async_computation.5 | async-start | bytes 393216 | tf_op jit(solution)/shard_map/psum | solution.py:35
  218.3 5.7 copy-start.80
  228.5 89.4 %all-reduce.30.cloned.1.call-start = ((), (), s32[]{:S(2)}) async-start(), calls=%async_computation.6 | async-start | bytes 393216 | tf_op jit(solution)/shard_map/psum | solution.py:35
  275.8 96.2 %all-gather.5.cloned.1.call-start = ((), (), s32[]{:S(2)}) async-start(), calls=%async_computation.7 | async-start | bytes 3342336 | tf_op jit(solution)/shard_map/all_gather | solution.py:310
  320.8 2.5 collective-permute-start.1
  323.3 105.8 %all-reduce.32.cloned.1.call-start = ((), (), s32[]{:S(2)}) async-start(), calls=%async_computation.8 | async-start | bytes 393216 | tf_op jit(solution)/shard_map/psum | solution.py:35
  388.7 88.6 %all-reduce.34.cloned.1.call-start = ((), (), s32[]{:S(2)}) async-start(), calls=%async_computation.9 | async-start | bytes 393216 | tf_op jit(solution)/shard_map/psum | solution.py:35
  435.3 89.9 %all-reduce.36.cloned.1.call-start = ((), (), s32[]{:S(2)}) async-start(), calls=%async_computation.10 | async-start | bytes 393216 | tf_op jit(solution)/shard_map/psum | solution.py:35
  483.2 138.6 %reduce-scatter.3.cloned.1.call-start = ((), (), s32[]{:S(2)}) async-start(), calls=%async_computation.11 | async-start | bytes 3342336 | tf_op jit(solution)/shard_map/reduce_scatter | solution.py:344
  545.2 119.5 %all-reduce.38.cloned.1.call-start = ((), (), s32[]{:S(2)}) async-start(), calls=%async_computation.12 | async-start | bytes 393216 | tf_op jit(solution)/shard_map/psum | solution.py:35
  621.9 94.5 %all-reduce.40.cloned.1.call-start = ((), (), s32[]{:S(2)}) async-start(), calls=%async_computation.13 | async-start | bytes 393216 | tf_op jit(solution)/shard_map/psum | solution.py:35
  664.7 3.7 collective-permute-start.2
  666.0 5.8 copy-start.7
  666.0 5.8 copy-start.104
  674.4 139.0 %reduce-scatter.5.cloned.1.call-start = ((), (), s32[]{:S(2)}) async-start(), calls=%async_computation.14 | async-start | bytes 3342336 | tf_op jit(solution)/shard_map/reduce_scatter | solution.py:344
  736.8 119.4 %all-reduce.42.cloned.1.call-start = ((), (), s32[]{:S(2)}) async-start(), calls=%async_computation.15 | async-start | bytes 393216 | tf_op jit(solution)/shard_map/psum | solution.py:35
  813.4 94.7 %all-reduce.44.cloned.1.call-start = ((), (), s32[]{:S(2)}) async-start(), calls=%async_computation.16 | async-start | bytes 393216 | tf_op jit(solution)/shard_map/psum | solution.py:35
  856.2 6.8 copy-start.8
  856.2 6.8 copy-start.78
  856.2 3.7 collective-permute-start.3
  865.7 96.3 %all-reduce.50.cloned.1.call-start = ((), (), s32[]{:S(2)}) async-start(), calls=%async_computation.19 | async-start | bytes 1179648 | tf_op jit(solution)/shard_map/psum | solution.py:35
  865.7 5.1 copy-start.29
  865.7 5.1 copy-start.30
  865.8 5.1 copy-start.35
  865.8 5.1 copy-start.62
  917.9 179.2 %all-reduce.46.cloned.1.call-start = ((), (), s32[]{:S(2)}) async-start(), calls=%async_computation.17 | async-start | bytes 9437184 | tf_op jit(solution)/shard_map/psum | solution.py:355
  921.2 40.8 %copy-start.22 = (bf16[128,768]{1,0:T(8,128)(2,1)S(1)}, bf16[128,768]{1,0:T(8,128)(2,1)}, u32[]{:S(2)}) copy-start(bf16[128,768]{1,0:T(8,128)(2,1)} %get-tuple-element.81) | copy-start | bytes 589828
  921.2 40.8 %copy-start.166 = (f32[128]{0:T(128)S(1)}, f32[128]{0:T(128)}, u32[]{:S(2)}) copy-start(f32[128]{0:T(128)} %copy-done.163) | copy-start | bytes 1540
  962.0 4.4 copy-start.28
  962.0 4.4 copy-start.169
  962.0 4.4 copy-start.171
  962.1 4.4 copy-start.197
  962.1 4.4 copy-start.200
  986.7 187.8 %all-reduce.48.cloned.1.call-start = ((), (), s32[]{:S(2)}) async-start(), calls=%async_computation.18 | async-start | bytes 1179648 | tf_op jit(solution)/shard_map/psum | solution.py:35
  993.1 104.1 %copy-start.184 = (f32[768]{0:T(1024)S(1)}, f32[768]{0:T(1024)}, u32[]{:S(2)}) copy-start(f32[768]{0:T(1024)} %get-tuple-element.18) | copy-start | bytes 9220
  993.1 104.1 %copy-start.185 = (f32[768]{0:T(1024)S(1)}, f32[768]{0:T(1024)}, u32[]{:S(2)}) copy-start(f32[768]{0:T(1024)} %get-tuple-element.41) | copy-start | bytes 9220
  993.1 104.1 %copy-start.186 = (f32[768]{0:T(1024)S(1)}, f32[768]{0:T(1024)}, u32[]{:S(2)}) copy-start(f32[768]{0:T(1024)} %get-tuple-element.44) | copy-start | bytes 9220
  993.2 189.9 %all-reduce.54.cloned.1.call-start = ((), (), s32[]{:S(2)}) async-start(), calls=%async_computation.21 | async-start | bytes 2359296 | tf_op jit(solution)/shard_map/psum | solution.py:368
  (228 other events, 416.4 us)
Sparse Core Ops, SparseCore 0:
  17.2 45.9 all-reduce.51
  68.7 42.0 all-reduce.23
  117.9 41.8 all-reduce.25
  165.8 48.6 all-gather.2
  228.6 40.1 all-reduce.27
  276.0 41.8 all-reduce.29
  323.4 48.6 all-gather.4
  388.9 40.1 all-reduce.31
  435.5 41.8 all-reduce.33
  483.3 41.8 all-reduce.35
  545.3 76.4 reduce-scatter.2
  624.1 40.4 all-reduce.37
  674.5 41.8 all-reduce.39
  736.9 76.4 reduce-scatter.4
  815.7 40.4 all-reduce.41
  865.8 42.2 all-reduce.43
  918.1 43.9 all-reduce.49
  986.8 110.3 all-reduce.45
  1099.7 43.1 all-reduce.47
  1145.4 26.2 all-reduce.53
where the time goes:
time: 1210 us; the launch traced here: 1190 us
  waiting for transfers between devices  859 us (71%)
  matrix products  109 us (9%)
  other arithmetic  77.4 us (6%)
  blocking collectives  74.8 us (6%)
  local copies, waits for them, and re-layouts  48.3 us (4%)
  between operations  17.8 us (1%)
    psum x14, waiting for transfers between devices, head_total(): lax.psum(partial_sum.astype(jnp.bfloat16), 'tensor').astype(jnp.float32)  526 us
    reduce_scatter x2, waiting for transfers between devices, body(): lax.psum_scatter(scattered.astype(jnp.bfloat16), 'dp', scatter_dimension=...  138 us
    psum x1, waiting for transfers between devices, body(): lax.psum(grads_self[0].astype(jnp.bfloat16), 'dp').astype(jnp.float32)  104 us
    all_gather x2, waiting for transfers between devices, body(): tables.append(lax.all_gather(arrived, 'dp', axis=0, tiled=True))  86.2 us
    psum x1, blocking collectives, body(): lax.psum(gain_stack.astype(jnp.bfloat16), 'dp').astype(jnp.float32)  72.3 us
    dot_general x21, matrix products, matmul_tn(): lax.dot_general(lhs_mat, rhs_mat, (((0,), (0,)), ((), ())), preferred_ele...  33.8 us
    dot_general x21, matrix products, matmul(): return jnp.dot(lhs_mat, rhs_mat, preferred_element_type=jnp.float32)  24.4 us
  transfers between devices with their start and end apart: 24, of which 22 were waited for; matrix products, arithmetic and copies ran while one was open for 5% of the time, Pallas kernels for 0%

commit v1 on v0

v1 whole, which is shorter than its diff:
```python
import jax
import jax.numpy as jnp
from jax import lax
from jax.experimental import pallas as pl
from jax.experimental.pallas import tpu as pltpu
from jax.sharding import PartitionSpec as P

BF = jnp.bfloat16
F32 = jnp.float32
MESH = pl.DeviceIdType.MESH
VMEM = pltpu.VMEM
DMA = pltpu.SemaphoreType.DMA

HEAD = 64
NH = 3
EPS = 1e-05
SCALE = HEAD**-0.5
TOK = 128
D = 768
SH = 32
KEYS = 256
QW = NH * HEAD
RINGS = (2, 1, 3)

A_BO, A_IG, A_Y1, A_Y2, A_DR2, A_DRC, A_DR1 = 0, 2, 4, 6, 7, 9, 10
N_AG = 12
R_SA, R_FF, R_CR, R_DFF, R_DQ, R_DSA, R_DST = 0, 2, 4, 5, 7, 8, 10
N_RS = 11
BLOCKS = {"ffd": 768, "ffe": 768, "crx": 384, "sad": 384, "sae": 384}


def nn(a, b):
    return jnp.dot(a, b, preferred_element_type=F32)


def nt(a, b):
    return lax.dot_general(a, b, (((1,), (1,)), ((), ())), preferred_element_type=F32)


def tn(a, b):
    return lax.dot_general(a, b, (((0,), (0,)), ((), ())), preferred_element_type=F32)


def scratch_list():
    out = [
        ("xin", VMEM((2, TOK, D), BF)),
        ("nv", VMEM((2, 8, D), F32)),
        ("wsa", VMEM((2, 768, D), BF)),
        ("wff", VMEM((2, 2, 768, D), BF)),
        ("wcr", VMEM((768, D), BF)),
        ("cot", VMEM((TOK, D), BF)),
        ("pk", VMEM((2, 3 * QW, TOK), BF)),
        ("pt", VMEM((2, NH, TOK, TOK), F32)),
        ("ot", VMEM((2, QW, TOK), BF)),
        ("n1", VMEM((2, SH, D), F32)),
        ("n2", VMEM((2, SH, D), F32)),
        ("nc", VMEM((SH, D), F32)),
        ("sp", VMEM((5, SH, 128), F32)),
        ("y1f", VMEM((2, SH, D), F32)),
        ("y2f", VMEM((SH, D), F32)),
        ("dres", VMEM((2, SH, D), F32)),
        ("act", VMEM((2, TOK, D), BF)),
        ("slope", VMEM((2, TOK, D), F32)),
        ("du", VMEM((2, TOK, D), BF)),
        ("dpk", VMEM((2, 3 * QW, TOK), BF)),
        ("qct", VMEM((QW, TOK), BF)),
        ("dqct", VMEM((QW, TOK), BF)),
        ("kvct", VMEM((2 * QW, KEYS), BF)),
        ("dkvct", VMEM((2 * QW, KEYS), BF)),
        ("ptc", VMEM((NH, KEYS, TOK), F32)),
        ("oct", VMEM((QW, TOK), BF)),
        ("hot", VMEM((16 * TOK, KEYS), BF)),
        ("kvt", VMEM((16, 2 * QW, TOK), BF)),
        ("dks", VMEM((16, 2 * QW, TOK), BF)),
        ("dk1", VMEM((3, 4, 2 * QW, TOK), BF)),
        ("dk2", VMEM((3, 2 * QW, TOK), BF)),
        ("dkv", VMEM((2 * QW, TOK), BF)),
        ("vec", VMEM((16, D), F32)),
        ("vx", VMEM((4, 16, D), F32)),
        ("vc", VMEM((2, 16, D), F32)),
        ("vy", VMEM((4, 16, D), F32)),
        ("vz", VMEM((4, 16, D), F32)),
        ("ag", VMEM((N_AG, TOK, D), BF)),
        ("rs", VMEM((N_RS, TOK, D), BF)),
        ("rr", VMEM((N_RS, 3, SH, D), BF)),
        ("bor", VMEM((TOK, D), BF)),
        ("igr", VMEM((TOK, D), BF)),
        ("gof", VMEM((2, 2, 768, 384), BF)),
        ("gos", VMEM((2, 2, 384, 384), BF)),
        ("goc", VMEM((2, 384, 384), BF)),
        ("gtf", VMEM((2, 768, 384), BF)),
        ("gts", VMEM((2, 384, 384), BF)),
        ("gtc", VMEM((2, 384, 384), BF)),
        ("m_w", DMA((2, 6))),
        ("m_ws", DMA((6,))),
        ("m_l", DMA((4,))),
        ("m_ags", DMA((N_AG, 3))),
        ("m_agr", DMA((N_AG, 3))),
        ("m_rss", DMA((N_RS, 3))),
        ("m_rsr", DMA((N_RS, 3))),
        ("m_kvs", DMA((15,))),
        ("m_kvr", DMA((15,))),
        ("m_dks", DMA((6,))),
        ("m_dkr", DMA((6,))),
        ("m_vs", DMA((10,))),
        ("m_vr", DMA((10,))),
        ("m_hs", DMA((5,))),
        ("m_hr", DMA((5,))),
    ]
    for name, rows in BLOCKS.items():
        out += [
            ("g_" + name, VMEM((2, 2, rows, 384), BF)),
            ("x_" + name, VMEM((2, rows, 384), BF)),
            ("a_" + name, VMEM((3, 2, rows // 4, 384), BF)),
            ("b_" + name, VMEM((3, rows // 8, 384), BF)),
            ("s_" + name, DMA((13,))),
            ("r_" + name, DMA((13,))),
        ]
    return out


class Refs:
    pass


def ln_forward(r, gain, bias):
    center = r - jnp.mean(r, axis=-1, keepdims=True)
    spread = lax.rsqrt(jnp.mean(center * center, axis=-1, keepdims=True) + EPS)
    n = center * spread
    return n * gain + bias, n, spread


def ln_backward(n, spread, gain, dy):
    s = dy * gain
    dr = spread * (
        s - jnp.mean(s, axis=-1, keepdims=True) - n * jnp.mean(s * n, axis=-1, keepdims=True)
    )
    return dr, jnp.sum(dy * n, axis=0, keepdims=True), jnp.sum(dy, axis=0, keepdims=True)


def kernel(names, n_in, n_out, *refs):
    (x_h, cot_h, dgr, ret, nrm_h, qkv_h, out_h, win_h, wfo_h, cq_h, ckv_h, co_h) = refs[:n_in]
    bo_o, ig_o, of_o, os_o, oc_o, on_o, oe_o = refs[n_in : n_in + n_out]
    R = Refs()
    for name, ref in zip(names, refs[n_in + n_out :]):
        setattr(R, name, ref)
    c = lax.axis_index("section")
    t = lax.axis_index("tensor")
    d = lax.axis_index("dp")
    o = 1 - c
    y = lax.rem(d, 4)
    z = d // 4
    p = y + c * (z - y)
    q = z + c * (y - z)
    sp, sq = 1 + 3 * c, 4 - 3 * c
    rows_t = pl.ds(pl.multiple_of(t * SH, SH), SH)

    def dev_x(k):
        return (c, lax.rem(t + k, 4), d)

    def dev_p(k):
        return (c, t, lax.rem(p + k, 4) * sp + q * sq)

    def dev_q(k):
        return (c, t, p * sp + lax.rem(q + k, 4) * sq)

    def dev_y(k):
        return (c, t, z * 4 + lax.rem(y + k, 4))

    def dev_z(k):
        return (c, t, lax.rem(z + k, 4) * 4 + y)

    dev_c = (o, t, d)
    sends = []

    def push(src, dst, ss, rs, dev):
        cp = pltpu.make_async_remote_copy(
            src_ref=src, dst_ref=dst, send_sem=ss, recv_sem=rs, device_id=dev, device_id_type=MESH
        )
        cp.start()
        sends.append(cp)
        return cp

    def landed(dst, rs, dev):
        pltpu.make_async_remote_copy(
            src_ref=dst, dst_ref=dst, send_sem=rs, recv_sem=rs, device_id=dev, device_id_type=MESH
        ).wait_recv()

    items = [
        (x_h.at[c], R.xin.at[c]),
        (nrm_h, R.nv.at[c]),
        (qkv_h, R.wsa.at[c, pl.ds(0, 576)]),
        (out_h, R.wsa.at[c, pl.ds(576, 192)]),
        (win_h, R.wff.at[c, 0]),
        (wfo_h, R.wff.at[c, 1]),
    ]

    def own(i):
        pltpu.make_async_copy(items[i][0], items[i][1], R.m_w.at[c, i]).start()

    def other(i):
        src = x_h.at[o] if i == 0 else items[i][0]
        push(src, items[i][1], R.m_ws.at[i], R.m_w.at[c, i], dev_c)

    for i in range(4):
        own(i)
    singles = [
        pltpu.make_async_copy(cq_h, R.wcr.at[pl.ds(0, 192)], R.m_l.at[0]),
        pltpu.make_async_copy(co_h, R.wcr.at[pl.ds(192, 192)], R.m_l.at[1]),
        pltpu.make_async_copy(ckv_h, R.wcr.at[pl.ds(384, 384)], R.m_l.at[2]),
        pltpu.make_async_copy(cot_h.at[c], R.cot, R.m_l.at[3]),
    ]
    for cp in singles:
        cp.start()
    own(4)
    own(5)
    bar = pltpu.get_barrier_semaphore()
    peers = [f(k) for f in (dev_x, dev_y, dev_z) for k in (1, 2, 3)] + [dev_c]
    for dev in peers:
        pl.semaphore_signal(bar, inc=1, device_id=dev, device_id_type=MESH)
    pl.semaphore_wait(bar, len(peers))
    for i in range(6):
        other(i)

    def need(s, i):
        src = x_h.at[s] if i == 0 else items[i][0]
        dst = [
            R.xin.at[s],
            R.nv.at[s],
            R.wsa.at[s, pl.ds(0, 576)],
            R.wsa.at[s, pl.ds(576, 192)],
            R.wff.at[s, 0],
            R.wff.at[s, 1],
        ][i]
        pltpu.make_async_copy(src, dst, R.m_w.at[s, i]).wait()

    def rs_start(i, value):
        R.rs[i] = value.astype(BF)
        for k in RINGS:
            to = lax.rem(t + k, 4)
            push(
                R.rs.at[i, pl.ds(pl.multiple_of(to * SH, SH), SH)],
                R.rr.at[i, k - 1],
                R.m_rss.at[i, k - 1],
                R.m_rsr.at[i, k - 1],
                dev_x(k),
            )

    def rs_sum(i):
        for k in (1, 3, 2):
            landed(R.rr.at[i, k - 1], R.m_rsr.at[i, k - 1], dev_x(k))
        total = R.rs[i, rows_t, :].astype(F32)
        for k in range(3):
            total += R.rr[i, k].astype(F32)
        return total

    def ag_start(i, value):
        R.ag[i, rows_t, :] = value.astype(BF)
        for k in RINGS:
            push(
                R.ag.at[i, rows_t],
                R.ag.at[i, rows_t],
                R.m_ags.at[i, k - 1],
                R.m_agr.at[i, k - 1],
                dev_x(k),
            )

    def ag_wait(i):
        for k in (1, 3, 2):
            landed(R.ag.at[i, rows_t], R.m_agr.at[i, k - 1], dev_x(k))

    def norm_row(s, i):
        return R.nv[s, pl.ds(i, 1), :]

    def self_forward(s):
        need(s, 0)
        need(s, 2)
        R.pk[s] = nt(R.wsa[s, 0:576, :], R.xin[s]).astype(BF)
        for h in range(NH):
            qt = R.pk[s, h * 64 : h * 64 + 64, :]
            kt = R.pk[s, QW + h * 64 : QW + h * 64 + 64, :]
            vt = R.pk[s, 2 * QW + h * 64 : 2 * QW + h * 64 + 64, :]
            st = tn(kt, qt) * SCALE
            if s == 1:
                key = lax.broadcasted_iota(jnp.int32, (TOK, TOK), 0)
                qry = lax.broadcasted_iota(jnp.int32, (TOK, TOK), 1)
                st = jnp.where(key <= qry, st, -1000000000.0)
            e = jnp.exp(st - jnp.max(st, axis=0, keepdims=True))
            pr = e / jnp.sum(e, axis=0, keepdims=True)
            R.pt[s, h] = pr
            R.ot[s, h * 64 : h * 64 + 64, :] = nn(vt, pr.astype(BF)).astype(BF)
        need(s, 3)
        rs_start(R_SA + s, tn(R.ot[s], R.wsa[s, 576:768, :]))

    def put_norm(slot, spread):
        R.sp[slot] = jnp.broadcast_to(spread, (SH, 128))

    def get_norm(slot):
        return R.sp[slot, :, 0:1]

    def self_finish(s):
        total = rs_sum(R_SA + s)
        r = R.xin[s, rows_t, :].astype(F32) + total
        need(s, 1)
        out, n, spread = ln_forward(r, norm_row(s, 0), norm_row(s, 2))
        ag_start(A_Y1 + s, out)
        R.y1f[s] = out
        R.n1[s] = n
        put_norm(s, spread)

    def ffn_forward(s, gathered):
        u = nn(R.ag[gathered], R.wff[s, 0])
        cdf = 0.5 * (1.0 + lax.erf(u * 0.7071067811865476))
        R.act[s] = (u * cdf).astype(BF)
        R.slope[s] = cdf + u * jnp.exp(-0.5 * u * u) * 0.3989422804014327
        rs_start(R_FF + s, nn(R.act[s], R.wff[s, 1]))

    def ffn_backward(s):
        ag_wait(A_DR2 + s)
        dg = nt(R.ag[A_DR2 + s], R.wff[s, 1])
        R.du[s] = (dg * R.slope[s]).astype(BF)
        rs_start(R_DFF + s, nt(R.du[s], R.wff[s, 0]))

    def put(ref, piece, r0, value):
        rows = value.shape[0]
        ref[piece, 0, r0 : r0 + rows, :] = value[:, 0:384].astype(BF)
        ref[piece, 1, r0 : r0 + rows, :] = value[:, 384:768].astype(BF)

    def ffn_grads(s, gathered, ref):
        put(ref, 0, 0, tn(R.ag[gathered], R.du[s]))
        put(ref, 1, 0, tn(R.act[s], R.ag[A_DR2 + s]))

    def blk(name):
        return tuple(getattr(R, pre + name) for pre in ("g_", "x_", "a_", "b_", "s_", "r_"))

    goal = {
        "ffd": R.gof.at[1],
        "ffe": R.gof.at[0],
        "sad": R.gos.at[1],
        "sae": R.gos.at[0],
        "crx": R.goc,
    }

    def g0(name):
        g, x, a, b, s, r = blk(name)
        push(g.at[o], x, s.at[0], r.at[0], dev_c)

    def p_rows(name, at):
        quarter = BLOCKS[name] // 4
        return pl.ds(pl.multiple_of(at * quarter, quarter), quarter)

    def q_rows(name, at_p, at_q):
        quarter, eighth = BLOCKS[name] // 4, BLOCKS[name] // 8
        return pl.ds(pl.multiple_of(at_p * quarter + (at_q // 2) * eighth, eighth), eighth)

    def g1(name):
        g, x, a, b, s, r = blk(name)
        landed(x, r.at[0], dev_c)
        g[c] = (g[c].astype(F32) + x[...].astype(F32)).astype(BF)
        for k in RINGS:
            to = lax.rem(p + k, 4)
            push(
                g.at[c, :, p_rows(name, to)], a.at[k - 1], s.at[k], r.at[k], dev_p(k)
            )

    def g2(name):
        g, x, a, b, s, r = blk(name)
        for k in (1, 3, 2):
            landed(a.at[k - 1], r.at[k], dev_p(k))
        mine = p_rows(name, p)
        total = g[c, :, mine, :].astype(F32)
        for k in range(3):
            total += a[k].astype(F32)
        g[c, :, mine, :] = total.astype(BF)
        for k in RINGS:
            to = lax.rem(q + k, 4)
            push(
                g.at[c, lax.rem(to, 2), q_rows(name, p, to)],
                b.at[k - 1],
                s.at[3 + k],
                r.at[3 + k],
                dev_q(k),
            )

    def g3(name):
        g, x, a, b, s, r = blk(name)
        for k in (1, 3, 2):
            landed(b.at[k - 1], r.at[3 + k], dev_q(k))
        rows, half = q_rows(name, p, q), lax.rem(q, 2)
        total = g[c, half, rows, :].astype(F32)
        for k in range(3):
            total += b[k].astype(F32)
        fin = goal[name]
        fin[half, rows, :] = total.astype(BF)
        for k in RINGS:
            push(fin.at[half, rows], fin.at[half, rows], s.at[6 + k], r.at[6 + k], dev_q(k))

    def g4(name):
        g, x, a, b, s, r = blk(name)
        fin = goal[name]
        for k in (1, 3, 2):
            landed(fin.at[lax.rem(q, 2), q_rows(name, p, q)], r.at[6 + k], dev_q(k))
        mine = p_rows(name, p)
        for k in RINGS:
            push(fin.at[:, mine], fin.at[:, mine], s.at[9 + k], r.at[9 + k], dev_p(k))

    def g5(name):
        g, x, a, b, s, r = blk(name)
        fin = goal[name]
        for k in (1, 3, 2):
            landed(fin.at[:, p_rows(name, p)], r.at[9 + k], dev_p(k))

    def vec_put(row, dg, db, step=2):
        R.vec[row : row + 1, :] = dg
        R.vec[row + step : row + step + 1, :] = db

    def vec_send(buf, at, value, base, dev, count):
        buf[at] = value
        for k in range(1, count):
            push(buf.at[at], buf.at[at], R.m_vs.at[base + k - 1], R.m_vr.at[base + k - 1], dev(k))

    def vec_sum(buf, at, base, dev, count):
        for k in range(1, count):
            landed(buf.at[at], R.m_vr.at[base + k - 1], dev(k))
        total = buf[0]
        for k in range(1, count):
            total += buf[k]
        return total

    def dev_c1(k):
        return dev_c

    for j in (10, 11, 12, 13, 14, 15):
        R.vec[j : j + 1, :] = jnp.zeros((1, D), F32)
    self_forward(0)
    self_forward(1)
    self_finish(0)
    self_finish(1)
    ag_wait(A_Y1)
    need(0, 4)
    need(0, 5)
    ffn_forward(0, A_Y1)

    for cp in singles:
        cp.wait()
    ag_wait(A_Y1 + 1)
    R.qct[...] = nt(R.wcr[0:192, :], R.ag[A_Y1 + 1]).astype(BF)
    micro = lax.broadcasted_iota(jnp.int32, (2, 16), 0)
    group = lax.broadcasted_iota(jnp.int32, (2, 16), 1)
    live = (micro == c) & (group <= d) & (dgr[...] > 0)
    first = jnp.max(jnp.where(live, group, 0), axis=1, keepdims=True)
    first = jnp.max(first, axis=0, keepdims=True)
    pick = lax.broadcasted_iota(jnp.int32, (2, KEYS), 0) == c
    rows = jnp.max(jnp.where(pick, ret[...], 0), axis=0, keepdims=True) + first * TOK
    g_at = rows // TOK
    b_at = jnp.where(c == 0, g_at, lax.rem(g_at, 4) * 4 + g_at // 4)
    at = b_at * TOK + lax.rem(rows, TOK)

    def build(i, carry):
        n = lax.broadcasted_iota(jnp.int32, (TOK, KEYS), 0) + i * TOK
        R.hot[pl.ds(pl.multiple_of(i * TOK, TOK), TOK), :] = jnp.where(n == at, 1.0, 0.0).astype(BF)
        return carry

    lax.fori_loop(0, 16, build, 0)

    out, n, spread = ln_forward(R.y1f[0] + rs_sum(R_FF), norm_row(0, 1), norm_row(0, 3))
    ag_start(A_BO, out)
    R.n2[0] = n
    put_norm(2, spread)
    ag_wait(A_BO)
    mine = q * 4 + p
    R.kvt[mine] = nt(R.wcr[384:768, :], R.ag[A_BO]).astype(BF)

    def kv_send(k, dev, slot, at_block):
        push(R.kvt.at[at_block], R.kvt.at[at_block], R.m_kvs.at[slot], R.m_kvr.at[slot], dev)

    for k in RINGS:
        kv_send(k, dev_p(k), k - 1, mine)
    for k in RINGS:
        kv_send(k, dev_q(k), 2 + k, mine)
    for j in (1, 3, 2):
        landed(R.kvt.at[mine], R.m_kvr.at[j - 1], dev_p(j))
        came = q * 4 + lax.rem(p + 4 - j, 4)
        for k in RINGS:
            kv_send(k, dev_q(k), 6 + (j - 1) * 3 + k - 1, came)
    for slot in range(3, 15):
        landed(R.kvt.at[mine], R.m_kvr.at[slot], dev_q(1))

    def gather(i, total):
        pair = jnp.concatenate([R.kvt[2 * i], R.kvt[2 * i + 1]], axis=1)
        return total + nn(pair, R.hot[pl.ds(pl.multiple_of(i * 256, 256), 256), :])

    R.kvct[...] = lax.fori_loop(0, 8, gather, jnp.zeros((2 * QW, KEYS), F32)).astype(BF)
    for h in range(NH):
        lo = h * 64
        st = tn(R.kvct[lo : lo + 64, :], R.qct[lo : lo + 64, :]) * SCALE
        e = jnp.exp(st - jnp.max(st, axis=0, keepdims=True))
        pr = e / jnp.sum(e, axis=0, keepdims=True)
        R.ptc[h] = pr
        R.oct[lo : lo + 64, :] = nn(R.kvct[QW + lo : QW + lo + 64, :], pr.astype(BF)).astype(BF)
    rs_start(R_CR, tn(R.oct[...], R.wcr[192:384, :]))
    need(1, 4)
    need(1, 5)
    out, n, spread = ln_forward(R.y1f[1] + rs_sum(R_CR), norm_row(0, 4), norm_row(0, 5))
    ag_start(A_Y2, out)
    R.y2f[...] = out
    R.nc[...] = n
    put_norm(4, spread)
    ag_wait(A_Y2)
    ffn_forward(1, A_Y2)
    out, n, spread = ln_forward(R.y2f[...] + rs_sum(R_FF + 1), norm_row(1, 1), norm_row(1, 3))

    dr, dg, db = ln_backward(n, spread, norm_row(1, 1), R.cot[rows_t, :].astype(F32))
    ag_start(A_DR2 + 1, dr)
    R.dres[1] = dr
    vec_put(5, dg, db)
    ag_start(A_BO + 1, out)
    ffn_backward(1)
    ffn_grads(1, A_Y2, R.g_ffd)
    g0("ffd")
    dy = R.dres[1] + rs_sum(R_DFF + 1)
    dr, dg, db = ln_backward(R.nc[...], get_norm(4), norm_row(0, 4), dy)
    ag_start(A_DRC, dr)
    R.dres[1] = dr
    vec_put(8, dg, db, 1)
    g1("ffd")
    ag_wait(A_DRC)

    def attend_backward(qt, kt, vt, pr, dot):
        dvt = nt(dot, pr.astype(BF))
        dpt = tn(vt, dot)
        dst = (pr * (dpt - jnp.sum(dpt * pr, axis=0, keepdims=True))).astype(BF)
        return nn(kt, dst) * SCALE, nt(qt, dst) * SCALE, dvt

    doc = nt(R.wcr[192:384, :], R.ag[A_DRC]).astype(BF)
    for h in range(NH):
        lo = h * 64
        dqt, dkt, dvt = attend_backward(
            R.qct[lo : lo + 64, :],
            R.kvct[lo : lo + 64, :],
            R.kvct[QW + lo : QW + lo + 64, :],
            R.ptc[h],
            doc[lo : lo + 64, :],
        )
        R.dqct[lo : lo + 64, :] = dqt.astype(BF)
        R.dkvct[lo : lo + 64, :] = dkt.astype(BF)
        R.dkvct[QW + lo : QW + lo + 64, :] = dvt.astype(BF)

    def scatter(i, carry):
        part = nt(R.dkvct[...], R.hot[pl.ds(pl.multiple_of(i * TOK, TOK), TOK), :])
        R.dks[i] = part.astype(BF)
        return carry

    lax.fori_loop(0, 16, scatter, 0)
    for k in RINGS:
        to = lax.rem(q + k, 4)
        push(
            R.dks.at[pl.ds(to * 4, 4)],
            R.dk1.at[k - 1],
            R.m_dks.at[k - 1],
            R.m_dkr.at[k - 1],
            dev_q(k),
        )
    rs_start(R_DQ, tn(R.dqct[...], R.wcr[0:192, :]))
    put(R.g_crx, 0, 0, nn(R.dqct[...], R.ag[A_Y1 + 1]))
    put(R.g_crx, 0, 192, nn(R.oct[...], R.ag[A_DRC]))
    g2("ffd")
    for k in (1, 3, 2):
        landed(R.dk1.at[k - 1], R.m_dkr.at[k - 1], dev_q(k))
    for j in range(4):
        at_block = q * 4 + j
        total = R.dks[at_block].astype(F32)
        for k in range(3):
            total += R.dk1[k, j].astype(F32)
        R.dks[at_block] = total.astype(BF)
    for k in RINGS:
        to = lax.rem(p + k, 4)
        push(
            R.dks.at[q * 4 + to], R.dk2.at[k - 1], R.m_dks.at[2 + k], R.m_dkr.at[2 + k], dev_p(k)
        )
    dy = R.dres[1] + rs_sum(R_DQ)
    dr, dg, db = ln_backward(R.n1[1], get_norm(1), norm_row(1, 0), dy)
    ag_start(A_DR1 + 1, dr)
    R.dres[1] = dr
    vec_put(4, dg, db)
    for k in (1, 3, 2):
        landed(R.dk2.at[k - 1], R.m_dkr.at[2 + k], dev_p(k))
    total = R.dks[mine].astype(F32)
    for k in range(3):
        total += R.dk2[k].astype(F32)
    R.dkv[...] = total.astype(BF)
    rs_start(R_DST, tn(R.dkv[...], R.wcr[384:768, :]))
    put(R.g_crx, 1, 0, nn(R.dkv[...], R.ag[A_BO]))
    g0("crx")
    g3("ffd")

    def self_backward(s):
        ag_wait(A_DR1 + s)
        dot = nt(R.wsa[s, 576:768, :], R.ag[A_DR1 + s]).astype(BF)
        for h in range(NH):
            lo = h * 64
            dqt, dkt, dvt = attend_backward(
                R.pk[s, lo : lo + 64, :],
                R.pk[s, QW + lo : QW + lo + 64, :],
                R.pk[s, 2 * QW + lo : 2 * QW + lo + 64, :],
                R.pt[s, h],
                dot[lo : lo + 64, :],
            )
            R.dpk[s, lo : lo + 64, :] = dqt.astype(BF)
            R.dpk[s, QW + lo : QW + lo + 64, :] = dkt.astype(BF)
            R.dpk[s, 2 * QW + lo : 2 * QW + lo + 64, :] = dvt.astype(BF)
        rs_start(R_DSA + s, tn(R.dpk[s], R.wsa[s, 0:576, :]))

    def self_grads(s, ref):
        put(ref, 0, 0, nn(R.dpk[s, 0:384, :], R.xin[s]))
        put(ref, 1, 0, nn(R.dpk[s, 384:576, :], R.xin[s]))
        put(ref, 1, 192, nn(R.ot[s], R.ag[A_DR1 + s]))

    dy = rs_sum(R_DST)
    dr, dg, db = ln_backward(R.n2[0], get_norm(2), norm_row(0, 1), dy)
    ag_start(A_DR2, dr)
    R.dres[0] = dr
    vec_put(1, dg, db)
    g1("crx")
    ffn_backward(0)
    ffn_grads(0, A_Y1, R.g_ffe)
    g0("ffe")
    g4("ffd")
    dy = R.dres[0] + rs_sum(R_DFF)
    dr, dg, db = ln_backward(R.n1[0], get_norm(0), norm_row(0, 0), dy)
    ag_start(A_DR1, dr)
    R.dres[0] = dr
    vec_put(0, dg, db)
    g1("ffe")
    g2("crx")
    self_backward(0)
    self_grads(0, R.g_sae)
    g0("sae")
    self_backward(1)
    self_grads(1, R.g_sad)
    g0("sad")
    g1("sae")
    vec_send(R.vx, t, R.vec[...], 0, dev_x, 4)
    ag_start(A_IG, R.dres[0] + rs_sum(R_DSA))
    g1("sad")
    g2("ffe")
    g3("crx")
    ag_start(A_IG + 1, R.dres[1] + rs_sum(R_DSA + 1))
    total = vec_sum(R.vx, t, 0, dev_x, 4)
    vec_send(R.vc, c, total, 3, dev_c1, 2)
    g2("sae")
    g2("sad")
    g3("ffe")
    g4("crx")
    total = vec_sum(R.vc, c, 3, dev_c1, 2)
    vec_send(R.vy, y, total, 4, dev_y, 4)
    ag_wait(A_BO + 1)
    ag_wait(A_IG)
    ag_wait(A_IG + 1)
    push(R.ag.at[A_BO + o], R.bor, R.m_hs.at[0], R.m_hr.at[0], dev_c)
    push(R.ag.at[A_IG + o], R.igr, R.m_hs.at[1], R.m_hr.at[1], dev_c)
    g3("sae")
    g3("sad")
    g4("ffe")
    total = vec_sum(R.vy, y, 4, dev_y, 4)
    vec_send(R.vz, z, total, 7, dev_z, 4)
    g4("sae")
    g4("sad")
    bo_o[c] = R.ag[A_BO + c]
    ig_o[c] = R.ag[A_IG + c]
    g5("ffd")
    g5("crx")
    push(R.goc, R.gtc, R.m_hs.at[2], R.m_hr.at[2], dev_c)
    g5("ffe")
    push(R.gof.at[o], R.gtf, R.m_hs.at[3], R.m_hr.at[3], dev_c)
    total = vec_sum(R.vz, z, 7, dev_z, 4)
    on_o[...] = jnp.where(c == 0, total[0:4, :], total[4:8, :])
    oe_o[...] = total[8:10, :]
    landed(R.bor, R.m_hr.at[0], dev_c)
    bo_o[o] = R.bor[...]
    landed(R.igr, R.m_hr.at[1], dev_c)
    ig_o[o] = R.igr[...]

    def spread_out(dst, piece, src):
        dst[piece, :, 0:384] = src[0]
        dst[piece, :, 384:768] = src[1]

    landed(R.gtc, R.m_hr.at[2], dev_c)
    spread_out(oc_o, c, R.goc)
    spread_out(oc_o, o, R.gtc)
    landed(R.gtf, R.m_hr.at[3], dev_c)
    spread_out(of_o, c, R.gof.at[c])
    spread_out(of_o, o, R.gtf)
    g5("sae")
    g5("sad")
    push(R.gos.at[o], R.gts, R.m_hs.at[4], R.m_hr.at[4], dev_c)
    spread_out(os_o, c, R.gos.at[c])
    landed(R.gts, R.m_hr.at[4], dev_c)
    spread_out(os_o, o, R.gts)
    for cp in sends:
        cp.wait_send()


def body(
    layer_inputs,
    cotangent,
    doc_groups,
    retrieved_at,
    sa_qkv,
    sa_out,
    ffn_in,
    ffn_out,
    norm_gain,
    norm_bias,
    cross_q,
    cross_kv,
    cross_out,
    cross_gain,
    cross_bias,
):
    nrm = jnp.concatenate(
        [
            norm_gain[0],
            norm_bias[0],
            cross_gain[None],
            cross_bias[None],
            jnp.zeros((2, D), F32),
        ],
        axis=0,
    )
    ins = (
        layer_inputs[0],
        cotangent,
        doc_groups,
        retrieved_at[:, 0, :],
        nrm,
        jnp.transpose(sa_qkv[0], (1, 2, 0)).reshape(576, D),
        sa_out[0],
        ffn_in[0],
        ffn_out[0],
        jnp.transpose(cross_q, (1, 0)),
        jnp.transpose(cross_kv, (1, 2, 0)).reshape(384, D),
        cross_out,
    )
    hbm = pl.BlockSpec(memory_space=pl.ANY)
    vm = pl.BlockSpec(memory_space=VMEM)
    outs = (
        jax.ShapeDtypeStruct((2, TOK, D), BF),
        jax.ShapeDtypeStruct((2, TOK, D), BF),
        jax.ShapeDtypeStruct((2, 768, D), BF),
        jax.ShapeDtypeStruct((2, 384, D), BF),
        jax.ShapeDtypeStruct((2, 384, D), BF),
        jax.ShapeDtypeStruct((4, D), F32),
        jax.ShapeDtypeStruct((2, D), F32),
    )
    names = [n for n, _ in scratch_list()]

    def run(*refs):
        kernel(names, len(ins), len(outs), *refs)

    bo, ig, gf, gs, gc, gn, ge = pl.pallas_call(
        run,
        out_shape=outs,
        in_specs=[hbm, hbm, vm, vm] + [hbm] * 8,
        out_specs=[vm] * len(outs),
        scratch_shapes=[s for _, s in scratch_list()],
        compiler_params=pltpu.CompilerParams(
            collective_id=0, has_side_effects=True, vmem_limit_bytes=62 << 20
        ),
        name="layers",
    )(*ins)
    sa = gs.reshape(768, D)
    cr = gc.reshape(768, D)
    d_qkv = jnp.transpose(sa[0:576].astype(F32).reshape(3, 192, D), (2, 0, 1))
    d_q = jnp.transpose(cr[0:192].astype(F32), (1, 0))
    d_kv = jnp.transpose(cr[384:768].astype(F32).reshape(2, 192, D), (2, 0, 1))
    return (
        bo[None],
        ig.astype(F32)[None],
        d_qkv[None],
        sa[576:768].astype(F32)[None],
        gf[0].astype(F32)[None],
        gf[1].astype(F32)[None],
        gn[0:2][None],
        gn[2:4][None],
        d_q,
        d_kv,
        cr[192:384].astype(F32),
        ge[0],
        ge[1],
    )


def solution(mesh):
    placed = (
        P("section", None, "dp", None),
        P(None, "dp", None),
        P(),
        P(None, "dp", None),
        P("section", None, None, "tensor"),
        P("section", "tensor", None),
        P("section", None, "tensor"),
        P("section", "tensor", None),
        P("section", None, None),
        P("section", None, None),
        P(None, "tensor"),
        P(None, None, "tensor"),
        P("tensor", None),
        P(),
        P(),
    )
    return jax.shard_map(
        body,
        mesh=mesh,
        in_specs=placed,
        out_specs=(
            P("section", None, "dp", None),
            P("section", None, "dp", None),
            P("section", None, None, "tensor"),
            P("section", "tensor", None),
            P("section", None, "tensor"),
            P("section", "tensor", None),
            P("section", None, None),
            P("section", None, None),
            P(None, "tensor"),
            P(None, None, "tensor"),
            P("tensor", None),
            P(),
            P(),
        ),
        check_vma=False,
    )
```

time: 1210 us -> 190 us (0.16); the launches traced: 1190 us -> 188 us
  waiting for transfers between devices: 859 us -> 0 us
  Pallas kernels: 0 us -> 170 us
  matrix products: 109 us -> 0 us
  blocking collectives: 74.8 us -> 0 us
  other arithmetic: 77.4 us -> 10.6 us
  local copies, waits for them, and re-layouts: 48.3 us -> 6.42 us
  between operations: 17.8 us -> 0.7 us
    psum x16 -> x0, waiting for transfers between devices: 629 us -> none  [the longest x14 526 us: head_total(): lax.psum(partial_sum.astype(jnp.bfloat16), 'tensor').astype(jnp.float32)]
    pallas_call x0 -> x1, Pallas kernels: none -> 170 us  [body(): pl.pallas_call(run, out_shape=outs, in_specs=[hbm, hbm, vm, vm] + [hbm] *...]
    reduce_scatter x2 -> x0, waiting for transfers between devices: 138 us -> none  [body(): lax.psum_scatter(scattered.astype(jnp.bfloat16), 'dp', scatter_dimension=...]
    dot_general x92 -> x0, matrix products: 101 us -> none  [the longest x21 33.8 us: matmul_tn(): lax.dot_general(lhs_mat, rhs_mat, (((0,), (0,)), ((), ())), preferred_ele...]
    all_gather x2 -> x0, waiting for transfers between devices: 86.2 us -> none  [body(): tables.append(lax.all_gather(arrived, 'dp', axis=0, tiled=True))]
    psum x2 -> x0, blocking collectives: 74.8 us -> none  [the longest x1 72.3 us: body(): lax.psum(gain_stack.astype(jnp.bfloat16), 'dp').astype(jnp.float32)]
    reduce_sum x22 -> x0, other arithmetic: 27 us -> none  [the longest x7 16.1 us: norm_backward(): jnp.sum(upstream * normed, axis=0)]
    unnamed x506 -> x14, local copies, waits for them, and re-layouts: 22.2 us -> 2.39 us
  transfers between devices with their start and end apart: 24 -> 0, of which waited for: 22 -> 0; matrix products, arithmetic and copies ran while one was open for 5% -> 0% of each run, Pallas kernels for 0% -> 0%
where the time goes in v1:
time: 190 us; the launch traced here: 188 us
  Pallas kernels  170 us (89%)
  other arithmetic  10.6 us (6%)
  local copies, waits for them, and re-layouts  6.42 us (3%)
    pallas_call x1, Pallas kernels, body(): pl.pallas_call(run, out_shape=outs, in_specs=[hbm, hbm, vm, vm] + [hbm] *...  170 us
    convert_element_type x1, other arithmetic, body(): gf[1].astype(F32)[None]  4.27 us

profile of v1, /device:TPU:0, one launch (start us, length us, event | category | flops | bytes accessed | tf_op | source)
XLA Modules:
  0.0 187.7 jit_solution(3658944597305196300)
XLA Ops:
  0.6 0.7 broadcast_in_dim.38
  1.3 0.7 broadcast_in_dim.39
  2.0 1.3 concatenate.3.refs_4_
  3.4 1.3 copy.30
  4.6 169.9 %layers.1 = (bf16[2,128,768]{2,1,0:T(8,128)(2,1)}, bf16[2,128,768]{2,1,0:T(8,128)(2,1)}, bf16[2,768,768]{2,1,0:T(8,128)(2,1)}, bf16[2,384,768]{2,1,0:T(8,128)(2,...) custom-call(bf16[2,128,768]{2,1,0:T(8,128)(2,1)} %bitcast.54, bf16[2,128,768]{2,1,0:T(8,128)(2,1)} %refs_1_.1, ...), custom_call_target="tpu_custom_call" | custom-call | tf_op jit(solution)/shard_map/layers/pallas_call | solution.py:761
  174.6 2.1 %slice_convert_fusion.2 = (f32[192,768]{1,0:T(8,128)}, f32[768,192]{0,1:T(8,128)}) fusion(bf16[768,768]{1,0:T(8,128)(2,1)} %bitcast.49), kind=kLoop, calls=%fused_computation.6 | loop fusion | flops 294912 | bytes 1769472 | tf_op jit(solution)/shard_map/convert_element_type | solution.py:788
  176.7 0.0 copy-start
  176.7 4.3 %slice_convert_fusion = (f32[1,768,768]{2,1,0:T(8,128)}, f32[1,768,768]{2,1,0:T(8,128)}) fusion(bf16[2,768,768]{2,1,0:T(8,128)(2,1)} %get-tuple-element.23), kind=kLoop, calls=%fused_computation.2 | loop fusion | flops 1179648 | bytes 7077888 | tf_op jit(solution)/shard_map/convert_element_type | solution.py:783
  181.0 0.0 copy-done
  181.0 0.1 slice.45
  181.0 0.0 copy-start.1
  181.0 1.4 convert_bitcast_fusion
  182.4 0.4 copy-done.1
  182.8 0.0 copy-start.4
  182.8 0.0 copy-start.5
  182.8 0.0 copy-start.3
  182.8 1.1 convert_bitcast_fusion.1
  183.9 0.0 copy-start.2
  183.9 0.9 fusion
  184.8 0.0 copy-done.4
  184.8 0.6 slice_bitcast_fusion.1
  185.4 0.0 copy-done.5
  185.4 0.6 slice_reduce_fusion
  186.0 0.0 copy-done.3
  186.0 0.9 bitcast_convert_fusion
  186.9 0.0 copy-done.2
  186.9 0.7 copy.32
  (2 shorter events, 0.0 us)
Async XLA Ops:
  176.7 4.3 %copy-start = (bf16[2,384,768]{2,1,0:T(8,128)(2,1)S(1)}, bf16[2,384,768]{2,1,0:T(8,128)(2,1)}, u32[]{:S(2)}) copy-start(bf16[2,384,768]{2,1,0:T(8,128)(2,1)} %get-tuple-element.22) | copy-start | bytes 3538948
  181.0 1.7 copy-start.1
  182.8 2.0 %copy-start.4 = (f32[4,768]{1,0:T(4,128)S(1)}, f32[4,768]{1,0:T(4,128)}, u32[]{:S(2)}) copy-start(f32[4,768]{1,0:T(4,128)} %get-tuple-element.24) | copy-start | bytes 36868
  182.8 2.6 %copy-start.5 = (f32[2,768]{1,0:T(2,128)S(1)}, f32[2,768]{1,0:T(2,128)}, u32[]{:S(2)}) copy-start(f32[2,768]{1,0:T(2,128)} %get-tuple-element.26) | copy-start | bytes 18436
  182.8 3.2 %copy-start.3 = (bf16[2,128,768]{2,1,0:T(8,128)(2,1)S(1)}, bf16[2,128,768]{2,1,0:T(8,128)(2,1)}, u32[]{:S(2)}) copy-start(bf16[2,128,768]{2,1,0:T(8,128)(2,1)} %get-tuple-element.21) | copy-start | bytes 1179652
  183.9 3.0 %copy-start.2 = (bf16[2,128,768]{2,1,0:T(8,128)(2,1)S(1)}, bf16[2,128,768]{2,1,0:T(8,128)(2,1)}, u32[]{:S(2)}) copy-start(bf16[2,128,768]{2,1,0:T(8,128)(2,1)} %get-tuple-element.20) | copy-start | bytes 1179652

commit v2 on v1

--- a/solution.py
+++ b/solution.py
@@ -44,7 +44,7 @@
 def scratch_list():
     out = [
         ("xin", VMEM((2, TOK, D), BF)),
-        ("nv", VMEM((2, 8, D), F32)),
+        ("nv", VMEM((2, 2, 2, D), F32)),
         ("wsa", VMEM((2, 768, D), BF)),
         ("wff", VMEM((2, 2, 768, D), BF)),
         ("wcr", VMEM((768, D), BF)),
@@ -83,16 +83,12 @@
         ("ag", VMEM((N_AG, TOK, D), BF)),
         ("rs", VMEM((N_RS, TOK, D), BF)),
         ("rr", VMEM((N_RS, 3, SH, D), BF)),
-        ("bor", VMEM((TOK, D), BF)),
-        ("igr", VMEM((TOK, D), BF)),
+        ("kva", VMEM((2 * QW, KEYS), F32)),
         ("gof", VMEM((2, 2, 768, 384), BF)),
         ("gos", VMEM((2, 2, 384, 384), BF)),
         ("goc", VMEM((2, 384, 384), BF)),
-        ("gtf", VMEM((2, 768, 384), BF)),
-        ("gts", VMEM((2, 384, 384), BF)),
-        ("gtc", VMEM((2, 384, 384), BF)),
-        ("m_w", DMA((2, 6))),
-        ("m_ws", DMA((6,))),
+        ("m_w", DMA((2, 7))),
+        ("m_ws", DMA((7,))),
         ("m_l", DMA((4,))),
         ("m_ags", DMA((N_AG, 3))),
         ("m_agr", DMA((N_AG, 3))),
@@ -104,8 +100,9 @@
         ("m_dkr", DMA((6,))),
         ("m_vs", DMA((10,))),
         ("m_vr", DMA((10,))),
-        ("m_hs", DMA((5,))),
-        ("m_hr", DMA((5,))),
+        ("m_hs", DMA((3,))),
+        ("m_hr", DMA((3,))),
+        ("m_o", DMA((3,))),
     ]
     for name, rows in BLOCKS.items():
         out += [
@@ -113,8 +110,9 @@
             ("x_" + name, VMEM((2, rows, 384), BF)),
             ("a_" + name, VMEM((3, 2, rows // 4, 384), BF)),
             ("b_" + name, VMEM((3, rows // 8, 384), BF)),
-            ("s_" + name, DMA((13,))),
-            ("r_" + name, DMA((13,))),
+            ("s_" + name, DMA((14,))),
+            ("r_" + name, DMA((10,))),
+            ("f_" + name, DMA((2, 4))),
         ]
     return out
 
@@ -139,7 +137,9 @@
 
 
 def kernel(names, n_in, n_out, *refs):
-    (x_h, cot_h, dgr, ret, nrm_h, qkv_h, out_h, win_h, wfo_h, cq_h, ckv_h, co_h) = refs[:n_in]
+    (x_h, cot_h, dgr, ret, ng_h, nb_h, cg, cb, qkv_h, out_h, win_h, wfo_h, cq_h, ckv_h, co_h) = refs[
+        :n_in
+    ]
     bo_o, ig_o, of_o, os_o, oc_o, on_o, oe_o = refs[n_in : n_in + n_out]
     R = Refs()
     for name, ref in zip(names, refs[n_in + n_out :]):
@@ -158,8 +158,11 @@
     def dev_x(k):
         return (c, lax.rem(t + k, 4), d)
 
+    def dp_p(k):
+        return lax.rem(p + k, 4) * sp + q * sq
+
     def dev_p(k):
-        return (c, t, lax.rem(p + k, 4) * sp + q * sq)
+        return (c, t, dp_p(k))
 
     def dev_q(k):
         return (c, t, p * sp + lax.rem(q + k, 4) * sq)
@@ -173,12 +176,13 @@
     dev_c = (o, t, d)
     sends = []
 
-    def push(src, dst, ss, rs, dev):
+    def push(src, dst, ss, rs, dev, wait=True):
         cp = pltpu.make_async_remote_copy(
             src_ref=src, dst_ref=dst, send_sem=ss, recv_sem=rs, device_id=dev, device_id_type=MESH
         )
         cp.start()
-        sends.append(cp)
+        if wait:
+            sends.append(cp)
         return cp
 
     def landed(dst, rs, dev):
@@ -186,23 +190,36 @@
             src_ref=dst, dst_ref=dst, send_sem=rs, recv_sem=rs, device_id=dev, device_id_type=MESH
         ).wait_recv()
 
-    items = [
-        (x_h.at[c], R.xin.at[c]),
-        (nrm_h, R.nv.at[c]),
-        (qkv_h, R.wsa.at[c, pl.ds(0, 576)]),
-        (out_h, R.wsa.at[c, pl.ds(576, 192)]),
-        (win_h, R.wff.at[c, 0]),
-        (wfo_h, R.wff.at[c, 1]),
-    ]
+    def places(s):
+        return [
+            R.xin.at[s],
+            R.wsa.at[s, pl.ds(0, 576)],
+            R.wsa.at[s, pl.ds(576, 192)],
+            R.nv.at[s, 0],
+            R.nv.at[s, 1],
+            R.wff.at[s, 0],
+            R.wff.at[s, 1],
+        ]
+
+    items = [x_h.at[c], qkv_h, out_h, ng_h, nb_h, win_h, wfo_h]
+    bar = pltpu.get_barrier_semaphore()
+    peers = [dev_c]
+    for k in (1, 2, 3):
+        for dev in (dev_x(k), dev_y(k), dev_z(k)):
+            peers.append(dev)
+        peers.append((o,) + dev_y(k)[1:])
+        peers.append((o,) + dev_z(k)[1:])
+    for dev in peers:
+        pl.semaphore_signal(bar, inc=1, device_id=dev, device_id_type=MESH)
 
     def own(i):
-        pltpu.make_async_copy(items[i][0], items[i][1], R.m_w.at[c, i]).start()
+        pltpu.make_async_copy(items[i], places(c)[i], R.m_w.at[c, i]).start()
 
     def other(i):
-        src = x_h.at[o] if i == 0 else items[i][0]
-        push(src, items[i][1], R.m_ws.at[i], R.m_w.at[c, i], dev_c)
-
-    for i in range(4):
+        src = x_h.at[o] if i == 0 else items[i]
+        push(src, places(c)[i], R.m_ws.at[i], R.m_w.at[c, i], dev_c)
+
+    for i in range(5):
         own(i)
     singles = [
         pltpu.make_async_copy(cq_h, R.wcr.at[pl.ds(0, 192)], R.m_l.at[0]),
@@ -210,29 +227,18 @@
         pltpu.make_async_copy(ckv_h, R.wcr.at[pl.ds(384, 384)], R.m_l.at[2]),
         pltpu.make_async_copy(cot_h.at[c], R.cot, R.m_l.at[3]),
     ]
+    pl.semaphore_wait(bar, len(peers))
+    for i in range(5):
+        other(i)
+    for i in (5, 6):
+        own(i)
+        other(i)
     for cp in singles:
         cp.start()
-    own(4)
-    own(5)
-    bar = pltpu.get_barrier_semaphore()
-    peers = [f(k) for f in (dev_x, dev_y, dev_z) for k in (1, 2, 3)] + [dev_c]
-    for dev in peers:
-        pl.semaphore_signal(bar, inc=1, device_id=dev, device_id_type=MESH)
-    pl.semaphore_wait(bar, len(peers))
-    for i in range(6):
-        other(i)
 
     def need(s, i):
-        src = x_h.at[s] if i == 0 else items[i][0]
-        dst = [
-            R.xin.at[s],
-            R.nv.at[s],
-            R.wsa.at[s, pl.ds(0, 576)],
-            R.wsa.at[s, pl.ds(576, 192)],
-            R.wff.at[s, 0],
-            R.wff.at[s, 1],
-        ][i]
-        pltpu.make_async_copy(src, dst, R.m_w.at[s, i]).wait()
+        src = x_h.at[s] if i == 0 else items[i]
+        pltpu.make_async_copy(src, places(s)[i], R.m_w.at[s, i]).wait()
 
     def rs_start(i, value):
         R.rs[i] = value.astype(BF)
@@ -269,12 +275,18 @@
         for k in (1, 3, 2):
             landed(R.ag.at[i, rows_t], R.m_agr.at[i, k - 1], dev_x(k))
 
-    def norm_row(s, i):
-        return R.nv[s, pl.ds(i, 1), :]
+    def gain_row(s, i):
+        return R.nv[s, 0, i : i + 1, :]
+
+    def bias_row(s, i):
+        return R.nv[s, 1, i : i + 1, :]
+
+    cross_gain = cg[...].reshape(1, D)
+    cross_bias = cb[...].reshape(1, D)
 
     def self_forward(s):
         need(s, 0)
-        need(s, 2)
+        need(s, 1)
         R.pk[s] = nt(R.wsa[s, 0:576, :], R.xin[s]).astype(BF)
         for h in range(NH):
             qt = R.pk[s, h * 64 : h * 64 + 64, :]
@@ -289,7 +301,7 @@
             pr = e / jnp.sum(e, axis=0, keepdims=True)
             R.pt[s, h] = pr
             R.ot[s, h * 64 : h * 64 + 64, :] = nn(vt, pr.astype(BF)).astype(BF)
-        need(s, 3)
+        need(s, 2)
         rs_start(R_SA + s, tn(R.ot[s], R.wsa[s, 576:768, :]))
 
     def put_norm(slot, spread):
@@ -301,8 +313,9 @@
     def self_finish(s):
         total = rs_sum(R_SA + s)
         r = R.xin[s, rows_t, :].astype(F32) + total
-        need(s, 1)
-        out, n, spread = ln_forward(r, norm_row(s, 0), norm_row(s, 2))
+        need(s, 3)
+        need(s, 4)
+        out, n, spread = ln_forward(r, gain_row(s, 0), bias_row(s, 0))
         ag_start(A_Y1 + s, out)
         R.y1f[s] = out
         R.n1[s] = n
@@ -395,20 +408,61 @@
         for k in RINGS:
             push(fin.at[half, rows], fin.at[half, rows], s.at[6 + k], r.at[6 + k], dev_q(k))
 
+    final = {"ffd": (1, of_o), "ffe": (0, of_o), "sad": (1, os_o), "sae": (0, os_o)}
+
     def g4(name):
         g, x, a, b, s, r = blk(name)
         fin = goal[name]
         for k in (1, 3, 2):
             landed(fin.at[lax.rem(q, 2), q_rows(name, p, q)], r.at[6 + k], dev_q(k))
         mine = p_rows(name, p)
+        if name not in final:
+            for k in RINGS:
+                push(
+                    fin.at[:, mine], fin.at[:, mine], s.at[9 + k], R.f_crx.at[c, k], dev_p(k)
+                )
+            return
+        owner, dst = final[name]
+        f = getattr(R, "f_" + name)
         for k in RINGS:
-            push(fin.at[:, mine], fin.at[:, mine], s.at[9 + k], r.at[9 + k], dev_p(k))
+            push(
+                fin.at[:, mine], dst.at[c, :, mine], s.at[9 + k], f.at[c, k], (owner, t, dp_p(k))
+            )
+
+        @pl.when(c == owner)
+        def _():
+            pltpu.make_async_copy(fin.at[:, mine], dst.at[c, :, mine], f.at[c, 0]).start()
+
+        @pl.when(c != owner)
+        def _():
+            push(fin.at[:, mine], dst.at[c, :, mine], s.at[13], f.at[c, 0], dev_c, False)
 
     def g5(name):
-        g, x, a, b, s, r = blk(name)
         fin = goal[name]
-        for k in (1, 3, 2):
-            landed(fin.at[:, p_rows(name, p)], r.at[9 + k], dev_p(k))
+        mine = p_rows(name, p)
+        if name not in final:
+            for k in (1, 3, 2):
+                landed(fin.at[:, mine], R.f_crx.at[c, k], dev_p(k))
+            return
+        owner, dst = final[name]
+        f = getattr(R, "f_" + name)
+
+        @pl.when(c == owner)
+        def _():
+            for piece in (0, 1):
+                for k in range(4):
+                    landed(dst.at[piece, :, mine], f.at[piece, k], dev_p(1))
+
+        @pl.when(c != owner)
+        def _():
+            pltpu.make_async_remote_copy(
+                src_ref=fin.at[:, mine],
+                dst_ref=dst.at[c, :, mine],
+                send_sem=getattr(R, "s_" + name).at[13],
+                recv_sem=f.at[c, 0],
+                device_id=dev_c,
+                device_id_type=MESH,
+            ).wait_send()
 
     def vec_put(row, dg, db, step=2):
         R.vec[row : row + 1, :] = dg
@@ -437,8 +491,8 @@
     self_finish(0)
     self_finish(1)
     ag_wait(A_Y1)
-    need(0, 4)
     need(0, 5)
+    need(0, 6)
     ffn_forward(0, A_Y1)
 
     for cp in singles:
@@ -450,8 +504,7 @@
     live = (micro == c) & (group <= d) & (dgr[...] > 0)
     first = jnp.max(jnp.where(live, group, 0), axis=1, keepdims=True)
     first = jnp.max(first, axis=0, keepdims=True)
-    pick = lax.broadcasted_iota(jnp.int32, (2, KEYS), 0) == c
-    rows = jnp.max(jnp.where(pick, ret[...], 0), axis=0, keepdims=True) + first * TOK
+    rows = jnp.where(c == 0, ret[0], ret[1]) + first * TOK
     g_at = rows // TOK
     b_at = jnp.where(c == 0, g_at, lax.rem(g_at, 4) * 4 + g_at // 4)
     at = b_at * TOK + lax.rem(rows, TOK)
@@ -463,7 +516,7 @@
 
     lax.fori_loop(0, 16, build, 0)
 
-    out, n, spread = ln_forward(R.y1f[0] + rs_sum(R_FF), norm_row(0, 1), norm_row(0, 3))
+    out, n, spread = ln_forward(R.y1f[0] + rs_sum(R_FF), gain_row(0, 1), bias_row(0, 1))
     ag_start(A_BO, out)
     R.n2[0] = n
     put_norm(2, spread)
@@ -474,23 +527,29 @@
     def kv_send(k, dev, slot, at_block):
         push(R.kvt.at[at_block], R.kvt.at[at_block], R.m_kvs.at[slot], R.m_kvr.at[slot], dev)
 
+    def gather(b):
+        hot = R.hot[pl.ds(pl.multiple_of(b * TOK, TOK), TOK), :]
+        R.kva[...] += nn(R.kvt[b], hot)
+
     for k in RINGS:
         kv_send(k, dev_p(k), k - 1, mine)
     for k in RINGS:
         kv_send(k, dev_q(k), 2 + k, mine)
+    R.kva[...] = jnp.zeros((2 * QW, KEYS), F32)
+    gather(mine)
     for j in (1, 3, 2):
         landed(R.kvt.at[mine], R.m_kvr.at[j - 1], dev_p(j))
         came = q * 4 + lax.rem(p + 4 - j, 4)
         for k in RINGS:
             kv_send(k, dev_q(k), 6 + (j - 1) * 3 + k - 1, came)
-    for slot in range(3, 15):
-        landed(R.kvt.at[mine], R.m_kvr.at[slot], dev_q(1))
-
-    def gather(i, total):
-        pair = jnp.concatenate([R.kvt[2 * i], R.kvt[2 * i + 1]], axis=1)
-        return total + nn(pair, R.hot[pl.ds(pl.multiple_of(i * 256, 256), 256), :])
-
-    R.kvct[...] = lax.fori_loop(0, 8, gather, jnp.zeros((2 * QW, KEYS), F32)).astype(BF)
+        gather(came)
+    for j in (0, 1, 3, 2):
+        for k in (1, 3, 2):
+            slot = 2 + k if j == 0 else 6 + (j - 1) * 3 + k - 1
+            landed(R.kvt.at[mine], R.m_kvr.at[slot], dev_q(k))
+            gather(lax.rem(q + 4 - k, 4) * 4 + lax.rem(p + 4 - j, 4))
+
+    R.kvct[...] = R.kva[...].astype(BF)
     for h in range(NH):
         lo = h * 64
         st = tn(R.kvct[lo : lo + 64, :], R.qct[lo : lo + 64, :]) * SCALE
@@ -499,27 +558,27 @@
         R.ptc[h] = pr
         R.oct[lo : lo + 64, :] = nn(R.kvct[QW + lo : QW + lo + 64, :], pr.astype(BF)).astype(BF)
     rs_start(R_CR, tn(R.oct[...], R.wcr[192:384, :]))
-    need(1, 4)
     need(1, 5)
-    out, n, spread = ln_forward(R.y1f[1] + rs_sum(R_CR), norm_row(0, 4), norm_row(0, 5))
+    need(1, 6)
+    out, n, spread = ln_forward(R.y1f[1] + rs_sum(R_CR), cross_gain, cross_bias)
     ag_start(A_Y2, out)
     R.y2f[...] = out
     R.nc[...] = n
     put_norm(4, spread)
     ag_wait(A_Y2)
     ffn_forward(1, A_Y2)
-    out, n, spread = ln_forward(R.y2f[...] + rs_sum(R_FF + 1), norm_row(1, 1), norm_row(1, 3))
-
-    dr, dg, db = ln_backward(n, spread, norm_row(1, 1), R.cot[rows_t, :].astype(F32))
+    out, n, spread = ln_forward(R.y2f[...] + rs_sum(R_FF + 1), gain_row(1, 1), bias_row(1, 1))
+
+    dr, dg, db = ln_backward(n, spread, gain_row(1, 1), R.cot[rows_t, :].astype(F32))
     ag_start(A_DR2 + 1, dr)
     R.dres[1] = dr
     vec_put(5, dg, db)
+    ffn_backward(1)
     ag_start(A_BO + 1, out)
-    ffn_backward(1)
     ffn_grads(1, A_Y2, R.g_ffd)
     g0("ffd")
     dy = R.dres[1] + rs_sum(R_DFF + 1)
-    dr, dg, db = ln_backward(R.nc[...], get_norm(4), norm_row(0, 4), dy)
+    dr, dg, db = ln_backward(R.nc[...], get_norm(4), cross_gain, dy)
     ag_start(A_DRC, dr)
     R.dres[1] = dr
     vec_put(8, dg, db, 1)
@@ -546,53 +605,29 @@
         R.dkvct[lo : lo + 64, :] = dkt.astype(BF)
         R.dkvct[QW + lo : QW + lo + 64, :] = dvt.astype(BF)
 
-    def scatter(i, carry):
-        part = nt(R.dkvct[...], R.hot[pl.ds(pl.multiple_of(i * TOK, TOK), TOK), :])
-        R.dks[i] = part.astype(BF)
-        return carry
-
-    lax.fori_loop(0, 16, scatter, 0)
-    for k in RINGS:
+    for k in RINGS + (0,):
         to = lax.rem(q + k, 4)
-        push(
-            R.dks.at[pl.ds(to * 4, 4)],
-            R.dk1.at[k - 1],
-            R.m_dks.at[k - 1],
-            R.m_dkr.at[k - 1],
-            dev_q(k),
-        )
+        for j in range(4):
+            b = to * 4 + j
+            hot = R.hot[pl.ds(pl.multiple_of(b * TOK, TOK), TOK), :]
+            R.dks[b] = nt(R.dkvct[...], hot).astype(BF)
+        if k:
+            push(
+                R.dks.at[pl.ds(to * 4, 4)],
+                R.dk1.at[k - 1],
+                R.m_dks.at[k - 1],
+                R.m_dkr.at[k - 1],
+                dev_q(k),
+            )
     rs_start(R_DQ, tn(R.dqct[...], R.wcr[0:192, :]))
     put(R.g_crx, 0, 0, nn(R.dqct[...], R.ag[A_Y1 + 1]))
     put(R.g_crx, 0, 192, nn(R.oct[...], R.ag[A_DRC]))
-    g2("ffd")
-    for k in (1, 3, 2):
-        landed(R.dk1.at[k - 1], R.m_dkr.at[k - 1], dev_q(k))
-    for j in range(4):
-        at_block = q * 4 + j
-        total = R.dks[at_block].astype(F32)
-        for k in range(3):
-            total += R.dk1[k, j].astype(F32)
-        R.dks[at_block] = total.astype(BF)
-    for k in RINGS:
-        to = lax.rem(p + k, 4)
-        push(
-            R.dks.at[q * 4 + to], R.dk2.at[k - 1], R.m_dks.at[2 + k], R.m_dkr.at[2 + k], dev_p(k)
-        )
     dy = R.dres[1] + rs_sum(R_DQ)
-    dr, dg, db = ln_backward(R.n1[1], get_norm(1), norm_row(1, 0), dy)
+    dr, dg, db = ln_backward(R.n1[1], get_norm(1), gain_row(1, 0), dy)
     ag_start(A_DR1 + 1, dr)
     R.dres[1] = dr
     vec_put(4, dg, db)
-    for k in (1, 3, 2):
-        landed(R.dk2.at[k - 1], R.m_dkr.at[2 + k], dev_p(k))
-    total = R.dks[mine].astype(F32)
-    for k in range(3):
-        total += R.dk2[k].astype(F32)
-    R.dkv[...] = total.astype(BF)
-    rs_start(R_DST, tn(R.dkv[...], R.wcr[384:768, :]))
-    put(R.g_crx, 1, 0, nn(R.dkv[...], R.ag[A_BO]))
-    g0("crx")
-    g3("ffd")
+    g2("ffd")
 
     def self_backward(s):
         ag_wait(A_DR1 + s)
@@ -609,96 +644,164 @@
             R.dpk[s, lo : lo + 64, :] = dqt.astype(BF)
             R.dpk[s, QW + lo : QW + lo + 64, :] = dkt.astype(BF)
             R.dpk[s, 2 * QW + lo : 2 * QW + lo + 64, :] = dvt.astype(BF)
-        rs_start(R_DSA + s, tn(R.dpk[s], R.wsa[s, 0:576, :]))
 
     def self_grads(s, ref):
         put(ref, 0, 0, nn(R.dpk[s, 0:384, :], R.xin[s]))
         put(ref, 1, 0, nn(R.dpk[s, 384:576, :], R.xin[s]))
         put(ref, 1, 192, nn(R.ot[s], R.ag[A_DR1 + s]))
 
+    def input_part(s):
+        rs_start(R_DSA + s, tn(R.dpk[s], R.wsa[s, 0:576, :]))
+
+    for k in (1, 3, 2):
+        landed(R.dk1.at[k - 1], R.m_dkr.at[k - 1], dev_q(k))
+    for k in RINGS + (0,):
+        to = lax.rem(p + k, 4)
+        b = q * 4 + to
+        total = R.dks[b].astype(F32)
+        for j in range(3):
+            total += R.dk1[j, to].astype(F32)
+        R.dks[b] = total.astype(BF)
+        if k:
+            push(R.dks.at[b], R.dk2.at[k - 1], R.m_dks.at[2 + k], R.m_dkr.at[2 + k], dev_p(k))
+    self_backward(1)
+    input_part(1)
+    self_grads(1, R.g_sad)
+    g0("sad")
+    for k in (1, 3, 2):
+        landed(R.dk2.at[k - 1], R.m_dkr.at[2 + k], dev_p(k))
+    total = R.dks[mine].astype(F32)
+    for k in range(3):
+        total += R.dk2[k].astype(F32)
+    R.dkv[...] = total.astype(BF)
+    rs_start(R_DST, tn(R.dkv[...], R.wcr[384:768, :]))
+    put(R.g_crx, 1, 0, nn(R.dkv[...], R.ag[A_BO]))
+    g0("crx")
+    g3("ffd")
+    g1("sad")
     dy = rs_sum(R_DST)
-    dr, dg, db = ln_backward(R.n2[0], get_norm(2), norm_row(0, 1), dy)
+    dr, dg, db = ln_backward(R.n2[0], get_norm(2), gain_row(0, 1), dy)
     ag_start(A_DR2, dr)
     R.dres[0] = dr
     vec_put(1, dg, db)
+    g4("ffd")
     g1("crx")
     ffn_backward(0)
     ffn_grads(0, A_Y1, R.g_ffe)
     g0("ffe")
-    g4("ffd")
+    g2("sad")
+    ag_start(A_IG + 1, R.dres[1] + rs_sum(R_DSA + 1))
     dy = R.dres[0] + rs_sum(R_DFF)
-    dr, dg, db = ln_backward(R.n1[0], get_norm(0), norm_row(0, 0), dy)
+    dr, dg, db = ln_backward(R.n1[0], get_norm(0), gain_row(0, 0), dy)
     ag_start(A_DR1, dr)
     R.dres[0] = dr
     vec_put(0, dg, db)
+    vec_send(R.vx, t, R.vec[...], 0, dev_x, 4)
     g1("ffe")
     g2("crx")
+    g3("sad")
     self_backward(0)
     self_grads(0, R.g_sae)
     g0("sae")
-    self_backward(1)
-    self_grads(1, R.g_sad)
-    g0("sad")
-    g1("sae")
-    vec_send(R.vx, t, R.vec[...], 0, dev_x, 4)
-    ag_start(A_IG, R.dres[0] + rs_sum(R_DSA))
-    g1("sad")
-    g2("ffe")
-    g3("crx")
-    ag_start(A_IG + 1, R.dres[1] + rs_sum(R_DSA + 1))
+    input_part(0)
     total = vec_sum(R.vx, t, 0, dev_x, 4)
     vec_send(R.vc, c, total, 3, dev_c1, 2)
-    g2("sae")
-    g2("sad")
-    g3("ffe")
-    g4("crx")
+    g4("sad")
+    g3("crx")
+    g1("sae")
+    g2("ffe")
     total = vec_sum(R.vc, c, 3, dev_c1, 2)
     vec_send(R.vy, y, total, 4, dev_y, 4)
+    ag_start(A_IG, R.dres[0] + rs_sum(R_DSA))
+    g4("crx")
     ag_wait(A_BO + 1)
+    push(R.ag.at[A_BO + o], bo_o.at[c], R.m_hs.at[0], R.m_hr.at[0], dev_c)
+    outs = [pltpu.make_async_copy(R.ag.at[A_BO + c], bo_o.at[c], R.m_o.at[0])]
+    outs[0].start()
+    g3("ffe")
+    g2("sae")
+    total = vec_sum(R.vy, y, 4, dev_y, 4)
+    vec_send(R.vz, z, total, 7, dev_z, 4)
+    g4("ffe")
+    g3("sae")
+    g5("crx")
+    push(R.goc, oc_o.at[c], R.m_hs.at[1], R.m_hr.at[1], dev_c)
+    outs.append(pltpu.make_async_copy(R.goc, oc_o.at[c], R.m_o.at[1]))
+    outs[1].start()
     ag_wait(A_IG)
     ag_wait(A_IG + 1)
-    push(R.ag.at[A_BO + o], R.bor, R.m_hs.at[0], R.m_hr.at[0], dev_c)
-    push(R.ag.at[A_IG + o], R.igr, R.m_hs.at[1], R.m_hr.at[1], dev_c)
-    g3("sae")
-    g3("sad")
-    g4("ffe")
-    total = vec_sum(R.vy, y, 4, dev_y, 4)
-    vec_send(R.vz, z, total, 7, dev_z, 4)
-    g4("sae")
-    g4("sad")
-    bo_o[c] = R.ag[A_BO + c]
-    ig_o[c] = R.ag[A_IG + c]
-    g5("ffd")
-    g5("crx")
-    push(R.goc, R.gtc, R.m_hs.at[2], R.m_hr.at[2], dev_c)
-    g5("ffe")
-    push(R.gof.at[o], R.gtf, R.m_hs.at[3], R.m_hr.at[3], dev_c)
+    push(R.ag.at[A_IG + o], ig_o.at[c], R.m_hs.at[2], R.m_hr.at[2], dev_c)
+    outs.append(pltpu.make_async_copy(R.ag.at[A_IG + c], ig_o.at[c], R.m_o.at[2]))
+    outs[2].start()
     total = vec_sum(R.vz, z, 7, dev_z, 4)
     on_o[...] = jnp.where(c == 0, total[0:4, :], total[4:8, :])
     oe_o[...] = total[8:10, :]
-    landed(R.bor, R.m_hr.at[0], dev_c)
-    bo_o[o] = R.bor[...]
-    landed(R.igr, R.m_hr.at[1], dev_c)
-    ig_o[o] = R.igr[...]
-
-    def spread_out(dst, piece, src):
-        dst[piece, :, 0:384] = src[0]
-        dst[piece, :, 384:768] = src[1]
-
-    landed(R.gtc, R.m_hr.at[2], dev_c)
-    spread_out(oc_o, c, R.goc)
-    spread_out(oc_o, o, R.gtc)
-    landed(R.gtf, R.m_hr.at[3], dev_c)
-    spread_out(of_o, c, R.gof.at[c])
-    spread_out(of_o, o, R.gtf)
+    g4("sae")
+    g5("ffd")
+    g5("sad")
+    g5("ffe")
+    landed(bo_o.at[c], R.m_hr.at[0], dev_c)
+    landed(oc_o.at[c], R.m_hr.at[1], dev_c)
+    landed(ig_o.at[c], R.m_hr.at[2], dev_c)
+    for cp in outs:
+        cp.wait()
     g5("sae")
-    g5("sad")
-    push(R.gos.at[o], R.gts, R.m_hs.at[4], R.m_hr.at[4], dev_c)
-    spread_out(os_o, c, R.gos.at[c])
-    landed(R.gts, R.m_hr.at[4], dev_c)
-    spread_out(os_o, o, R.gts)
     for cp in sends:
         cp.wait_send()
+
+
+JOBS = (
+    [("gf", 0, r, "win", r) for r in (0, 192, 384, 576)]
+    + [("gf", 1, r, "wfo", r) for r in (0, 192, 384, 576)]
+    + [("gc", 0, 0, "q", 0), ("gc", 0, 192, "co", 0), ("gc", 1, 0, "kv", 0), ("gc", 1, 192, "kv", 192)]
+    + [("gs", 0, 0, "qkv", 0), ("gs", 0, 192, "qkv", 192), ("gs", 1, 0, "qkv", 384)]
+    + [("gs", 1, 192, "out", 0)]
+)
+
+
+def widen(*refs):
+    bo, ig, gf, gs, gc, gn, ge = refs[:7]
+    bo_o, ig_o, qkv_o, out_o, win_o, wfo_o, ng_o, nb_o, q_o, kv_o, co_o, cg_o, cb_o = refs[7:20]
+    low, wide, ig_low, ig_wide, rows, m_in, m_out, m_x = refs[20:]
+    from_ = {"gf": gf, "gs": gs, "gc": gc}
+    to = {"qkv": qkv_o, "out": out_o, "win": win_o, "wfo": wfo_o, "q": q_o, "kv": kv_o, "co": co_o}
+    straight = pltpu.make_async_copy(bo, bo_o, m_x.at[0])
+    straight.start()
+    ig_in = pltpu.make_async_copy(ig, ig_low, m_x.at[1])
+    ig_in.start()
+    loads = []
+    small = [
+        pltpu.make_async_copy(gn, rows.at[pl.ds(0, 4)], m_x.at[3]),
+        pltpu.make_async_copy(ge, rows.at[pl.ds(4, 2)], m_x.at[4]),
+    ]
+    for cp in small:
+        cp.start()
+    for i, (src, piece, r0, dst, d0) in enumerate(JOBS):
+        cp = pltpu.make_async_copy(
+            from_[src].at[piece, :, pl.ds(r0, 192)], low.at[i], m_in.at[i]
+        )
+        cp.start()
+        loads.append(cp)
+    ig_in.wait()
+    ig_wide[...] = ig_low[...].astype(F32)
+    stores = [pltpu.make_async_copy(ig_wide, ig_o, m_x.at[2])]
+    stores[0].start()
+    for cp in small:
+        cp.wait()
+    ng_o[...] = rows[0:2, :]
+    nb_o[...] = rows[2:4, :]
+    cg_o[...] = rows[4:5, :].reshape(D)
+    cb_o[...] = rows[5:6, :].reshape(D)
+    for i, (src, piece, r0, dst, d0) in enumerate(JOBS):
+        loads[i].wait()
+        wide[i, :, 0:384] = low[i, 0].astype(F32)
+        wide[i, :, 384:768] = low[i, 1].astype(F32)
+        cp = pltpu.make_async_copy(wide.at[i], to[dst].at[pl.ds(d0, 192)], m_out.at[i])
+        cp.start()
+        stores.append(cp)
+    for cp in stores:
+        cp.wait()
+    straight.wait()
 
 
 def body(
@@ -718,22 +821,15 @@
     cross_gain,
     cross_bias,
 ):
-    nrm = jnp.concatenate(
-        [
-            norm_gain[0],
-            norm_bias[0],
-            cross_gain[None],
-            cross_bias[None],
-            jnp.zeros((2, D), F32),
-        ],
-        axis=0,
-    )
     ins = (
         layer_inputs[0],
         cotangent,
         doc_groups,
-        retrieved_at[:, 0, :],
-        nrm,
+        retrieved_at,
+        norm_gain[0],
+        norm_bias[0],
+        cross_gain,
+        cross_bias,
         jnp.transpose(sa_qkv[0], (1, 2, 0)).reshape(576, D),
         sa_out[0],
         ffn_in[0],
@@ -747,9 +843,9 @@
     outs = (
         jax.ShapeDtypeStruct((2, TOK, D), BF),
         jax.ShapeDtypeStruct((2, TOK, D), BF),
-        jax.ShapeDtypeStruct((2, 768, D), BF),
-        jax.ShapeDtypeStruct((2, 384, D), BF),
-        jax.ShapeDtypeStruct((2, 384, D), BF),
+        jax.ShapeDtypeStruct((2, 2, 768, 384), BF),
+        jax.ShapeDtypeStruct((2, 2, 384, 384), BF),
+        jax.ShapeDtypeStruct((2, 2, 384, 384), BF),
         jax.ShapeDtypeStruct((4, D), F32),
         jax.ShapeDtypeStruct((2, D), F32),
     )
@@ -758,36 +854,64 @@
     def run(*refs):
         kernel(names, len(ins), len(outs), *refs)
 
-    bo, ig, gf, gs, gc, gn, ge = pl.pallas_call(
+    results = pl.pallas_call(
         run,
         out_shape=outs,
-        in_specs=[hbm, hbm, vm, vm] + [hbm] * 8,
-        out_specs=[vm] * len(outs),
+        in_specs=[hbm, hbm, vm, vm, hbm, hbm, vm, vm] + [hbm] * 7,
+        out_specs=[hbm] * 5 + [vm] * 2,
         scratch_shapes=[s for _, s in scratch_list()],
         compiler_params=pltpu.CompilerParams(
             collective_id=0, has_side_effects=True, vmem_limit_bytes=62 << 20
         ),
         name="layers",
     )(*ins)
-    sa = gs.reshape(768, D)
-    cr = gc.reshape(768, D)
-    d_qkv = jnp.transpose(sa[0:576].astype(F32).reshape(3, 192, D), (2, 0, 1))
-    d_q = jnp.transpose(cr[0:192].astype(F32), (1, 0))
-    d_kv = jnp.transpose(cr[384:768].astype(F32).reshape(2, 192, D), (2, 0, 1))
+    wide_outs = (
+        jax.ShapeDtypeStruct((2, TOK, D), BF),
+        jax.ShapeDtypeStruct((2, TOK, D), F32),
+        jax.ShapeDtypeStruct((576, D), F32),
+        jax.ShapeDtypeStruct((192, D), F32),
+        jax.ShapeDtypeStruct((768, D), F32),
+        jax.ShapeDtypeStruct((768, D), F32),
+        jax.ShapeDtypeStruct((2, D), F32),
+        jax.ShapeDtypeStruct((2, D), F32),
+        jax.ShapeDtypeStruct((192, D), F32),
+        jax.ShapeDtypeStruct((384, D), F32),
+        jax.ShapeDtypeStruct((192, D), F32),
+        jax.ShapeDtypeStruct((D,), F32),
+        jax.ShapeDtypeStruct((D,), F32),
+    )
+    bo, ig, d_qkv, d_out, d_in, d_fo, ng, nb, d_q, d_kv, d_co, dcg, dcb = pl.pallas_call(
+        widen,
+        out_shape=wide_outs,
+        in_specs=[hbm] * 7,
+        out_specs=[hbm] * 6 + [vm] * 2 + [hbm] * 3 + [vm] * 2,
+        scratch_shapes=[
+            VMEM((len(JOBS), 2, 192, 384), BF),
+            VMEM((len(JOBS), 192, D), F32),
+            VMEM((2, TOK, D), BF),
+            VMEM((2, TOK, D), F32),
+            VMEM((8, D), F32),
+            DMA((len(JOBS),)),
+            DMA((len(JOBS),)),
+            DMA((5,)),
+        ],
+        compiler_params=pltpu.CompilerParams(vmem_limit_bytes=32 << 20),
+        name="widen",
+    )(*[pltpu.with_memory_space_constraint(r, pltpu.HBM) for r in results])
     return (
         bo[None],
-        ig.astype(F32)[None],
-        d_qkv[None],
-        sa[576:768].astype(F32)[None],
-        gf[0].astype(F32)[None],
-        gf[1].astype(F32)[None],
-        gn[0:2][None],
-        gn[2:4][None],
-        d_q,
-        d_kv,
-        cr[192:384].astype(F32),
-        ge[0],
-        ge[1],
+        ig[None],
+        jnp.transpose(d_qkv.reshape(3, 192, D), (2, 0, 1))[None],
+        d_out[None],
+        d_in[None],
+        d_fo[None],
+        ng[None],
+        nb[None],
+        jnp.transpose(d_q, (1, 0)),
+        jnp.transpose(d_kv.reshape(2, 192, D), (2, 0, 1)),
+        d_co,
+        dcg,
+        dcb,
     )
 
 

time: 190 us -> 173 us (0.911); the launches traced: 188 us -> 173 us
  other arithmetic: 10.6 us -> 0 us
  local copies, waits for them, and re-layouts: 6.42 us -> 0 us
  Pallas kernels: 170 us -> 172 us
    convert_element_type x2 -> x0, other arithmetic: 6.41 us -> none  [the longest x1 4.27 us: body(): gf[1].astype(F32)[None]]
    broadcast_in_dim x3 -> x0, other arithmetic: 3.14 us -> none  [the longest x1 1.35 us: body(): d_qkv[None]]
    unnamed x14 -> x0, local copies, waits for them, and re-layouts: 2.39 us -> none
    pallas_call x1 -> x2, Pallas kernels: 170 us -> 172 us  [the longest x1 158 us: body(): pl.pallas_call(run, out_shape=outs, in_specs=[hbm, hbm, vm, vm, hbm, hbm,...]
    broadcast_in_dim x4 -> x0, local copies, waits for them, and re-layouts: 1.99 us -> none  [the longest x1 0.69 us: body(): cross_gain[None]]
where the time goes in v2:
time: 173 us
  Pallas kernels  172 us (99%)
    pallas_call x1, Pallas kernels, body(): pl.pallas_call(run, out_shape=outs, in_specs=[hbm, hbm, vm, vm, hbm, hbm,...  158 us
    pallas_call x1, Pallas kernels, body(): pl.pallas_call(widen, out_shape=wide_outs, in_specs=[hbm] * 7, out_specs=...  14 us

profile of v2, /device:TPU:0, one launch (start us, length us, event | category | flops | bytes accessed | tf_op | source)
XLA Modules:
  0.0 172.8 jit_solution(9780581260205229995)
XLA Ops:
  0.7 158.0 %layers.1 = (bf16[2,128,768]{2,1,0:T(8,128)(2,1)}, bf16[2,128,768]{2,1,0:T(8,128)(2,1)}, bf16[2,2,768,384]{3,2,1,0:T(8,128)(2,1)}, bf16[2,2,384,384]{3,2,1,0:T(8...) custom-call(bf16[2,128,768]{2,1,0:T(8,128)(2,1)} %bitcast.35, ...), custom_call_target="tpu_custom_call" | custom-call | tf_op jit(solution)/shard_map/layers/pallas_call | solution.py:857
  158.7 14.0 %widen.1 = (bf16[2,128,768]{2,1,0:T(8,128)(2,1)}, f32[2,128,768]{2,1,0:T(8,128)}, f32[576,768]{1,0:T(8,128)}, f32[192,768]{1,0:T(8,128)}, f32[768,768]{1,0:T(8,1...) custom-call(bf16[2,128,768]{2,1,0:T(8,128)(2,1)} %get-tuple-element., ...), custom_call_target="tpu_custom_call" | custom-call | tf_op jit(solution)/shard_map/widen/pallas_call | solution.py:883

commit v3 on v2

--- a/solution.py
+++ b/solution.py
@@ -69,10 +69,14 @@
         ("dkvct", VMEM((2 * QW, KEYS), BF)),
         ("ptc", VMEM((NH, KEYS, TOK), F32)),
         ("oct", VMEM((QW, TOK), BF)),
-        ("hot", VMEM((16 * TOK, KEYS), BF)),
-        ("kvt", VMEM((16, 2 * QW, TOK), BF)),
-        ("dks", VMEM((16, 2 * QW, TOK), BF)),
-        ("dk1", VMEM((3, 4, 2 * QW, TOK), BF)),
+        ("pos", VMEM((4, 8, KEYS), jnp.int32)),
+        ("hot", VMEM((4, 4 * TOK, KEYS), BF)),
+        ("kvt", VMEM((4, 2 * QW, TOK), BF)),
+        ("kvs", VMEM((4, 2 * QW, KEYS), BF)),
+        ("kvr", VMEM((3, 2 * QW, KEYS), BF)),
+        ("dkr", VMEM((3, 2 * QW, KEYS), BF)),
+        ("dkf", VMEM((4, 2 * QW, TOK), F32)),
+        ("dks", VMEM((4, 2 * QW, TOK), BF)),
         ("dk2", VMEM((3, 2 * QW, TOK), BF)),
         ("dkv", VMEM((2 * QW, TOK), BF)),
         ("vec", VMEM((16, D), F32)),
@@ -83,7 +87,6 @@
         ("ag", VMEM((N_AG, TOK, D), BF)),
         ("rs", VMEM((N_RS, TOK, D), BF)),
         ("rr", VMEM((N_RS, 3, SH, D), BF)),
-        ("kva", VMEM((2 * QW, KEYS), F32)),
         ("gof", VMEM((2, 2, 768, 384), BF)),
         ("gos", VMEM((2, 2, 384, 384), BF)),
         ("goc", VMEM((2, 384, 384), BF)),
@@ -94,8 +97,8 @@
         ("m_agr", DMA((N_AG, 3))),
         ("m_rss", DMA((N_RS, 3))),
         ("m_rsr", DMA((N_RS, 3))),
-        ("m_kvs", DMA((15,))),
-        ("m_kvr", DMA((15,))),
+        ("m_kvs", DMA((9,))),
+        ("m_kvr", DMA((9,))),
         ("m_dks", DMA((6,))),
         ("m_dkr", DMA((6,))),
         ("m_vs", DMA((10,))),
@@ -486,19 +489,7 @@
 
     for j in (10, 11, 12, 13, 14, 15):
         R.vec[j : j + 1, :] = jnp.zeros((1, D), F32)
-    self_forward(0)
-    self_forward(1)
-    self_finish(0)
-    self_finish(1)
-    ag_wait(A_Y1)
-    need(0, 5)
-    need(0, 6)
-    ffn_forward(0, A_Y1)
-
-    for cp in singles:
-        cp.wait()
-    ag_wait(A_Y1 + 1)
-    R.qct[...] = nt(R.wcr[0:192, :], R.ag[A_Y1 + 1]).astype(BF)
+
     micro = lax.broadcasted_iota(jnp.int32, (2, 16), 0)
     group = lax.broadcasted_iota(jnp.int32, (2, 16), 1)
     live = (micro == c) & (group <= d) & (dgr[...] > 0)
@@ -508,48 +499,59 @@
     g_at = rows // TOK
     b_at = jnp.where(c == 0, g_at, lax.rem(g_at, 4) * 4 + g_at // 4)
     at = b_at * TOK + lax.rem(rows, TOK)
+    R.pos[0] = jnp.broadcast_to(at, (8, KEYS))
+    for k in RINGS:
+        push(R.pos.at[0], R.pos.at[k], R.m_kvs.at[5 + k], R.m_kvr.at[5 + k], dev_q(k))
+    self_forward(0)
+    self_forward(1)
+    self_finish(0)
+    self_finish(1)
+    ag_wait(A_Y1)
+    need(0, 5)
+    need(0, 6)
+    ffn_forward(0, A_Y1)
+
+    for cp in singles:
+        cp.wait()
+    ag_wait(A_Y1 + 1)
+    R.qct[...] = nt(R.wcr[0:192, :], R.ag[A_Y1 + 1]).astype(BF)
+    for k in (1, 3, 2):
+        landed(R.pos.at[k], R.m_kvr.at[5 + k], dev_q(k))
 
     def build(i, carry):
-        n = lax.broadcasted_iota(jnp.int32, (TOK, KEYS), 0) + i * TOK
-        R.hot[pl.ds(pl.multiple_of(i * TOK, TOK), TOK), :] = jnp.where(n == at, 1.0, 0.0).astype(BF)
+        n = lax.broadcasted_iota(jnp.int32, (TOK, KEYS), 0) + (q * 4 + i) * TOK
+        rows = pl.ds(pl.multiple_of(i * TOK, TOK), TOK)
+        for k in range(4):
+            R.hot[k, rows, :] = jnp.where(n == R.pos[k, 0:1, :], 1.0, 0.0).astype(BF)
         return carry
 
-    lax.fori_loop(0, 16, build, 0)
+    lax.fori_loop(0, 4, build, 0)
 
     out, n, spread = ln_forward(R.y1f[0] + rs_sum(R_FF), gain_row(0, 1), bias_row(0, 1))
     ag_start(A_BO, out)
     R.n2[0] = n
     put_norm(2, spread)
     ag_wait(A_BO)
-    mine = q * 4 + p
-    R.kvt[mine] = nt(R.wcr[384:768, :], R.ag[A_BO]).astype(BF)
-
-    def kv_send(k, dev, slot, at_block):
-        push(R.kvt.at[at_block], R.kvt.at[at_block], R.m_kvs.at[slot], R.m_kvr.at[slot], dev)
-
-    def gather(b):
-        hot = R.hot[pl.ds(pl.multiple_of(b * TOK, TOK), TOK), :]
-        R.kva[...] += nn(R.kvt[b], hot)
+    R.kvt[p] = nt(R.wcr[384:768, :], R.ag[A_BO]).astype(BF)
 
     for k in RINGS:
-        kv_send(k, dev_p(k), k - 1, mine)
-    for k in RINGS:
-        kv_send(k, dev_q(k), 2 + k, mine)
-    R.kva[...] = jnp.zeros((2 * QW, KEYS), F32)
-    gather(mine)
-    for j in (1, 3, 2):
-        landed(R.kvt.at[mine], R.m_kvr.at[j - 1], dev_p(j))
-        came = q * 4 + lax.rem(p + 4 - j, 4)
-        for k in RINGS:
-            kv_send(k, dev_q(k), 6 + (j - 1) * 3 + k - 1, came)
-        gather(came)
-    for j in (0, 1, 3, 2):
-        for k in (1, 3, 2):
-            slot = 2 + k if j == 0 else 6 + (j - 1) * 3 + k - 1
-            landed(R.kvt.at[mine], R.m_kvr.at[slot], dev_q(k))
-            gather(lax.rem(q + 4 - k, 4) * 4 + lax.rem(p + 4 - j, 4))
-
-    R.kvct[...] = R.kva[...].astype(BF)
+        push(R.kvt.at[p], R.kvt.at[p], R.m_kvs.at[k - 1], R.m_kvr.at[k - 1], dev_p(k))
+    for k in (1, 3, 2):
+        landed(R.kvt.at[p], R.m_kvr.at[k - 1], dev_p(k))
+    column = jnp.concatenate([R.kvt[j] for j in range(4)], axis=1)
+    for k in RINGS + (0,):
+        R.kvs[k] = nn(column, R.hot[k]).astype(BF)
+        if k:
+            push(
+                R.kvs.at[k], R.kvr.at[3 - k], R.m_kvs.at[6 - k], R.m_kvr.at[6 - k], dev_q(4 - k)
+            )
+    for k in (1, 3, 2):
+        landed(R.kvr.at[k - 1], R.m_kvr.at[2 + k], dev_q(k))
+
+    total = R.kvs[0].astype(F32)
+    for k in range(3):
+        total += R.kvr[k].astype(F32)
+    R.kvct[...] = total.astype(BF)
     for h in range(NH):
         lo = h * 64
         st = tn(R.kvct[lo : lo + 64, :], R.qct[lo : lo + 64, :]) * SCALE
@@ -605,20 +607,8 @@
         R.dkvct[lo : lo + 64, :] = dkt.astype(BF)
         R.dkvct[QW + lo : QW + lo + 64, :] = dvt.astype(BF)
 
-    for k in RINGS + (0,):
-        to = lax.rem(q + k, 4)
-        for j in range(4):
-            b = to * 4 + j
-            hot = R.hot[pl.ds(pl.multiple_of(b * TOK, TOK), TOK), :]
-            R.dks[b] = nt(R.dkvct[...], hot).astype(BF)
-        if k:
-            push(
-                R.dks.at[pl.ds(to * 4, 4)],
-                R.dk1.at[k - 1],
-                R.m_dks.at[k - 1],
-                R.m_dkr.at[k - 1],
-                dev_q(k),
-            )
+    for k in RINGS:
+        push(R.dkvct, R.dkr.at[k - 1], R.m_dks.at[k - 1], R.m_dkr.at[k - 1], dev_q(k))
     rs_start(R_DQ, tn(R.dqct[...], R.wcr[0:192, :]))
     put(R.g_crx, 0, 0, nn(R.dqct[...], R.ag[A_Y1 + 1]))
     put(R.g_crx, 0, 192, nn(R.oct[...], R.ag[A_DRC]))
@@ -653,31 +643,33 @@
     def input_part(s):
         rs_start(R_DSA + s, tn(R.dpk[s], R.wsa[s, 0:576, :]))
 
+    for j in range(4):
+        R.dkf[j] = nt(R.dkvct[...], R.hot[0, j * TOK : (j + 1) * TOK, :])
     for k in (1, 3, 2):
-        landed(R.dk1.at[k - 1], R.m_dkr.at[k - 1], dev_q(k))
+        landed(R.dkr.at[k - 1], R.m_dkr.at[k - 1], dev_q(k))
     for k in RINGS + (0,):
         to = lax.rem(p + k, 4)
-        b = q * 4 + to
-        total = R.dks[b].astype(F32)
-        for j in range(3):
-            total += R.dk1[j, to].astype(F32)
-        R.dks[b] = total.astype(BF)
+        part = R.dkf[to]
+        for j in (1, 2, 3):
+            hot = R.hot[j, pl.ds(pl.multiple_of(to * TOK, TOK), TOK), :]
+            part += nt(R.dkr[j - 1], hot)
+        R.dks[to] = part.astype(BF)
         if k:
-            push(R.dks.at[b], R.dk2.at[k - 1], R.m_dks.at[2 + k], R.m_dkr.at[2 + k], dev_p(k))
+            push(R.dks.at[to], R.dk2.at[k - 1], R.m_dks.at[2 + k], R.m_dkr.at[2 + k], dev_p(k))
     self_backward(1)
     input_part(1)
     self_grads(1, R.g_sad)
     g0("sad")
+    g3("ffd")
     for k in (1, 3, 2):
         landed(R.dk2.at[k - 1], R.m_dkr.at[2 + k], dev_p(k))
-    total = R.dks[mine].astype(F32)
+    total = R.dks[p].astype(F32)
     for k in range(3):
         total += R.dk2[k].astype(F32)
     R.dkv[...] = total.astype(BF)
     rs_start(R_DST, tn(R.dkv[...], R.wcr[384:768, :]))
     put(R.g_crx, 1, 0, nn(R.dkv[...], R.ag[A_BO]))
     g0("crx")
-    g3("ffd")
     g1("sad")
     dy = rs_sum(R_DST)
     dr, dg, db = ln_backward(R.n2[0], get_norm(2), gain_row(0, 1), dy)
@@ -762,46 +754,26 @@
 def widen(*refs):
     bo, ig, gf, gs, gc, gn, ge = refs[:7]
     bo_o, ig_o, qkv_o, out_o, win_o, wfo_o, ng_o, nb_o, q_o, kv_o, co_o, cg_o, cb_o = refs[7:20]
-    low, wide, ig_low, ig_wide, rows, m_in, m_out, m_x = refs[20:]
+    wide, ig_wide, m_out, m_x = refs[20:]
     from_ = {"gf": gf, "gs": gs, "gc": gc}
     to = {"qkv": qkv_o, "out": out_o, "win": win_o, "wfo": wfo_o, "q": q_o, "kv": kv_o, "co": co_o}
-    straight = pltpu.make_async_copy(bo, bo_o, m_x.at[0])
-    straight.start()
-    ig_in = pltpu.make_async_copy(ig, ig_low, m_x.at[1])
-    ig_in.start()
-    loads = []
-    small = [
-        pltpu.make_async_copy(gn, rows.at[pl.ds(0, 4)], m_x.at[3]),
-        pltpu.make_async_copy(ge, rows.at[pl.ds(4, 2)], m_x.at[4]),
-    ]
-    for cp in small:
-        cp.start()
+    stores = [pltpu.make_async_copy(bo, bo_o, m_x.at[0])]
+    stores[0].start()
     for i, (src, piece, r0, dst, d0) in enumerate(JOBS):
-        cp = pltpu.make_async_copy(
-            from_[src].at[piece, :, pl.ds(r0, 192)], low.at[i], m_in.at[i]
-        )
-        cp.start()
-        loads.append(cp)
-    ig_in.wait()
-    ig_wide[...] = ig_low[...].astype(F32)
-    stores = [pltpu.make_async_copy(ig_wide, ig_o, m_x.at[2])]
-    stores[0].start()
-    for cp in small:
-        cp.wait()
-    ng_o[...] = rows[0:2, :]
-    nb_o[...] = rows[2:4, :]
-    cg_o[...] = rows[4:5, :].reshape(D)
-    cb_o[...] = rows[5:6, :].reshape(D)
-    for i, (src, piece, r0, dst, d0) in enumerate(JOBS):
-        loads[i].wait()
-        wide[i, :, 0:384] = low[i, 0].astype(F32)
-        wide[i, :, 384:768] = low[i, 1].astype(F32)
+        wide[i, :, 0:384] = from_[src][piece, 0, r0 : r0 + 192, :].astype(F32)
+        wide[i, :, 384:768] = from_[src][piece, 1, r0 : r0 + 192, :].astype(F32)
         cp = pltpu.make_async_copy(wide.at[i], to[dst].at[pl.ds(d0, 192)], m_out.at[i])
         cp.start()
         stores.append(cp)
+    ig_wide[...] = ig[...].astype(F32)
+    stores.append(pltpu.make_async_copy(ig_wide, ig_o, m_x.at[1]))
+    stores[-1].start()
+    ng_o[...] = gn[0:2, :]
+    nb_o[...] = gn[2:4, :]
+    cg_o[...] = ge[0:1, :].reshape(D)
+    cb_o[...] = ge[1:2, :].reshape(D)
     for cp in stores:
         cp.wait()
-    straight.wait()
 
 
 def body(
@@ -841,13 +813,13 @@
     hbm = pl.BlockSpec(memory_space=pl.ANY)
     vm = pl.BlockSpec(memory_space=VMEM)
     outs = (
-        jax.ShapeDtypeStruct((2, TOK, D), BF),
-        jax.ShapeDtypeStruct((2, TOK, D), BF),
-        jax.ShapeDtypeStruct((2, 2, 768, 384), BF),
-        jax.ShapeDtypeStruct((2, 2, 384, 384), BF),
-        jax.ShapeDtypeStruct((2, 2, 384, 384), BF),
-        jax.ShapeDtypeStruct((4, D), F32),
-        jax.ShapeDtypeStruct((2, D), F32),
+        VMEM((2, TOK, D), BF),
+        VMEM((2, TOK, D), BF),
+        VMEM((2, 2, 768, 384), BF),
+        VMEM((2, 2, 384, 384), BF),
+        VMEM((2, 2, 384, 384), BF),
+        VMEM((4, D), F32),
+        VMEM((2, D), F32),
     )
     names = [n for n, _ in scratch_list()]
 
@@ -858,10 +830,10 @@
         run,
         out_shape=outs,
         in_specs=[hbm, hbm, vm, vm, hbm, hbm, vm, vm] + [hbm] * 7,
-        out_specs=[hbm] * 5 + [vm] * 2,
+        out_specs=[vm] * len(outs),
         scratch_shapes=[s for _, s in scratch_list()],
         compiler_params=pltpu.CompilerParams(
-            collective_id=0, has_side_effects=True, vmem_limit_bytes=62 << 20
+            collective_id=0, has_side_effects=True, vmem_limit_bytes=52 << 20
         ),
         name="layers",
     )(*ins)
@@ -883,21 +855,17 @@
     bo, ig, d_qkv, d_out, d_in, d_fo, ng, nb, d_q, d_kv, d_co, dcg, dcb = pl.pallas_call(
         widen,
         out_shape=wide_outs,
-        in_specs=[hbm] * 7,
+        in_specs=[vm] * 7,
         out_specs=[hbm] * 6 + [vm] * 2 + [hbm] * 3 + [vm] * 2,
         scratch_shapes=[
-            VMEM((len(JOBS), 2, 192, 384), BF),
             VMEM((len(JOBS), 192, D), F32),
-            VMEM((2, TOK, D), BF),
             VMEM((2, TOK, D), F32),
-            VMEM((8, D), F32),
             DMA((len(JOBS),)),
-            DMA((len(JOBS),)),
-            DMA((5,)),
+            DMA((2,)),
         ],
         compiler_params=pltpu.CompilerParams(vmem_limit_bytes=32 << 20),
         name="widen",
-    )(*[pltpu.with_memory_space_constraint(r, pltpu.HBM) for r in results])
+    )(*[pltpu.with_memory_space_constraint(r, VMEM) for r in results])
     return (
         bo[None],
         ig[None],

time: 173 us -> 158 us (0.913)
  Pallas kernels: 172 us -> 157 us
    pallas_call x1, Pallas kernels: 14 us -> 4.77 us  [body(): pl.pallas_call(widen, out_shape=wide_outs, in_specs=[vm] * 7, out_specs=[...]
    pallas_call x1, Pallas kernels: 158 us -> 152 us  [body(): pl.pallas_call(run, out_shape=outs, in_specs=[hbm, hbm, vm, vm, hbm, hbm,...]
where the time goes in v3:
time: 158 us
  Pallas kernels  157 us (99%)
    pallas_call x1, Pallas kernels, body(): pl.pallas_call(run, out_shape=outs, in_specs=[hbm, hbm, vm, vm, hbm, hbm,...  152 us
    pallas_call x1, Pallas kernels, body(): pl.pallas_call(widen, out_shape=wide_outs, in_specs=[vm] * 7, out_specs=[...  4.77 us

profile of v3, /device:TPU:0, one launch (start us, length us, event | category | flops | bytes accessed | tf_op | source)
XLA Modules:
  0.0 157.5 jit_solution(7907787320078087044)
XLA Ops:
  0.7 151.9 %layers.1 = (bf16[2,128,768]{2,1,0:T(8,128)(2,1)S(1)}, bf16[2,128,768]{2,1,0:T(8,128)(2,1)S(1)}, bf16[2,2,768,384]{3,2,1,0:T(8,128)(2,1)S(1)}, bf16[2,2,384,384]...) custom-call(bf16[2,128,768]{2,1,0:T(8,128)(2,1)} %bitcast.35, ...), custom_call_target="tpu_custom_call" | custom-call | tf_op jit(solution)/shard_map/layers/pallas_call | solution.py:829
  152.6 4.8 %widen.1 = (bf16[2,128,768]{2,1,0:T(8,128)(2,1)}, f32[2,128,768]{2,1,0:T(8,128)}, f32[576,768]{1,0:T(8,128)}, f32[192,768]{1,0:T(8,128)}, f32[768,768]{1,0:T(8,1...) custom-call(bf16[2,128,768]{2,1,0:T(8,128)(2,1)S(1)} %get-tuple-elem, ...), custom_call_target="tpu_custom_call" | custom-call | tf_op jit(solution)/shard_map/widen/pallas_call | solution.py:855

commit v4 on v3

--- a/solution.py
+++ b/solution.py
@@ -14,6 +14,7 @@
 HEAD = 64
 NH = 3
 EPS = 1e-05
+HEADS = (0, 64, 128)
 SCALE = HEAD**-0.5
 TOK = 128
 D = 768
@@ -61,6 +62,7 @@
         ("dres", VMEM((2, SH, D), F32)),
         ("act", VMEM((2, TOK, D), BF)),
         ("slope", VMEM((2, TOK, D), F32)),
+        ("hid", VMEM((TOK, D), F32)),
         ("du", VMEM((2, TOK, D), BF)),
         ("dpk", VMEM((2, 3 * QW, TOK), BF)),
         ("qct", VMEM((QW, TOK), BF)),
@@ -80,10 +82,10 @@
         ("dk2", VMEM((3, 2 * QW, TOK), BF)),
         ("dkv", VMEM((2 * QW, TOK), BF)),
         ("vec", VMEM((16, D), F32)),
-        ("vx", VMEM((4, 16, D), F32)),
-        ("vc", VMEM((2, 16, D), F32)),
-        ("vy", VMEM((4, 16, D), F32)),
-        ("vz", VMEM((4, 16, D), F32)),
+        ("vx", VMEM((4, 16, D), BF)),
+        ("vc", VMEM((2, 16, D), BF)),
+        ("vy", VMEM((4, 16, D), BF)),
+        ("vz", VMEM((4, 16, D), BF)),
         ("ag", VMEM((N_AG, TOK, D), BF)),
         ("rs", VMEM((N_RS, TOK, D), BF)),
         ("rr", VMEM((N_RS, 3, SH, D), BF)),
@@ -103,19 +105,20 @@
         ("m_dkr", DMA((6,))),
         ("m_vs", DMA((10,))),
         ("m_vr", DMA((10,))),
-        ("m_hs", DMA((3,))),
-        ("m_hr", DMA((3,))),
-        ("m_o", DMA((3,))),
+        ("m_hs", DMA((2,))),
+        ("m_hr", DMA((2,))),
+        ("m_o", DMA((2,))),
     ]
     for name, rows in BLOCKS.items():
         out += [
             ("g_" + name, VMEM((2, 2, rows, 384), BF)),
             ("x_" + name, VMEM((2, rows, 384), BF)),
-            ("a_" + name, VMEM((3, 2, rows // 4, 384), BF)),
+            ("h_" + name, VMEM((2, 2, rows // 8, 384), BF)),
+            ("a_" + name, VMEM((2, 2, rows // 4, 384), BF)),
             ("b_" + name, VMEM((3, rows // 8, 384), BF)),
-            ("s_" + name, DMA((14,))),
-            ("r_" + name, DMA((10,))),
-            ("f_" + name, DMA((2, 4))),
+            ("s_" + name, DMA((18,))),
+            ("r_" + name, DMA((16,))),
+            ("f_" + name, DMA((2, 5))),
         ]
     return out
 
@@ -177,15 +180,20 @@
         return (c, t, lax.rem(z + k, 4) * 4 + y)
 
     dev_c = (o, t, d)
-    sends = []
-
-    def push(src, dst, ss, rs, dev, wait=True):
+    sends = {}
+
+    def flush(kind, keep=0):
+        queue = sends.get(kind, [])
+        while len(queue) > keep:
+            queue.pop(0).wait_send()
+
+    def push(src, dst, ss, rs, dev, kind="", wait=True):
         cp = pltpu.make_async_remote_copy(
             src_ref=src, dst_ref=dst, send_sem=ss, recv_sem=rs, device_id=dev, device_id_type=MESH
         )
         cp.start()
         if wait:
-            sends.append(cp)
+            sends.setdefault(kind, []).append(cp)
         return cp
 
     def landed(dst, rs, dev):
@@ -253,9 +261,11 @@
                 R.m_rss.at[i, k - 1],
                 R.m_rsr.at[i, k - 1],
                 dev_x(k),
+                "x",
             )
 
     def rs_sum(i):
+        flush("x", 9)
         for k in (1, 3, 2):
             landed(R.rr.at[i, k - 1], R.m_rsr.at[i, k - 1], dev_x(k))
         total = R.rs[i, rows_t, :].astype(F32)
@@ -272,9 +282,11 @@
                 R.m_ags.at[i, k - 1],
                 R.m_agr.at[i, k - 1],
                 dev_x(k),
+                "x",
             )
 
     def ag_wait(i):
+        flush("x", 9)
         for k in (1, 3, 2):
             landed(R.ag.at[i, rows_t], R.m_agr.at[i, k - 1], dev_x(k))
 
@@ -286,24 +298,39 @@
 
     cross_gain = cg[...].reshape(1, D)
     cross_bias = cb[...].reshape(1, D)
+
+    def softmax(scores):
+        tops = [jnp.max(st, axis=0, keepdims=True) for st in scores]
+        exps = [jnp.exp(st - top) for st, top in zip(scores, tops)]
+        sums = [jnp.sum(e, axis=0, keepdims=True) for e in exps]
+        return [e / total for e, total in zip(exps, sums)]
+
+    def attend_backward(qts, kts, vts, prs, dots):
+        heads = range(NH)
+        dpts = [tn(vts[h], dots[h]) for h in heads]
+        dvts = [nt(dots[h], prs[h].astype(BF)) for h in heads]
+        sums = [jnp.sum(dpts[h] * prs[h], axis=0, keepdims=True) for h in heads]
+        dsts = [(prs[h] * (dpts[h] - sums[h])).astype(BF) for h in heads]
+        dqts = [nn(kts[h], dsts[h]) * SCALE for h in heads]
+        dkts = [nt(qts[h], dsts[h]) * SCALE for h in heads]
+        return dqts, dkts, dvts
 
     def self_forward(s):
         need(s, 0)
         need(s, 1)
         R.pk[s] = nt(R.wsa[s, 0:576, :], R.xin[s]).astype(BF)
-        for h in range(NH):
-            qt = R.pk[s, h * 64 : h * 64 + 64, :]
-            kt = R.pk[s, QW + h * 64 : QW + h * 64 + 64, :]
-            vt = R.pk[s, 2 * QW + h * 64 : 2 * QW + h * 64 + 64, :]
-            st = tn(kt, qt) * SCALE
-            if s == 1:
-                key = lax.broadcasted_iota(jnp.int32, (TOK, TOK), 0)
-                qry = lax.broadcasted_iota(jnp.int32, (TOK, TOK), 1)
-                st = jnp.where(key <= qry, st, -1000000000.0)
-            e = jnp.exp(st - jnp.max(st, axis=0, keepdims=True))
-            pr = e / jnp.sum(e, axis=0, keepdims=True)
-            R.pt[s, h] = pr
-            R.ot[s, h * 64 : h * 64 + 64, :] = nn(vt, pr.astype(BF)).astype(BF)
+        scores = [
+            tn(R.pk[s, QW + lo : QW + lo + 64, :], R.pk[s, lo : lo + 64, :]) * SCALE for lo in HEADS
+        ]
+        if s == 1:
+            key = lax.broadcasted_iota(jnp.int32, (TOK, TOK), 0)
+            qry = lax.broadcasted_iota(jnp.int32, (TOK, TOK), 1)
+            scores = [jnp.where(key <= qry, st, -1000000000.0) for st in scores]
+        probs = softmax(scores)
+        for h, lo in enumerate(HEADS):
+            vt = R.pk[s, 2 * QW + lo : 2 * QW + lo + 64, :]
+            R.ot[s, lo : lo + 64, :] = nn(vt, probs[h].astype(BF)).astype(BF)
+            R.pt[s, h] = probs[h]
         need(s, 2)
         rs_start(R_SA + s, tn(R.ot[s], R.wsa[s, 576:768, :]))
 
@@ -328,8 +355,11 @@
         u = nn(R.ag[gathered], R.wff[s, 0])
         cdf = 0.5 * (1.0 + lax.erf(u * 0.7071067811865476))
         R.act[s] = (u * cdf).astype(BF)
-        R.slope[s] = cdf + u * jnp.exp(-0.5 * u * u) * 0.3989422804014327
+        R.hid[...] = u
+        R.slope[s] = cdf
         rs_start(R_FF + s, nn(R.act[s], R.wff[s, 1]))
+        u = R.hid[...]
+        R.slope[s] += u * jnp.exp(-0.5 * u * u) * 0.3989422804014327
 
     def ffn_backward(s):
         ag_wait(A_DR2 + s)
@@ -359,7 +389,7 @@
 
     def g0(name):
         g, x, a, b, s, r = blk(name)
-        push(g.at[o], x, s.at[0], r.at[0], dev_c)
+        push(g.at[o], x, s.at[0], r.at[0], dev_c, name)
 
     def p_rows(name, at):
         quarter = BLOCKS[name] // 4
@@ -368,40 +398,58 @@
     def q_rows(name, at_p, at_q):
         quarter, eighth = BLOCKS[name] // 4, BLOCKS[name] // 8
         return pl.ds(pl.multiple_of(at_p * quarter + (at_q // 2) * eighth, eighth), eighth)
+
+    def half_rows(name, at, half):
+        quarter, eighth = BLOCKS[name] // 4, BLOCKS[name] // 8
+        return pl.ds(pl.multiple_of(at * quarter + half * eighth, eighth), eighth)
+
+    def p_at(k):
+        return lax.rem(p + k, 4)
 
     def g1(name):
         g, x, a, b, s, r = blk(name)
         landed(x, r.at[0], dev_c)
         g[c] = (g[c].astype(F32) + x[...].astype(F32)).astype(BF)
-        for k in RINGS:
-            to = lax.rem(p + k, 4)
+        h = getattr(R, "h_" + name)
+        for i, k in ((0, 1), (1, 3)):
+            part = g.at[c, :, half_rows(name, p_at(2), i)]
+            push(part, h.at[i], s.at[1 + i], r.at[1 + i], dev_p(k), name)
+
+    def g1b(name):
+        g, x, a, b, s, r = blk(name)
+        h = getattr(R, "h_" + name)
+        for i, k in ((0, 1), (1, 3)):
+            landed(h.at[i], r.at[1 + i], dev_p(k))
+            part = half_rows(name, p_at(k), i)
+            g[c, :, part, :] = (g[c, :, part, :].astype(F32) + h[i].astype(F32)).astype(BF)
             push(
-                g.at[c, :, p_rows(name, to)], a.at[k - 1], s.at[k], r.at[k], dev_p(k)
+                g.at[c, :, p_rows(name, p_at(k))], a.at[i], s.at[3 + i], r.at[3 + i], dev_p(k), name
             )
 
     def g2(name):
         g, x, a, b, s, r = blk(name)
-        for k in (1, 3, 2):
-            landed(a.at[k - 1], r.at[k], dev_p(k))
         mine = p_rows(name, p)
         total = g[c, :, mine, :].astype(F32)
-        for k in range(3):
-            total += a[k].astype(F32)
+        for i in (0, 1):
+            landed(a.at[i], r.at[3 + i], dev_p(1))
+            total += a[i].astype(F32)
         g[c, :, mine, :] = total.astype(BF)
         for k in RINGS:
             to = lax.rem(q + k, 4)
             push(
                 g.at[c, lax.rem(to, 2), q_rows(name, p, to)],
                 b.at[k - 1],
-                s.at[3 + k],
-                r.at[3 + k],
+                s.at[4 + k],
+                r.at[4 + k],
                 dev_q(k),
+                name,
             )
 
     def g3(name):
         g, x, a, b, s, r = blk(name)
+        flush(name, 3)
         for k in (1, 3, 2):
-            landed(b.at[k - 1], r.at[3 + k], dev_q(k))
+            landed(b.at[k - 1], r.at[4 + k], dev_q(k))
         rows, half = q_rows(name, p, q), lax.rem(q, 2)
         total = g[c, half, rows, :].astype(F32)
         for k in range(3):
@@ -409,79 +457,115 @@
         fin = goal[name]
         fin[half, rows, :] = total.astype(BF)
         for k in RINGS:
-            push(fin.at[half, rows], fin.at[half, rows], s.at[6 + k], r.at[6 + k], dev_q(k))
+            push(fin.at[half, rows], fin.at[half, rows], s.at[7 + k], r.at[7 + k], dev_q(k), name)
 
     final = {"ffd": (1, of_o), "ffe": (0, of_o), "sad": (1, os_o), "sae": (0, os_o)}
+
+    def hop(name, rows, j):
+        owner, dst = final[name]
+        fin, f = goal[name], getattr(R, "f_" + name)
+
+        @pl.when(c == owner)
+        def _():
+            pltpu.make_async_copy(fin.at[:, rows], dst.at[c, :, rows], f.at[c, j]).start()
+
+        @pl.when(c != owner)
+        def _():
+            s = getattr(R, "s_" + name)
+            push(fin.at[:, rows], dst.at[c, :, rows], s.at[15 + j], f.at[c, j], dev_c, wait=False)
+
+    def hop_gone(name, rows, j):
+        owner, dst = final[name]
+        fin, f = goal[name], getattr(R, "f_" + name)
+
+        @pl.when(c != owner)
+        def _():
+            s = getattr(R, "s_" + name)
+            pltpu.make_async_remote_copy(
+                src_ref=fin.at[:, rows],
+                dst_ref=dst.at[c, :, rows],
+                send_sem=s.at[15 + j],
+                recv_sem=f.at[c, j],
+                device_id=dev_c,
+                device_id_type=MESH,
+            ).wait_send()
 
     def g4(name):
         g, x, a, b, s, r = blk(name)
         fin = goal[name]
         for k in (1, 3, 2):
-            landed(fin.at[lax.rem(q, 2), q_rows(name, p, q)], r.at[6 + k], dev_q(k))
+            landed(fin.at[lax.rem(q, 2), q_rows(name, p, q)], r.at[7 + k], dev_q(k))
         mine = p_rows(name, p)
+        for i, k in ((0, 1), (1, 3)):
+            push(fin.at[:, mine], fin.at[:, mine], s.at[11 + i], r.at[11 + i], dev_p(k), name)
+        if name in final:
+            hop(name, mine, 0)
+
+    def g4b(name):
+        g, x, a, b, s, r = blk(name)
+        fin = goal[name]
+        for i, k in ((0, 1), (1, 3)):
+            landed(fin.at[:, p_rows(name, p)], r.at[11 + i], dev_p(k))
+            part = half_rows(name, p_at(4 - k), i)
+            if name in final:
+                owner, dst = final[name]
+                f = getattr(R, "f_" + name)
+                to = (owner, t, dp_p(k))
+                push(
+                    fin.at[:, part], dst.at[c, :, part], s.at[13 + i], f.at[c, 3 + i], to, name
+                )
+            else:
+                push(
+                    fin.at[:, part], fin.at[:, part], s.at[13 + i], r.at[13 + i], dev_p(k), name
+                )
+        if name in final:
+            for i, k in ((0, 1), (1, 3)):
+                hop(name, p_rows(name, p_at(4 - k)), 1 + i)
+
+    def g5(name):
+        g, x, a, b, s, r = blk(name)
+        flush(name, 2)
+        fin = goal[name]
         if name not in final:
-            for k in RINGS:
-                push(
-                    fin.at[:, mine], fin.at[:, mine], s.at[9 + k], R.f_crx.at[c, k], dev_p(k)
-                )
+            f = getattr(R, "f_" + name)
+            for i, k in ((0, 1), (1, 3)):
+                landed(fin.at[:, half_rows(name, p, i)], r.at[13 + i], dev_p(k))
+            push(fin, oc_o.at[c], s.at[15], f.at[c, 0], dev_c, name)
+            pltpu.make_async_copy(fin, oc_o.at[c], f.at[c, 1]).start()
+
+    def g6(name):
+        f = getattr(R, "f_" + name)
+        if name not in final:
+            landed(oc_o.at[o], f.at[o, 0], dev_c)
+            landed(oc_o.at[c], f.at[c, 1], dev_c)
             return
         owner, dst = final[name]
-        f = getattr(R, "f_" + name)
-        for k in RINGS:
-            push(
-                fin.at[:, mine], dst.at[c, :, mine], s.at[9 + k], f.at[c, k], (owner, t, dp_p(k))
-            )
-
-        @pl.when(c == owner)
-        def _():
-            pltpu.make_async_copy(fin.at[:, mine], dst.at[c, :, mine], f.at[c, 0]).start()
-
-        @pl.when(c != owner)
-        def _():
-            push(fin.at[:, mine], dst.at[c, :, mine], s.at[13], f.at[c, 0], dev_c, False)
-
-    def g5(name):
-        fin = goal[name]
-        mine = p_rows(name, p)
-        if name not in final:
-            for k in (1, 3, 2):
-                landed(fin.at[:, mine], R.f_crx.at[c, k], dev_p(k))
-            return
-        owner, dst = final[name]
-        f = getattr(R, "f_" + name)
 
         @pl.when(c == owner)
         def _():
             for piece in (0, 1):
-                for k in range(4):
-                    landed(dst.at[piece, :, mine], f.at[piece, k], dev_p(1))
-
-        @pl.when(c != owner)
-        def _():
-            pltpu.make_async_remote_copy(
-                src_ref=fin.at[:, mine],
-                dst_ref=dst.at[c, :, mine],
-                send_sem=getattr(R, "s_" + name).at[13],
-                recv_sem=f.at[c, 0],
-                device_id=dev_c,
-                device_id_type=MESH,
-            ).wait_send()
+                for j in range(5):
+                    rows = p_rows(name, p) if j < 3 else half_rows(name, p, 0)
+                    landed(dst.at[piece, :, rows], f.at[piece, j], dev_c)
+
+        for j, k in ((0, 0), (1, 3), (2, 1)):
+            hop_gone(name, p_rows(name, p_at(k)), j)
 
     def vec_put(row, dg, db, step=2):
         R.vec[row : row + 1, :] = dg
         R.vec[row + step : row + step + 1, :] = db
 
     def vec_send(buf, at, value, base, dev, count):
-        buf[at] = value
+        buf[at] = value.astype(BF)
         for k in range(1, count):
             push(buf.at[at], buf.at[at], R.m_vs.at[base + k - 1], R.m_vr.at[base + k - 1], dev(k))
 
     def vec_sum(buf, at, base, dev, count):
         for k in range(1, count):
             landed(buf.at[at], R.m_vr.at[base + k - 1], dev(k))
-        total = buf[0]
+        total = buf[0].astype(F32)
         for k in range(1, count):
-            total += buf[k]
+            total += buf[k].astype(F32)
         return total
 
     def dev_c1(k):
@@ -552,13 +636,13 @@
     for k in range(3):
         total += R.kvr[k].astype(F32)
     R.kvct[...] = total.astype(BF)
-    for h in range(NH):
-        lo = h * 64
-        st = tn(R.kvct[lo : lo + 64, :], R.qct[lo : lo + 64, :]) * SCALE
-        e = jnp.exp(st - jnp.max(st, axis=0, keepdims=True))
-        pr = e / jnp.sum(e, axis=0, keepdims=True)
-        R.ptc[h] = pr
-        R.oct[lo : lo + 64, :] = nn(R.kvct[QW + lo : QW + lo + 64, :], pr.astype(BF)).astype(BF)
+    probs = softmax(
+        [tn(R.kvct[lo : lo + 64, :], R.qct[lo : lo + 64, :]) * SCALE for lo in HEADS]
+    )
+    for h, lo in enumerate(HEADS):
+        vt = R.kvct[QW + lo : QW + lo + 64, :]
+        R.oct[lo : lo + 64, :] = nn(vt, probs[h].astype(BF)).astype(BF)
+        R.ptc[h] = probs[h]
     rs_start(R_CR, tn(R.oct[...], R.wcr[192:384, :]))
     need(1, 5)
     need(1, 6)
@@ -577,6 +661,7 @@
     vec_put(5, dg, db)
     ffn_backward(1)
     ag_start(A_BO + 1, out)
+    flush("")
     ffn_grads(1, A_Y2, R.g_ffd)
     g0("ffd")
     dy = R.dres[1] + rs_sum(R_DFF + 1)
@@ -587,53 +672,45 @@
     g1("ffd")
     ag_wait(A_DRC)
 
-    def attend_backward(qt, kt, vt, pr, dot):
-        dvt = nt(dot, pr.astype(BF))
-        dpt = tn(vt, dot)
-        dst = (pr * (dpt - jnp.sum(dpt * pr, axis=0, keepdims=True))).astype(BF)
-        return nn(kt, dst) * SCALE, nt(qt, dst) * SCALE, dvt
-
     doc = nt(R.wcr[192:384, :], R.ag[A_DRC]).astype(BF)
-    for h in range(NH):
-        lo = h * 64
-        dqt, dkt, dvt = attend_backward(
-            R.qct[lo : lo + 64, :],
-            R.kvct[lo : lo + 64, :],
-            R.kvct[QW + lo : QW + lo + 64, :],
-            R.ptc[h],
-            doc[lo : lo + 64, :],
-        )
-        R.dqct[lo : lo + 64, :] = dqt.astype(BF)
-        R.dkvct[lo : lo + 64, :] = dkt.astype(BF)
-        R.dkvct[QW + lo : QW + lo + 64, :] = dvt.astype(BF)
+    dqts, dkts, dvts = attend_backward(
+        [R.qct[lo : lo + 64, :] for lo in HEADS],
+        [R.kvct[lo : lo + 64, :] for lo in HEADS],
+        [R.kvct[QW + lo : QW + lo + 64, :] for lo in HEADS],
+        [R.ptc[h] for h in range(NH)],
+        [doc[lo : lo + 64, :] for lo in HEADS],
+    )
+    for h, lo in enumerate(HEADS):
+        R.dkvct[lo : lo + 64, :] = dkts[h].astype(BF)
+        R.dkvct[QW + lo : QW + lo + 64, :] = dvts[h].astype(BF)
+        R.dqct[lo : lo + 64, :] = dqts[h].astype(BF)
 
     for k in RINGS:
         push(R.dkvct, R.dkr.at[k - 1], R.m_dks.at[k - 1], R.m_dkr.at[k - 1], dev_q(k))
     rs_start(R_DQ, tn(R.dqct[...], R.wcr[0:192, :]))
     put(R.g_crx, 0, 0, nn(R.dqct[...], R.ag[A_Y1 + 1]))
     put(R.g_crx, 0, 192, nn(R.oct[...], R.ag[A_DRC]))
+    g1b("ffd")
     dy = R.dres[1] + rs_sum(R_DQ)
     dr, dg, db = ln_backward(R.n1[1], get_norm(1), gain_row(1, 0), dy)
     ag_start(A_DR1 + 1, dr)
     R.dres[1] = dr
     vec_put(4, dg, db)
-    g2("ffd")
 
     def self_backward(s):
         ag_wait(A_DR1 + s)
         dot = nt(R.wsa[s, 576:768, :], R.ag[A_DR1 + s]).astype(BF)
-        for h in range(NH):
-            lo = h * 64
-            dqt, dkt, dvt = attend_backward(
-                R.pk[s, lo : lo + 64, :],
-                R.pk[s, QW + lo : QW + lo + 64, :],
-                R.pk[s, 2 * QW + lo : 2 * QW + lo + 64, :],
-                R.pt[s, h],
-                dot[lo : lo + 64, :],
-            )
-            R.dpk[s, lo : lo + 64, :] = dqt.astype(BF)
-            R.dpk[s, QW + lo : QW + lo + 64, :] = dkt.astype(BF)
-            R.dpk[s, 2 * QW + lo : 2 * QW + lo + 64, :] = dvt.astype(BF)
+        dqts, dkts, dvts = attend_backward(
+            [R.pk[s, lo : lo + 64, :] for lo in HEADS],
+            [R.pk[s, QW + lo : QW + lo + 64, :] for lo in HEADS],
+            [R.pk[s, 2 * QW + lo : 2 * QW + lo + 64, :] for lo in HEADS],
+            [R.pt[s, h] for h in range(NH)],
+            [dot[lo : lo + 64, :] for lo in HEADS],
+        )
+        for h, lo in enumerate(HEADS):
+            R.dpk[s, lo : lo + 64, :] = dqts[h].astype(BF)
+            R.dpk[s, QW + lo : QW + lo + 64, :] = dkts[h].astype(BF)
+            R.dpk[s, 2 * QW + lo : 2 * QW + lo + 64, :] = dvts[h].astype(BF)
 
     def self_grads(s, ref):
         put(ref, 0, 0, nn(R.dpk[s, 0:384, :], R.xin[s]))
@@ -656,11 +733,11 @@
         R.dks[to] = part.astype(BF)
         if k:
             push(R.dks.at[to], R.dk2.at[k - 1], R.m_dks.at[2 + k], R.m_dkr.at[2 + k], dev_p(k))
+    g2("ffd")
     self_backward(1)
     input_part(1)
     self_grads(1, R.g_sad)
     g0("sad")
-    g3("ffd")
     for k in (1, 3, 2):
         landed(R.dk2.at[k - 1], R.m_dkr.at[2 + k], dev_p(k))
     total = R.dks[p].astype(F32)
@@ -670,19 +747,23 @@
     rs_start(R_DST, tn(R.dkv[...], R.wcr[384:768, :]))
     put(R.g_crx, 1, 0, nn(R.dkv[...], R.ag[A_BO]))
     g0("crx")
+    g3("ffd")
     g1("sad")
     dy = rs_sum(R_DST)
     dr, dg, db = ln_backward(R.n2[0], get_norm(2), gain_row(0, 1), dy)
     ag_start(A_DR2, dr)
     R.dres[0] = dr
     vec_put(1, dg, db)
+    g1("crx")
     g4("ffd")
-    g1("crx")
+    g1b("sad")
+    flush("")
     ffn_backward(0)
     ffn_grads(0, A_Y1, R.g_ffe)
     g0("ffe")
+    g1b("crx")
     g2("sad")
-    ag_start(A_IG + 1, R.dres[1] + rs_sum(R_DSA + 1))
+    g4b("ffd")
     dy = R.dres[0] + rs_sum(R_DFF)
     dr, dg, db = ln_backward(R.n1[0], get_norm(0), gain_row(0, 0), dy)
     ag_start(A_DR1, dr)
@@ -690,56 +771,62 @@
     vec_put(0, dg, db)
     vec_send(R.vx, t, R.vec[...], 0, dev_x, 4)
     g1("ffe")
+    ag_start(A_IG + 1, R.dres[1] + rs_sum(R_DSA + 1))
     g2("crx")
-    g3("sad")
     self_backward(0)
+    g1b("ffe")
     self_grads(0, R.g_sae)
     g0("sae")
     input_part(0)
+    g3("sad")
+    g3("crx")
     total = vec_sum(R.vx, t, 0, dev_x, 4)
     vec_send(R.vc, c, total, 3, dev_c1, 2)
-    g4("sad")
-    g3("crx")
     g1("sae")
-    g2("ffe")
     total = vec_sum(R.vc, c, 3, dev_c1, 2)
     vec_send(R.vy, y, total, 4, dev_y, 4)
     ag_start(A_IG, R.dres[0] + rs_sum(R_DSA))
+    g2("ffe")
+    g1b("sae")
+    g4("sad")
     g4("crx")
+    total = vec_sum(R.vy, y, 4, dev_y, 4)
+    vec_send(R.vz, z, total, 7, dev_z, 4)
     ag_wait(A_BO + 1)
     push(R.ag.at[A_BO + o], bo_o.at[c], R.m_hs.at[0], R.m_hr.at[0], dev_c)
     outs = [pltpu.make_async_copy(R.ag.at[A_BO + c], bo_o.at[c], R.m_o.at[0])]
     outs[0].start()
     g3("ffe")
     g2("sae")
-    total = vec_sum(R.vy, y, 4, dev_y, 4)
-    vec_send(R.vz, z, total, 7, dev_z, 4)
-    g4("ffe")
-    g3("sae")
-    g5("crx")
-    push(R.goc, oc_o.at[c], R.m_hs.at[1], R.m_hr.at[1], dev_c)
-    outs.append(pltpu.make_async_copy(R.goc, oc_o.at[c], R.m_o.at[1]))
-    outs[1].start()
     ag_wait(A_IG)
     ag_wait(A_IG + 1)
-    push(R.ag.at[A_IG + o], ig_o.at[c], R.m_hs.at[2], R.m_hr.at[2], dev_c)
-    outs.append(pltpu.make_async_copy(R.ag.at[A_IG + c], ig_o.at[c], R.m_o.at[2]))
-    outs[2].start()
+    push(R.ag.at[A_IG + o], ig_o.at[c], R.m_hs.at[1], R.m_hr.at[1], dev_c)
+    outs.append(pltpu.make_async_copy(R.ag.at[A_IG + c], ig_o.at[c], R.m_o.at[1]))
+    outs[1].start()
+    g4b("sad")
+    g4b("crx")
     total = vec_sum(R.vz, z, 7, dev_z, 4)
     on_o[...] = jnp.where(c == 0, total[0:4, :], total[4:8, :])
     oe_o[...] = total[8:10, :]
+    g4("ffe")
+    g3("sae")
+    flush("x")
+    flush("")
+    g5("crx")
     g4("sae")
-    g5("ffd")
-    g5("sad")
-    g5("ffe")
+    g4b("ffe")
+    g4b("sae")
     landed(bo_o.at[c], R.m_hr.at[0], dev_c)
-    landed(oc_o.at[c], R.m_hr.at[1], dev_c)
-    landed(ig_o.at[c], R.m_hr.at[2], dev_c)
+    landed(ig_o.at[c], R.m_hr.at[1], dev_c)
     for cp in outs:
         cp.wait()
-    g5("sae")
-    for cp in sends:
-        cp.wait_send()
+    g6("ffd")
+    g6("sad")
+    g6("crx")
+    g6("ffe")
+    g6("sae")
+    for kind in list(sends):
+        flush(kind)
 
 
 JOBS = (

time: 158 us -> 154 us (0.975)
  Pallas kernels: 157 us -> 154 us
    pallas_call x1, Pallas kernels: 152 us -> 149 us  [body(): pl.pallas_call(run, out_shape=outs, in_specs=[hbm, hbm, vm, vm, hbm, hbm,...]
where the time goes in v4:
time: 154 us
  Pallas kernels  154 us (100%)
    pallas_call x1, Pallas kernels, body(): pl.pallas_call(run, out_shape=outs, in_specs=[hbm, hbm, vm, vm, hbm, hbm,...  149 us
    pallas_call x1, Pallas kernels, body(): pl.pallas_call(widen, out_shape=wide_outs, in_specs=[vm] * 7, out_specs=[...  4.77 us

profile of v4, /device:TPU:0, one launch (start us, length us, event | category | flops | bytes accessed | tf_op | source)
XLA Modules:
  0.0 154.3 jit_solution(12023485690480462423)
XLA Ops:
  0.7 148.7 %layers.1 = (bf16[2,128,768]{2,1,0:T(8,128)(2,1)S(1)}, bf16[2,128,768]{2,1,0:T(8,128)(2,1)S(1)}, bf16[2,2,768,384]{3,2,1,0:T(8,128)(2,1)S(1)}, bf16[2,2,384,384]...) custom-call(bf16[2,128,768]{2,1,0:T(8,128)(2,1)} %bitcast.35, ...), custom_call_target="tpu_custom_call" | custom-call | tf_op jit(solution)/shard_map/layers/pallas_call | solution.py:916
  149.4 4.8 %widen.1 = (bf16[2,128,768]{2,1,0:T(8,128)(2,1)}, f32[2,128,768]{2,1,0:T(8,128)}, f32[576,768]{1,0:T(8,128)}, f32[192,768]{1,0:T(8,128)}, f32[768,768]{1,0:T(8,1...) custom-call(bf16[2,128,768]{2,1,0:T(8,128)(2,1)S(1)} %get-tuple-elem, ...), custom_call_target="tpu_custom_call" | custom-call | tf_op jit(solution)/shard_map/widen/pallas_call | solution.py:942

commit v5 on v4

--- a/solution.py
+++ b/solution.py
@@ -27,7 +27,12 @@
 N_AG = 12
 R_SA, R_FF, R_CR, R_DFF, R_DQ, R_DSA, R_DST = 0, 2, 4, 5, 7, 8, 10
 N_RS = 11
-BLOCKS = {"ffd": 768, "ffe": 768, "crx": 384, "sad": 384, "sae": 384}
+BLOCKS = {"ffd": 768, "ffo": 384, "ffi": 384, "crx": 384, "sad": 384, "sae": 384}
+WORKER = {"ffd": 1, "crx": 1, "sad": 1, "ffo": 0, "ffi": 0, "sae": 1}
+OWNER = {"ffd": 1, "sad": 1, "ffo": 0, "ffi": 0, "sae": 0}
+GROUP = {"ffd": "a", "crx": "b", "ffo": "b", "sad": "c", "ffi": "c", "sae": "d"}
+SECOND_RS = (R_SA + 1, R_DSA + 1)
+SECOND_AG = (A_BO + 1, A_IG + 1, A_Y1 + 1)
 
 
 def nn(a, b):
@@ -89,37 +94,34 @@
         ("ag", VMEM((N_AG, TOK, D), BF)),
         ("rs", VMEM((N_RS, TOK, D), BF)),
         ("rr", VMEM((N_RS, 3, SH, D), BF)),
-        ("gof", VMEM((2, 2, 768, 384), BF)),
-        ("gos", VMEM((2, 2, 384, 384), BF)),
-        ("goc", VMEM((2, 384, 384), BF)),
         ("m_w", DMA((2, 7))),
         ("m_ws", DMA((7,))),
         ("m_l", DMA((4,))),
-        ("m_ags", DMA((N_AG, 3))),
-        ("m_agr", DMA((N_AG, 3))),
-        ("m_rss", DMA((N_RS, 3))),
-        ("m_rsr", DMA((N_RS, 3))),
-        ("m_kvs", DMA((9,))),
+        ("m_ags", DMA((2, 3))),
+        ("m_agr", DMA((2, 3))),
+        ("m_rss", DMA((2, 3))),
+        ("m_rsr", DMA((2, 3))),
+        ("m_dps", DMA((10,))),
         ("m_kvr", DMA((9,))),
-        ("m_dks", DMA((6,))),
         ("m_dkr", DMA((6,))),
-        ("m_vs", DMA((10,))),
         ("m_vr", DMA((10,))),
         ("m_hs", DMA((2,))),
-        ("m_hr", DMA((2,))),
+        ("m_hr", DMA((3,))),
+        ("m_g0", DMA((len(BLOCKS), 2))),
+        ("f_sae", DMA((2, 5))),
         ("m_o", DMA((2,))),
     ]
     for name, rows in BLOCKS.items():
         out += [
             ("g_" + name, VMEM((2, 2, rows, 384), BF)),
-            ("x_" + name, VMEM((2, rows, 384), BF)),
-            ("h_" + name, VMEM((2, 2, rows // 8, 384), BF)),
-            ("a_" + name, VMEM((2, 2, rows // 4, 384), BF)),
-            ("b_" + name, VMEM((3, rows // 8, 384), BF)),
-            ("s_" + name, DMA((18,))),
-            ("r_" + name, DMA((16,))),
-            ("f_" + name, DMA((2, 5))),
+            ("x_" + name, VMEM((2, 2, rows, 384), BF)),
+            ("h_" + name, VMEM((2, 2, 2, rows // 8, 384), BF)),
+            ("a_" + name, VMEM((2, 2, 2, rows // 4, 384), BF)),
+            ("b_" + name, VMEM((2, 3, rows // 8, 384), BF)),
         ]
+    for group in sorted(set(GROUP.values())):
+        out.append(("s_" + group, DMA((2, 6 if group == GROUP["sae"] else 3))))
+        out.append(("r_" + group, DMA((2, 9 if group == GROUP["sae"] else 11))))
     return out
 
 
@@ -218,6 +220,7 @@
     for k in (1, 2, 3):
         for dev in (dev_x(k), dev_y(k), dev_z(k)):
             peers.append(dev)
+    for k in (1, 3):
         peers.append((o,) + dev_y(k)[1:])
         peers.append((o,) + dev_z(k)[1:])
     for dev in peers:
@@ -252,43 +255,45 @@
         pltpu.make_async_copy(src, places(s)[i], R.m_w.at[s, i]).wait()
 
     def rs_start(i, value):
+        m = int(i in SECOND_RS)
+        flush(("rs", m))
         R.rs[i] = value.astype(BF)
         for k in RINGS:
             to = lax.rem(t + k, 4)
             push(
                 R.rs.at[i, pl.ds(pl.multiple_of(to * SH, SH), SH)],
                 R.rr.at[i, k - 1],
-                R.m_rss.at[i, k - 1],
-                R.m_rsr.at[i, k - 1],
+                R.m_rss.at[m, k - 1],
+                R.m_rsr.at[m, k - 1],
                 dev_x(k),
-                "x",
+                ("rs", m),
             )
 
     def rs_sum(i):
-        flush("x", 9)
         for k in (1, 3, 2):
-            landed(R.rr.at[i, k - 1], R.m_rsr.at[i, k - 1], dev_x(k))
+            landed(R.rr.at[i, k - 1], R.m_rsr.at[int(i in SECOND_RS), k - 1], dev_x(k))
         total = R.rs[i, rows_t, :].astype(F32)
         for k in range(3):
             total += R.rr[i, k].astype(F32)
         return total
 
     def ag_start(i, value):
+        m = int(i in SECOND_AG)
+        flush(("ag", m))
         R.ag[i, rows_t, :] = value.astype(BF)
         for k in RINGS:
             push(
                 R.ag.at[i, rows_t],
                 R.ag.at[i, rows_t],
-                R.m_ags.at[i, k - 1],
-                R.m_agr.at[i, k - 1],
+                R.m_ags.at[m, k - 1],
+                R.m_agr.at[m, k - 1],
                 dev_x(k),
-                "x",
+                ("ag", m),
             )
 
     def ag_wait(i):
-        flush("x", 9)
         for k in (1, 3, 2):
-            landed(R.ag.at[i, rows_t], R.m_agr.at[i, k - 1], dev_x(k))
+            landed(R.ag.at[i, rows_t], R.m_agr.at[int(i in SECOND_AG), k - 1], dev_x(k))
 
     def gain_row(s, i):
         return R.nv[s, 0, i : i + 1, :]
@@ -372,184 +377,209 @@
         ref[piece, 0, r0 : r0 + rows, :] = value[:, 0:384].astype(BF)
         ref[piece, 1, r0 : r0 + rows, :] = value[:, 384:768].astype(BF)
 
-    def ffn_grads(s, gathered, ref):
-        put(ref, 0, 0, tn(R.ag[gathered], R.du[s]))
-        put(ref, 1, 0, tn(R.act[s], R.ag[A_DR2 + s]))
+    def out_grad(s):
+        return tn(R.act[s], R.ag[A_DR2 + s])
+
+    def in_grad(s, gathered):
+        return tn(R.ag[gathered], R.du[s])
+
+    def put_halves(ref, value):
+        put(ref, 0, 0, value[0:384])
+        put(ref, 1, 0, value[384:768])
 
     def blk(name):
-        return tuple(getattr(R, pre + name) for pre in ("g_", "x_", "a_", "b_", "s_", "r_"))
-
-    goal = {
-        "ffd": R.gof.at[1],
-        "ffe": R.gof.at[0],
-        "sad": R.gos.at[1],
-        "sae": R.gos.at[0],
-        "crx": R.goc,
-    }
-
-    def g0(name):
-        g, x, a, b, s, r = blk(name)
-        push(g.at[o], x, s.at[0], r.at[0], dev_c, name)
-
-    def p_rows(name, at):
-        quarter = BLOCKS[name] // 4
-        return pl.ds(pl.multiple_of(at * quarter, quarter), quarter)
-
-    def q_rows(name, at_p, at_q):
-        quarter, eighth = BLOCKS[name] // 4, BLOCKS[name] // 8
-        return pl.ds(pl.multiple_of(at_p * quarter + (at_q // 2) * eighth, eighth), eighth)
-
-    def half_rows(name, at, half):
-        quarter, eighth = BLOCKS[name] // 4, BLOCKS[name] // 8
-        return pl.ds(pl.multiple_of(at * quarter + half * eighth, eighth), eighth)
-
-    def p_at(k):
-        return lax.rem(p + k, 4)
-
-    def g1(name):
-        g, x, a, b, s, r = blk(name)
-        landed(x, r.at[0], dev_c)
-        g[c] = (g[c].astype(F32) + x[...].astype(F32)).astype(BF)
-        h = getattr(R, "h_" + name)
-        for i, k in ((0, 1), (1, 3)):
-            part = g.at[c, :, half_rows(name, p_at(2), i)]
-            push(part, h.at[i], s.at[1 + i], r.at[1 + i], dev_p(k), name)
-
-    def g1b(name):
-        g, x, a, b, s, r = blk(name)
-        h = getattr(R, "h_" + name)
-        for i, k in ((0, 1), (1, 3)):
-            landed(h.at[i], r.at[1 + i], dev_p(k))
-            part = half_rows(name, p_at(k), i)
-            g[c, :, part, :] = (g[c, :, part, :].astype(F32) + h[i].astype(F32)).astype(BF)
-            push(
-                g.at[c, :, p_rows(name, p_at(k))], a.at[i], s.at[3 + i], r.at[3 + i], dev_p(k), name
-            )
-
-    def g2(name):
-        g, x, a, b, s, r = blk(name)
-        mine = p_rows(name, p)
-        total = g[c, :, mine, :].astype(F32)
-        for i in (0, 1):
-            landed(a.at[i], r.at[3 + i], dev_p(1))
-            total += a[i].astype(F32)
-        g[c, :, mine, :] = total.astype(BF)
-        for k in RINGS:
-            to = lax.rem(q + k, 4)
-            push(
-                g.at[c, lax.rem(to, 2), q_rows(name, p, to)],
-                b.at[k - 1],
-                s.at[4 + k],
-                r.at[4 + k],
-                dev_q(k),
-                name,
-            )
-
-    def g3(name):
-        g, x, a, b, s, r = blk(name)
-        flush(name, 3)
-        for k in (1, 3, 2):
-            landed(b.at[k - 1], r.at[4 + k], dev_q(k))
-        rows, half = q_rows(name, p, q), lax.rem(q, 2)
-        total = g[c, half, rows, :].astype(F32)
-        for k in range(3):
-            total += b[k].astype(F32)
-        fin = goal[name]
-        fin[half, rows, :] = total.astype(BF)
-        for k in RINGS:
-            push(fin.at[half, rows], fin.at[half, rows], s.at[7 + k], r.at[7 + k], dev_q(k), name)
-
-    final = {"ffd": (1, of_o), "ffe": (0, of_o), "sad": (1, os_o), "sae": (0, os_o)}
-
-    def hop(name, rows, j):
-        owner, dst = final[name]
-        fin, f = goal[name], getattr(R, "f_" + name)
-
-        @pl.when(c == owner)
+        bufs = tuple(getattr(R, pre + name) for pre in ("g_", "x_", "h_", "a_", "b_"))
+        return bufs + (getattr(R, "s_" + GROUP[name]), getattr(R, "r_" + GROUP[name]))
+
+    place = ((y, z), (z, y))
+    devs = ((dev_y, dev_z), (dev_z, dev_y))
+
+    def quarter(name, where):
+        rows = BLOCKS[name] // 4
+        return pl.ds(pl.multiple_of(where * rows, rows), rows)
+
+    def eighth(name, where, half):
+        rows = BLOCKS[name] // 8
+        return pl.ds(pl.multiple_of(where * 2 * rows + half * rows, rows), rows)
+
+    def step(where, k):
+        return lax.rem(where + k, 4)
+
+    def work(name):
+        return pl.when(c == WORKER[name])
+
+    def gone(src, sem):
+        pltpu.make_async_remote_copy(
+            src_ref=src, dst_ref=src, send_sem=sem, recv_sem=sem, device_id=dev_c, device_id_type=MESH
+        ).wait_send()
+
+    def ship(src, dst, ss, rs, dev):
+        push(src, dst, ss, rs, dev, wait=False)
+
+    def result(name, i, rows, half=slice(None)):
+        if name == "crx":
+            return oc_o.at[i, half, rows]
+        if name == "ffd":
+            return of_o.at[i, half, rows]
+        if name in ("ffi", "ffo"):
+            rows = pl.ds(pl.multiple_of(i * 384 + rows.start, 48), rows.size)
+            return of_o.at[int(name == "ffo"), half, rows]
+        return os_o.at[i, half, rows]
+
+    def spot(name, i, rows, half=slice(None)):
+        return R.x_sae.at[i, half, rows] if name == "sae" else result(name, i, rows, half)
+
+    def g0(name, pieces=(0, 1)):
+        g, x = blk(name)[:2]
+
+        @pl.when(c != WORKER[name])
         def _():
-            pltpu.make_async_copy(fin.at[:, rows], dst.at[c, :, rows], f.at[c, j]).start()
-
-        @pl.when(c != owner)
+            for i in pieces:
+                sem = R.m_g0.at[tuple(BLOCKS).index(name), i]
+                ship(g.at[i], x.at[i], sem, blk(name)[6].at[i, 0], dev_c)
+
+    def g1(name, pieces=(0, 1)):
+        g, x, h, a, b, s, r = blk(name)
+
+        @work(name)
         def _():
-            s = getattr(R, "s_" + name)
-            push(fin.at[:, rows], dst.at[c, :, rows], s.at[15 + j], f.at[c, j], dev_c, wait=False)
-
-    def hop_gone(name, rows, j):
-        owner, dst = final[name]
-        fin, f = goal[name], getattr(R, "f_" + name)
-
-        @pl.when(c != owner)
+            for i in pieces:
+                landed(x.at[i], r.at[i, 0], dev_c)
+                g[i] = g[i] + x[i]
+                far = step(place[i][0], 2)
+                for j, k in ((0, 1), (1, 3)):
+                    part = g.at[i, :, eighth(name, far, j)]
+                    ship(part, h.at[i, j], s.at[i, j], r.at[i, 1 + j], devs[i][0](k))
+
+    def g1b(name, pieces=(0, 1)):
+        g, x, h, a, b, s, r = blk(name)
+
+        @work(name)
         def _():
-            s = getattr(R, "s_" + name)
-            pltpu.make_async_remote_copy(
-                src_ref=fin.at[:, rows],
-                dst_ref=dst.at[c, :, rows],
-                send_sem=s.at[15 + j],
-                recv_sem=f.at[c, j],
-                device_id=dev_c,
-                device_id_type=MESH,
-            ).wait_send()
-
-    def g4(name):
-        g, x, a, b, s, r = blk(name)
-        fin = goal[name]
-        for k in (1, 3, 2):
-            landed(fin.at[lax.rem(q, 2), q_rows(name, p, q)], r.at[7 + k], dev_q(k))
-        mine = p_rows(name, p)
-        for i, k in ((0, 1), (1, 3)):
-            push(fin.at[:, mine], fin.at[:, mine], s.at[11 + i], r.at[11 + i], dev_p(k), name)
-        if name in final:
-            hop(name, mine, 0)
-
-    def g4b(name):
-        g, x, a, b, s, r = blk(name)
-        fin = goal[name]
-        for i, k in ((0, 1), (1, 3)):
-            landed(fin.at[:, p_rows(name, p)], r.at[11 + i], dev_p(k))
-            part = half_rows(name, p_at(4 - k), i)
-            if name in final:
-                owner, dst = final[name]
-                f = getattr(R, "f_" + name)
-                to = (owner, t, dp_p(k))
-                push(
-                    fin.at[:, part], dst.at[c, :, part], s.at[13 + i], f.at[c, 3 + i], to, name
-                )
-            else:
-                push(
-                    fin.at[:, part], fin.at[:, part], s.at[13 + i], r.at[13 + i], dev_p(k), name
-                )
-        if name in final:
-            for i, k in ((0, 1), (1, 3)):
-                hop(name, p_rows(name, p_at(4 - k)), 1 + i)
+            for j, k in ((0, 1), (1, 3)):
+                for i in pieces:
+                    near = step(place[i][0], k)
+                    landed(h.at[i, j], r.at[i, 1 + j], dev_c)
+                    part = eighth(name, near, j)
+                    g[i, :, part, :] = g[i, :, part, :] + h[i, j]
+                    part = g.at[i, :, quarter(name, near)]
+                    gone(h.at[i, j], s.at[i, j])
+                    ship(part, a.at[i, j], s.at[i, j], r.at[i, 3 + j], devs[i][0](k))
+
+    def sub(name, i, where):
+        return eighth(name, place[i][0], where // 2), lax.rem(where, 2)
+
+    def g2(name, pieces=(0, 1)):
+        g, x, h, a, b, s, r = blk(name)
+
+        @work(name)
+        def _():
+            for i in pieces:
+                mine = quarter(name, place[i][0])
+                total = g[i, :, mine, :].astype(F32)
+                for j in (0, 1):
+                    landed(a.at[i, j], r.at[i, 3 + j], dev_c)
+                    total += a[i, j].astype(F32)
+                    gone(a.at[i, j], s.at[i, j])
+                g[i, :, mine, :] = total.astype(BF)
+                for k in RINGS:
+                    rows, half = sub(name, i, step(place[i][1], k))
+                    part = g.at[i, half, rows]
+                    ship(part, b.at[i, k - 1], s.at[i, k - 1], r.at[i, 4 + k], devs[i][1](k))
+
+    def g3(name, pieces=(0, 1)):
+        g, x, h, a, b, s, r = blk(name)
+
+        @work(name)
+        def _():
+            for i in pieces:
+                for k in (1, 3, 2):
+                    landed(b.at[i, k - 1], r.at[i, 4 + k], dev_c)
+                rows, half = sub(name, i, place[i][1])
+                total = g[i, half, rows, :].astype(F32)
+                for k in range(3):
+                    total += b[i, k].astype(F32)
+                part = spot(name, i, rows, half)
+                part[...] = total.astype(BF)
+                for k in RINGS:
+                    gone(b.at[i, k - 1], s.at[i, k - 1])
+                    ship(part, part, s.at[i, k - 1], r.at[i, (3, 4, 8)[k - 1]], devs[i][1](k))
+
+    def g4(name, pieces=(0, 1)):
+        g, x, h, a, b, s, r = blk(name)
+
+        @work(name)
+        def _():
+            for i in pieces:
+                mine = quarter(name, place[i][0])
+                part = spot(name, i, mine)
+                for k in (1, 3, 2):
+                    landed(b.at[i, k - 1], r.at[i, (3, 4, 8)[k - 1]], dev_c)
+                    gone(b.at[i, k - 1], s.at[i, k - 1])
+                for j, k in ((0, 1), (1, 3)):
+                    ship(part, part, s.at[i, j], r.at[i, 2 - j], devs[i][0](k))
+                if name == "sae":
+                    ship(part, result(name, i, mine), s.at[i, 3], R.f_sae.at[i, 0], dev_c)
+
+    def g4b(name, pieces=(0, 1)):
+        g, x, h, a, b, s, r = blk(name)
+
+        @work(name)
+        def _():
+            for j, k in ((0, 1), (1, 3)):
+                for i in pieces:
+                    behind = step(place[i][0], 4 - k)
+                    landed(a.at[i, j], r.at[i, 2 - j], dev_c)
+                    gone(a.at[i, j], s.at[i, j])
+                    rows = eighth(name, behind, j)
+                    part, to = spot(name, i, rows), devs[i][0](k)
+                    if name == "sae":
+                        to = (OWNER[name],) + to[1:]
+                        ship(part, result(name, i, rows), s.at[i, j], R.f_sae.at[i, 3 + j], to)
+                    else:
+                        ship(part, part, s.at[i, j], r.at[i, 9 + j], to)
+            if name == "sae":
+                for j, k in ((0, 1), (1, 3)):
+                    for i in pieces:
+                        rows = quarter(name, step(place[i][0], 4 - k))
+                        part = x.at[i, :, rows]
+                        ship(part, result(name, i, rows), s.at[i, 4 + j], R.f_sae.at[i, 1 + j], dev_c)
 
     def g5(name):
-        g, x, a, b, s, r = blk(name)
-        flush(name, 2)
-        fin = goal[name]
-        if name not in final:
-            f = getattr(R, "f_" + name)
-            for i, k in ((0, 1), (1, 3)):
-                landed(fin.at[:, half_rows(name, p, i)], r.at[13 + i], dev_p(k))
-            push(fin, oc_o.at[c], s.at[15], f.at[c, 0], dev_c, name)
-            pltpu.make_async_copy(fin, oc_o.at[c], f.at[c, 1]).start()
+        g, x, h, a, b, s, r = blk(name)
+
+        @work(name)
+        def _():
+            for i in (0, 1):
+                for j in (0, 1):
+                    landed(h.at[i, j], r.at[i, 9 + j], dev_c)
+            if name == "crx":
+                ship(oc_o, oc_o, s.at[0, 2], R.m_hr.at[2], dev_c)
 
     def g6(name):
-        f = getattr(R, "f_" + name)
-        if name not in final:
-            landed(oc_o.at[o], f.at[o, 0], dev_c)
-            landed(oc_o.at[c], f.at[c, 1], dev_c)
-            return
-        owner, dst = final[name]
-
-        @pl.when(c == owner)
+        g, x, h, a, b, s, r = blk(name)
+
+        @pl.when(c != WORKER[name])
         def _():
-            for piece in (0, 1):
-                for j in range(5):
-                    rows = p_rows(name, p) if j < 3 else half_rows(name, p, 0)
-                    landed(dst.at[piece, :, rows], f.at[piece, j], dev_c)
-
-        for j, k in ((0, 0), (1, 3), (2, 1)):
-            hop_gone(name, p_rows(name, p_at(k)), j)
+            for i in (0, 1):
+                gone(g.at[i], R.m_g0.at[tuple(BLOCKS).index(name), i])
+            if name == "crx":
+                landed(oc_o, R.m_hr.at[2], dev_c)
+            if name == "sae":
+                for i in (0, 1):
+                    for j in range(5):
+                        landed(a.at[i, 0] if j < 3 else h.at[i, 0], R.f_sae.at[i, j], dev_c)
+
+        @work(name)
+        def _():
+            for i in (0, 1):
+                for j in (0, 1):
+                    gone(h.at[i, j], s.at[i, j])
+                if name == "sae":
+                    for j in (0, 1, 2):
+                        gone(a.at[i, 0], s.at[i, 3 + j])
+            if name == "crx":
+                gone(oc_o, s.at[0, 2])
 
     def vec_put(row, dg, db, step=2):
         R.vec[row : row + 1, :] = dg
@@ -558,7 +588,7 @@
     def vec_send(buf, at, value, base, dev, count):
         buf[at] = value.astype(BF)
         for k in range(1, count):
-            push(buf.at[at], buf.at[at], R.m_vs.at[base + k - 1], R.m_vr.at[base + k - 1], dev(k))
+            push(buf.at[at], buf.at[at], R.m_dps.at[base + k - 1], R.m_vr.at[base + k - 1], dev(k))
 
     def vec_sum(buf, at, base, dev, count):
         for k in range(1, count):
@@ -585,7 +615,7 @@
     at = b_at * TOK + lax.rem(rows, TOK)
     R.pos[0] = jnp.broadcast_to(at, (8, KEYS))
     for k in RINGS:
-        push(R.pos.at[0], R.pos.at[k], R.m_kvs.at[5 + k], R.m_kvr.at[5 + k], dev_q(k))
+        push(R.pos.at[0], R.pos.at[k], R.m_dps.at[5 + k], R.m_kvr.at[5 + k], dev_q(k))
     self_forward(0)
     self_forward(1)
     self_finish(0)
@@ -619,7 +649,7 @@
     R.kvt[p] = nt(R.wcr[384:768, :], R.ag[A_BO]).astype(BF)
 
     for k in RINGS:
-        push(R.kvt.at[p], R.kvt.at[p], R.m_kvs.at[k - 1], R.m_kvr.at[k - 1], dev_p(k))
+        push(R.kvt.at[p], R.kvt.at[p], R.m_dps.at[k - 1], R.m_kvr.at[k - 1], dev_p(k))
     for k in (1, 3, 2):
         landed(R.kvt.at[p], R.m_kvr.at[k - 1], dev_p(k))
     column = jnp.concatenate([R.kvt[j] for j in range(4)], axis=1)
@@ -627,7 +657,7 @@
         R.kvs[k] = nn(column, R.hot[k]).astype(BF)
         if k:
             push(
-                R.kvs.at[k], R.kvr.at[3 - k], R.m_kvs.at[6 - k], R.m_kvr.at[6 - k], dev_q(4 - k)
+                R.kvs.at[k], R.kvr.at[3 - k], R.m_dps.at[6 - k], R.m_kvr.at[6 - k], dev_q(4 - k)
             )
     for k in (1, 3, 2):
         landed(R.kvr.at[k - 1], R.m_kvr.at[2 + k], dev_q(k))
@@ -662,7 +692,8 @@
     ffn_backward(1)
     ag_start(A_BO + 1, out)
     flush("")
-    ffn_grads(1, A_Y2, R.g_ffd)
+    put(R.g_ffd, 0, 0, in_grad(1, A_Y2))
+    put(R.g_ffd, 1, 0, out_grad(1))
     g0("ffd")
     dy = R.dres[1] + rs_sum(R_DFF + 1)
     dr, dg, db = ln_backward(R.nc[...], get_norm(4), cross_gain, dy)
@@ -686,7 +717,7 @@
         R.dqct[lo : lo + 64, :] = dqts[h].astype(BF)
 
     for k in RINGS:
-        push(R.dkvct, R.dkr.at[k - 1], R.m_dks.at[k - 1], R.m_dkr.at[k - 1], dev_q(k))
+        push(R.dkvct, R.dkr.at[k - 1], R.m_dps.at[k - 1], R.m_dkr.at[k - 1], dev_q(k))
     rs_start(R_DQ, tn(R.dqct[...], R.wcr[0:192, :]))
     put(R.g_crx, 0, 0, nn(R.dqct[...], R.ag[A_Y1 + 1]))
     put(R.g_crx, 0, 192, nn(R.oct[...], R.ag[A_DRC]))
@@ -732,7 +763,7 @@
             part += nt(R.dkr[j - 1], hot)
         R.dks[to] = part.astype(BF)
         if k:
-            push(R.dks.at[to], R.dk2.at[k - 1], R.m_dks.at[2 + k], R.m_dkr.at[2 + k], dev_p(k))
+            push(R.dks.at[to], R.dk2.at[k - 1], R.m_dps.at[2 + k], R.m_dkr.at[2 + k], dev_p(k))
     g2("ffd")
     self_backward(1)
     input_part(1)
@@ -747,84 +778,92 @@
     rs_start(R_DST, tn(R.dkv[...], R.wcr[384:768, :]))
     put(R.g_crx, 1, 0, nn(R.dkv[...], R.ag[A_BO]))
     g0("crx")
+    g1("sad")
     g3("ffd")
-    g1("sad")
+    g1("crx")
+    g1b("sad")
     dy = rs_sum(R_DST)
     dr, dg, db = ln_backward(R.n2[0], get_norm(2), gain_row(0, 1), dy)
     ag_start(A_DR2, dr)
     R.dres[0] = dr
     vec_put(1, dg, db)
-    g1("crx")
+    flush("")
+    ag_wait(A_BO + 1)
+    push(R.ag.at[A_BO + o], bo_o.at[c], R.m_hs.at[0], R.m_hr.at[0], dev_c)
+    outs = [pltpu.make_async_copy(R.ag.at[A_BO + c], bo_o.at[c], R.m_o.at[0])]
+    outs[0].start()
     g4("ffd")
-    g1b("sad")
-    flush("")
-    ffn_backward(0)
-    ffn_grads(0, A_Y1, R.g_ffe)
-    g0("ffe")
     g1b("crx")
     g2("sad")
+    ffn_backward(0)
+    put_halves(R.g_ffo, out_grad(0))
+    g0("ffo")
+    put_halves(R.g_ffi, in_grad(0, A_Y1))
+    g0("ffi")
     g4b("ffd")
+    g2("crx")
+    g1("ffo")
     dy = R.dres[0] + rs_sum(R_DFF)
     dr, dg, db = ln_backward(R.n1[0], get_norm(0), gain_row(0, 0), dy)
     ag_start(A_DR1, dr)
     R.dres[0] = dr
     vec_put(0, dg, db)
+    g1("ffi")
     vec_send(R.vx, t, R.vec[...], 0, dev_x, 4)
-    g1("ffe")
+    g3("sad")
     ag_start(A_IG + 1, R.dres[1] + rs_sum(R_DSA + 1))
-    g2("crx")
+    g1b("ffo")
+    g3("crx")
     self_backward(0)
-    g1b("ffe")
+    g1b("ffi")
     self_grads(0, R.g_sae)
     g0("sae")
     input_part(0)
-    g3("sad")
-    g3("crx")
+    g4("sad")
+    g2("ffo")
+    g4("crx")
     total = vec_sum(R.vx, t, 0, dev_x, 4)
     vec_send(R.vc, c, total, 3, dev_c1, 2)
     g1("sae")
+    g2("ffi")
     total = vec_sum(R.vc, c, 3, dev_c1, 2)
     vec_send(R.vy, y, total, 4, dev_y, 4)
+    g4b("sad")
+    g1b("sae")
     ag_start(A_IG, R.dres[0] + rs_sum(R_DSA))
-    g2("ffe")
-    g1b("sae")
-    g4("sad")
-    g4("crx")
+    g3("ffo")
+    g4b("crx")
+    g3("ffi")
+    g2("sae")
     total = vec_sum(R.vy, y, 4, dev_y, 4)
     vec_send(R.vz, z, total, 7, dev_z, 4)
-    ag_wait(A_BO + 1)
-    push(R.ag.at[A_BO + o], bo_o.at[c], R.m_hs.at[0], R.m_hr.at[0], dev_c)
-    outs = [pltpu.make_async_copy(R.ag.at[A_BO + c], bo_o.at[c], R.m_o.at[0])]
-    outs[0].start()
-    g3("ffe")
-    g2("sae")
+    g4("ffo")
+    g4("ffi")
     ag_wait(A_IG)
     ag_wait(A_IG + 1)
     push(R.ag.at[A_IG + o], ig_o.at[c], R.m_hs.at[1], R.m_hr.at[1], dev_c)
     outs.append(pltpu.make_async_copy(R.ag.at[A_IG + c], ig_o.at[c], R.m_o.at[1]))
     outs[1].start()
-    g4b("sad")
-    g4b("crx")
+    g3("sae")
+    g5("crx")
     total = vec_sum(R.vz, z, 7, dev_z, 4)
     on_o[...] = jnp.where(c == 0, total[0:4, :], total[4:8, :])
     oe_o[...] = total[8:10, :]
-    g4("ffe")
-    g3("sae")
-    flush("x")
     flush("")
-    g5("crx")
+    g4b("ffo")
     g4("sae")
-    g4b("ffe")
+    g4b("ffi")
     g4b("sae")
     landed(bo_o.at[c], R.m_hr.at[0], dev_c)
     landed(ig_o.at[c], R.m_hr.at[1], dev_c)
     for cp in outs:
         cp.wait()
-    g6("ffd")
-    g6("sad")
-    g6("crx")
-    g6("ffe")
-    g6("sae")
+    g5("ffd")
+    g5("sad")
+    g5("ffo")
+    g5("ffi")
+    for name in ("ffd", "sad", "crx", "ffo", "ffi", "sae"):
+        g6(name)
     for kind in list(sends):
         flush(kind)
 

time: 154 us -> 147 us (0.955)
  Pallas kernels: 154 us -> 146 us
    pallas_call x1, Pallas kernels: 149 us -> 141 us  [body(): pl.pallas_call(run, out_shape=outs, in_specs=[hbm, hbm, vm, vm, hbm, hbm,...]
where the time goes in v5:
time: 147 us; the launch traced here: 146 us
  Pallas kernels  146 us (99%)
    pallas_call x1, Pallas kernels, body(): pl.pallas_call(run, out_shape=outs, in_specs=[hbm, hbm, vm, vm, hbm, hbm,...  141 us
    pallas_call x1, Pallas kernels, body(): pl.pallas_call(widen, out_shape=wide_outs, in_specs=[vm] * 7, out_specs=[...  4.77 us

profile of v5, /device:TPU:0, one launch (start us, length us, event | category | flops | bytes accessed | tf_op | source)
XLA Modules:
  0.0 146.5 jit_solution(12683131557084869320)
XLA Ops:
  0.7 140.9 %layers.1 = (bf16[2,128,768]{2,1,0:T(8,128)(2,1)S(1)}, bf16[2,128,768]{2,1,0:T(8,128)(2,1)S(1)}, bf16[2,2,768,384]{3,2,1,0:T(8,128)(2,1)S(1)}, bf16[2,2,384,384]...) custom-call(bf16[2,128,768]{2,1,0:T(8,128)(2,1)} %bitcast.35, ...), custom_call_target="tpu_custom_call" | custom-call | tf_op jit(solution)/shard_map/layers/pallas_call | solution.py:955
  141.6 4.8 %widen.1 = (bf16[2,128,768]{2,1,0:T(8,128)(2,1)}, f32[2,128,768]{2,1,0:T(8,128)}, f32[576,768]{1,0:T(8,128)}, f32[192,768]{1,0:T(8,128)}, f32[768,768]{1,0:T(8,1...) custom-call(bf16[2,128,768]{2,1,0:T(8,128)(2,1)S(1)} %get-tuple-elem, ...), custom_call_target="tpu_custom_call" | custom-call | tf_op jit(solution)/shard_map/widen/pallas_call | solution.py:981

commit v6 on v5

--- a/solution.py
+++ b/solution.py
@@ -30,6 +30,7 @@
 BLOCKS = {"ffd": 768, "ffo": 384, "ffi": 384, "crx": 384, "sad": 384, "sae": 384}
 WORKER = {"ffd": 1, "crx": 1, "sad": 1, "ffo": 0, "ffi": 0, "sae": 1}
 OWNER = {"ffd": 1, "sad": 1, "ffo": 0, "ffi": 0, "sae": 0}
+WHOLE = ("sae",)
 GROUP = {"ffd": "a", "crx": "b", "ffo": "b", "sad": "c", "ffi": "c", "sae": "d"}
 SECOND_RS = (R_SA + 1, R_DSA + 1)
 SECOND_AG = (A_BO + 1, A_IG + 1, A_Y1 + 1)
@@ -79,6 +80,7 @@
         ("pos", VMEM((4, 8, KEYS), jnp.int32)),
         ("hot", VMEM((4, 4 * TOK, KEYS), BF)),
         ("kvt", VMEM((4, 2 * QW, TOK), BF)),
+        ("kvf", VMEM((4, 2 * QW, KEYS), F32)),
         ("kvs", VMEM((4, 2 * QW, KEYS), BF)),
         ("kvr", VMEM((3, 2 * QW, KEYS), BF)),
         ("dkr", VMEM((3, 2 * QW, KEYS), BF)),
@@ -108,7 +110,7 @@
         ("m_hs", DMA((2,))),
         ("m_hr", DMA((3,))),
         ("m_g0", DMA((len(BLOCKS), 2))),
-        ("f_sae", DMA((2, 5))),
+        ("f_sae", DMA((2, 4))),
         ("m_o", DMA((2,))),
     ]
     for name, rows in BLOCKS.items():
@@ -116,11 +118,14 @@
             ("g_" + name, VMEM((2, 2, rows, 384), BF)),
             ("x_" + name, VMEM((2, 2, rows, 384), BF)),
             ("h_" + name, VMEM((2, 2, 2, rows // 8, 384), BF)),
-            ("a_" + name, VMEM((2, 2, 2, rows // 4, 384), BF)),
-            ("b_" + name, VMEM((2, 3, rows // 8, 384), BF)),
+            ("a_" + name, VMEM((2, 3 if name == "sae" else 2, 2, rows // 4, 384), BF)),
+            (
+                "b_" + name,
+                VMEM((2, 4, 2, rows // 4, 384) if name in WHOLE else (2, 3, rows // 8, 384), BF),
+            ),
         ]
     for group in sorted(set(GROUP.values())):
-        out.append(("s_" + group, DMA((2, 6 if group == GROUP["sae"] else 3))))
+        out.append(("s_" + group, DMA((2, 4 if group == GROUP["sae"] else 3))))
         out.append(("r_" + group, DMA((2, 9 if group == GROUP["sae"] else 11))))
     return out
 
@@ -220,7 +225,7 @@
     for k in (1, 2, 3):
         for dev in (dev_x(k), dev_y(k), dev_z(k)):
             peers.append(dev)
-    for k in (1, 3):
+    for k in (1, 2, 3):
         peers.append((o,) + dev_y(k)[1:])
         peers.append((o,) + dev_z(k)[1:])
     for dev in peers:
@@ -446,6 +451,11 @@
             for i in pieces:
                 landed(x.at[i], r.at[i, 0], dev_c)
                 g[i] = g[i] + x[i]
+                if name == "sae":
+                    for k in RINGS:
+                        part = g.at[i, :, quarter(name, step(place[i][0], k))]
+                        ship(part, a.at[i, k - 1], s.at[i, k - 1], r.at[i, k], devs[i][0](k))
+                    continue
                 far = step(place[i][0], 2)
                 for j, k in ((0, 1), (1, 3)):
                     part = g.at[i, :, eighth(name, far, j)]
@@ -477,11 +487,17 @@
             for i in pieces:
                 mine = quarter(name, place[i][0])
                 total = g[i, :, mine, :].astype(F32)
-                for j in (0, 1):
-                    landed(a.at[i, j], r.at[i, 3 + j], dev_c)
+                for j in range(a.shape[1]):
+                    landed(a.at[i, j], r.at[i, j + (1 if name == "sae" else 3)], dev_c)
                     total += a[i, j].astype(F32)
                     gone(a.at[i, j], s.at[i, j])
                 g[i, :, mine, :] = total.astype(BF)
+                if name in WHOLE:
+                    part = g.at[i, :, mine]
+                    for k in RINGS:
+                        dst = b.at[i, place[i][1]]
+                        ship(part, dst, s.at[i, k - 1], r.at[i, 4 + k], devs[i][1](k))
+                    continue
                 for k in RINGS:
                     rows, half = sub(name, i, step(place[i][1], k))
                     part = g.at[i, half, rows]
@@ -493,6 +509,17 @@
         @work(name)
         def _():
             for i in pieces:
+                if name in WHOLE:
+                    mine = quarter(name, place[i][0])
+                    b[i, place[i][1]] = g[i, :, mine, :]
+                    for k in (1, 3, 2):
+                        landed(a.at[i, 0], r.at[i, 4 + k], dev_c)
+                        gone(a.at[i, 0], s.at[i, k - 1])
+                    total = b[i, 0].astype(F32)
+                    for j in (1, 2, 3):
+                        total += b[i, j].astype(F32)
+                    spot(name, i, mine)[...] = total.astype(BF)
+                    continue
                 for k in (1, 3, 2):
                     landed(b.at[i, k - 1], r.at[i, 4 + k], dev_c)
                 rows, half = sub(name, i, place[i][1])
@@ -513,13 +540,18 @@
             for i in pieces:
                 mine = quarter(name, place[i][0])
                 part = spot(name, i, mine)
-                for k in (1, 3, 2):
+                for k in () if name in WHOLE else (1, 3, 2):
                     landed(b.at[i, k - 1], r.at[i, (3, 4, 8)[k - 1]], dev_c)
                     gone(b.at[i, k - 1], s.at[i, k - 1])
+                if name == "sae":
+                    dst = result(name, i, mine)
+                    for k in RINGS:
+                        to = (OWNER[name],) + devs[i][0](k)[1:]
+                        ship(part, dst, s.at[i, k - 1], R.f_sae.at[i, k], to)
+                    ship(part, dst, s.at[i, 3], R.f_sae.at[i, 0], dev_c)
+                    continue
                 for j, k in ((0, 1), (1, 3)):
                     ship(part, part, s.at[i, j], r.at[i, 2 - j], devs[i][0](k))
-                if name == "sae":
-                    ship(part, result(name, i, mine), s.at[i, 3], R.f_sae.at[i, 0], dev_c)
 
     def g4b(name, pieces=(0, 1)):
         g, x, h, a, b, s, r = blk(name)
@@ -532,18 +564,8 @@
                     landed(a.at[i, j], r.at[i, 2 - j], dev_c)
                     gone(a.at[i, j], s.at[i, j])
                     rows = eighth(name, behind, j)
-                    part, to = spot(name, i, rows), devs[i][0](k)
-                    if name == "sae":
-                        to = (OWNER[name],) + to[1:]
-                        ship(part, result(name, i, rows), s.at[i, j], R.f_sae.at[i, 3 + j], to)
-                    else:
-                        ship(part, part, s.at[i, j], r.at[i, 9 + j], to)
-            if name == "sae":
-                for j, k in ((0, 1), (1, 3)):
-                    for i in pieces:
-                        rows = quarter(name, step(place[i][0], 4 - k))
-                        part = x.at[i, :, rows]
-                        ship(part, result(name, i, rows), s.at[i, 4 + j], R.f_sae.at[i, 1 + j], dev_c)
+                    part = spot(name, i, rows)
+                    ship(part, part, s.at[i, j], r.at[i, 9 + j], devs[i][0](k))
 
     def g5(name):
         g, x, h, a, b, s, r = blk(name)
@@ -567,17 +589,18 @@
                 landed(oc_o, R.m_hr.at[2], dev_c)
             if name == "sae":
                 for i in (0, 1):
-                    for j in range(5):
-                        landed(a.at[i, 0] if j < 3 else h.at[i, 0], R.f_sae.at[i, j], dev_c)
+                    for j in range(4):
+                        landed(a.at[i, 0], R.f_sae.at[i, j], dev_c)
 
         @work(name)
         def _():
             for i in (0, 1):
+                if name == "sae":
+                    for j in range(4):
+                        gone(a.at[i, 0], s.at[i, j])
+                    continue
                 for j in (0, 1):
                     gone(h.at[i, j], s.at[i, j])
-                if name == "sae":
-                    for j in (0, 1, 2):
-                        gone(a.at[i, 0], s.at[i, 3 + j])
             if name == "crx":
                 gone(oc_o, s.at[0, 2])
 
@@ -617,9 +640,7 @@
     for k in RINGS:
         push(R.pos.at[0], R.pos.at[k], R.m_dps.at[5 + k], R.m_kvr.at[5 + k], dev_q(k))
     self_forward(0)
-    self_forward(1)
     self_finish(0)
-    self_finish(1)
     ag_wait(A_Y1)
     need(0, 5)
     need(0, 6)
@@ -627,8 +648,6 @@
 
     for cp in singles:
         cp.wait()
-    ag_wait(A_Y1 + 1)
-    R.qct[...] = nt(R.wcr[0:192, :], R.ag[A_Y1 + 1]).astype(BF)
     for k in (1, 3, 2):
         landed(R.pos.at[k], R.m_kvr.at[5 + k], dev_q(k))
 
@@ -650,15 +669,27 @@
 
     for k in RINGS:
         push(R.kvt.at[p], R.kvt.at[p], R.m_dps.at[k - 1], R.m_kvr.at[k - 1], dev_p(k))
-    for k in (1, 3, 2):
-        landed(R.kvt.at[p], R.m_kvr.at[k - 1], dev_p(k))
-    column = jnp.concatenate([R.kvt[j] for j in range(4)], axis=1)
+
+    def picked(k, j):
+        return nn(R.kvt[j], R.hot[k, pl.ds(pl.multiple_of(j * TOK, TOK), TOK), :])
+
+    self_forward(1)
+    for k in range(4):
+        R.kvf[k] = picked(k, p)
+    for j in (1, 3):
+        landed(R.kvt.at[p], R.m_kvr.at[j - 1], dev_p(j))
+        for k in range(4):
+            R.kvf[k] += picked(k, lax.rem(p + 4 - j, 4))
+    landed(R.kvt.at[p], R.m_kvr.at[1], dev_p(2))
     for k in RINGS + (0,):
-        R.kvs[k] = nn(column, R.hot[k]).astype(BF)
+        R.kvs[k] = (R.kvf[k] + picked(k, lax.rem(p + 2, 4))).astype(BF)
         if k:
             push(
                 R.kvs.at[k], R.kvr.at[3 - k], R.m_dps.at[6 - k], R.m_kvr.at[6 - k], dev_q(4 - k)
             )
+    self_finish(1)
+    ag_wait(A_Y1 + 1)
+    R.qct[...] = nt(R.wcr[0:192, :], R.ag[A_Y1 + 1]).astype(BF)
     for k in (1, 3, 2):
         landed(R.kvr.at[k - 1], R.m_kvr.at[2 + k], dev_q(k))
 
@@ -721,7 +752,7 @@
     rs_start(R_DQ, tn(R.dqct[...], R.wcr[0:192, :]))
     put(R.g_crx, 0, 0, nn(R.dqct[...], R.ag[A_Y1 + 1]))
     put(R.g_crx, 0, 192, nn(R.oct[...], R.ag[A_DRC]))
-    g1b("ffd")
+    g0("crx", (0,))
     dy = R.dres[1] + rs_sum(R_DQ)
     dr, dg, db = ln_backward(R.n1[1], get_norm(1), gain_row(1, 0), dy)
     ag_start(A_DR1 + 1, dr)
@@ -743,32 +774,35 @@
             R.dpk[s, QW + lo : QW + lo + 64, :] = dkts[h].astype(BF)
             R.dpk[s, 2 * QW + lo : 2 * QW + lo + 64, :] = dvts[h].astype(BF)
 
-    def self_grads(s, ref):
+    def self_grads(s, name):
+        ref = getattr(R, "g_" + name)
         put(ref, 0, 0, nn(R.dpk[s, 0:384, :], R.xin[s]))
+        g0(name, (0,))
         put(ref, 1, 0, nn(R.dpk[s, 384:576, :], R.xin[s]))
         put(ref, 1, 192, nn(R.ot[s], R.ag[A_DR1 + s]))
+        g0(name, (1,))
 
     def input_part(s):
         rs_start(R_DSA + s, tn(R.dpk[s], R.wsa[s, 0:576, :]))
 
     for j in range(4):
         R.dkf[j] = nt(R.dkvct[...], R.hot[0, j * TOK : (j + 1) * TOK, :])
-    for k in (1, 3, 2):
+    for k in (1, 3):
         landed(R.dkr.at[k - 1], R.m_dkr.at[k - 1], dev_q(k))
+        for j in range(4):
+            R.dkf[j] += nt(R.dkr[k - 1], R.hot[k, j * TOK : (j + 1) * TOK, :])
+    landed(R.dkr.at[1], R.m_dkr.at[1], dev_q(2))
     for k in RINGS + (0,):
         to = lax.rem(p + k, 4)
-        part = R.dkf[to]
-        for j in (1, 2, 3):
-            hot = R.hot[j, pl.ds(pl.multiple_of(to * TOK, TOK), TOK), :]
-            part += nt(R.dkr[j - 1], hot)
-        R.dks[to] = part.astype(BF)
+        hot = R.hot[2, pl.ds(pl.multiple_of(to * TOK, TOK), TOK), :]
+        R.dks[to] = (R.dkf[to] + nt(R.dkr[1], hot)).astype(BF)
         if k:
             push(R.dks.at[to], R.dk2.at[k - 1], R.m_dps.at[2 + k], R.m_dkr.at[2 + k], dev_p(k))
-    g2("ffd")
+    g1b("ffd")
     self_backward(1)
     input_part(1)
-    self_grads(1, R.g_sad)
-    g0("sad")
+    self_grads(1, "sad")
+    g1("crx", (0,))
     for k in (1, 3, 2):
         landed(R.dk2.at[k - 1], R.m_dkr.at[2 + k], dev_p(k))
     total = R.dks[p].astype(F32)
@@ -777,11 +811,10 @@
     R.dkv[...] = total.astype(BF)
     rs_start(R_DST, tn(R.dkv[...], R.wcr[384:768, :]))
     put(R.g_crx, 1, 0, nn(R.dkv[...], R.ag[A_BO]))
-    g0("crx")
+    g0("crx", (1,))
+    g2("ffd")
     g1("sad")
-    g3("ffd")
-    g1("crx")
-    g1b("sad")
+    g1b("crx", (0,))
     dy = rs_sum(R_DST)
     dr, dg, db = ln_backward(R.n2[0], get_norm(2), gain_row(0, 1), dy)
     ag_start(A_DR2, dr)
@@ -792,16 +825,19 @@
     push(R.ag.at[A_BO + o], bo_o.at[c], R.m_hs.at[0], R.m_hr.at[0], dev_c)
     outs = [pltpu.make_async_copy(R.ag.at[A_BO + c], bo_o.at[c], R.m_o.at[0])]
     outs[0].start()
-    g4("ffd")
-    g1b("crx")
-    g2("sad")
+    g3("ffd")
+    g1("crx", (1,))
+    g1b("sad")
+    g2("crx", (0,))
     ffn_backward(0)
     put_halves(R.g_ffo, out_grad(0))
     g0("ffo")
     put_halves(R.g_ffi, in_grad(0, A_Y1))
     g0("ffi")
-    g4b("ffd")
-    g2("crx")
+    g4("ffd")
+    g1b("crx", (1,))
+    g3("crx", (0,))
+    g2("sad")
     g1("ffo")
     dy = R.dres[0] + rs_sum(R_DFF)
     dr, dg, db = ln_backward(R.n1[0], get_norm(0), gain_row(0, 0), dy)
@@ -809,51 +845,52 @@
     R.dres[0] = dr
     vec_put(0, dg, db)
     g1("ffi")
-    vec_send(R.vx, t, R.vec[...], 0, dev_x, 4)
+    g2("crx", (1,))
+    g4b("ffd")
+    g4("crx", (0,))
     g3("sad")
-    ag_start(A_IG + 1, R.dres[1] + rs_sum(R_DSA + 1))
     g1b("ffo")
-    g3("crx")
     self_backward(0)
     g1b("ffi")
-    self_grads(0, R.g_sae)
-    g0("sae")
+    self_grads(0, "sae")
+    vec_send(R.vx, t, R.vec[...], 0, dev_x, 4)
     input_part(0)
-    g4("sad")
+    ag_start(A_IG + 1, R.dres[1] + rs_sum(R_DSA + 1))
+    g1("sae")
     g2("ffo")
-    g4("crx")
     total = vec_sum(R.vx, t, 0, dev_x, 4)
     vec_send(R.vc, c, total, 3, dev_c1, 2)
-    g1("sae")
+    g3("crx", (1,))
+    g4b("crx", (0,))
+    g4("sad")
     g2("ffi")
     total = vec_sum(R.vc, c, 3, dev_c1, 2)
     vec_send(R.vy, y, total, 4, dev_y, 4)
-    g4b("sad")
-    g1b("sae")
     ag_start(A_IG, R.dres[0] + rs_sum(R_DSA))
     g3("ffo")
-    g4b("crx")
+    g2("sae")
+    g4("crx", (1,))
+    g4b("sad")
     g3("ffi")
-    g2("sae")
     total = vec_sum(R.vy, y, 4, dev_y, 4)
     vec_send(R.vz, z, total, 7, dev_z, 4)
     g4("ffo")
+    g4b("crx", (1,))
+    g3("sae")
+    g4("sae")
+    g5("crx")
     g4("ffi")
     ag_wait(A_IG)
     ag_wait(A_IG + 1)
     push(R.ag.at[A_IG + o], ig_o.at[c], R.m_hs.at[1], R.m_hr.at[1], dev_c)
     outs.append(pltpu.make_async_copy(R.ag.at[A_IG + c], ig_o.at[c], R.m_o.at[1]))
     outs[1].start()
-    g3("sae")
-    g5("crx")
+    g4b("ffo")
     total = vec_sum(R.vz, z, 7, dev_z, 4)
     on_o[...] = jnp.where(c == 0, total[0:4, :], total[4:8, :])
     oe_o[...] = total[8:10, :]
     flush("")
-    g4b("ffo")
-    g4("sae")
     g4b("ffi")
-    g4b("sae")
     landed(bo_o.at[c], R.m_hr.at[0], dev_c)
     landed(ig_o.at[c], R.m_hr.at[1], dev_c)
     for cp in outs:

time: 147 us -> 144 us (0.980)
  Pallas kernels: 146 us -> 143 us
    pallas_call x1, Pallas kernels: 141 us -> 139 us  [body(): pl.pallas_call(run, out_shape=outs, in_specs=[hbm, hbm, vm, vm, hbm, hbm,...]
where the time goes in v6:
time: 144 us
  Pallas kernels  143 us (99%)
    pallas_call x1, Pallas kernels, body(): pl.pallas_call(run, out_shape=outs, in_specs=[hbm, hbm, vm, vm, hbm, hbm,...  139 us
    pallas_call x1, Pallas kernels, body(): pl.pallas_call(widen, out_shape=wide_outs, in_specs=[vm] * 7, out_specs=[...  4.77 us

profile of v6, /device:TPU:0, one launch (start us, length us, event | category | flops | bytes accessed | tf_op | source)
XLA Modules:
  0.0 144.1 jit_solution(17833052357451863639)
XLA Ops:
  0.7 138.5 %layers.1 = (bf16[2,128,768]{2,1,0:T(8,128)(2,1)S(1)}, bf16[2,128,768]{2,1,0:T(8,128)(2,1)S(1)}, bf16[2,2,768,384]{3,2,1,0:T(8,128)(2,1)S(1)}, bf16[2,2,384,384]...) custom-call(bf16[2,128,768]{2,1,0:T(8,128)(2,1)} %bitcast.35, ...), custom_call_target="tpu_custom_call" | custom-call | tf_op jit(solution)/shard_map/layers/pallas_call | solution.py:992
  139.2 4.8 %widen.1 = (bf16[2,128,768]{2,1,0:T(8,128)(2,1)}, f32[2,128,768]{2,1,0:T(8,128)}, f32[576,768]{1,0:T(8,128)}, f32[192,768]{1,0:T(8,128)}, f32[768,768]{1,0:T(8,1...) custom-call(bf16[2,128,768]{2,1,0:T(8,128)(2,1)S(1)} %get-tuple-elem, ...), custom_call_target="tpu_custom_call" | custom-call | tf_op jit(solution)/shard_map/widen/pallas_call | solution.py:1018

commit v7 on v6

--- a/solution.py
+++ b/solution.py
@@ -30,7 +30,7 @@
 BLOCKS = {"ffd": 768, "ffo": 384, "ffi": 384, "crx": 384, "sad": 384, "sae": 384}
 WORKER = {"ffd": 1, "crx": 1, "sad": 1, "ffo": 0, "ffi": 0, "sae": 1}
 OWNER = {"ffd": 1, "sad": 1, "ffo": 0, "ffi": 0, "sae": 0}
-WHOLE = ("sae",)
+WHOLE = ()
 GROUP = {"ffd": "a", "crx": "b", "ffo": "b", "sad": "c", "ffi": "c", "sae": "d"}
 SECOND_RS = (R_SA + 1, R_DSA + 1)
 SECOND_AG = (A_BO + 1, A_IG + 1, A_Y1 + 1)
@@ -246,14 +246,19 @@
         pltpu.make_async_copy(ckv_h, R.wcr.at[pl.ds(384, 384)], R.m_l.at[2]),
         pltpu.make_async_copy(cot_h.at[c], R.cot, R.m_l.at[3]),
     ]
-    pl.semaphore_wait(bar, len(peers))
-    for i in range(5):
-        other(i)
-    for i in (5, 6):
-        own(i)
-        other(i)
-    for cp in singles:
-        cp.start()
+    def enter():
+        pl.semaphore_wait(bar, len(peers))
+        for i in range(3):
+            other(i)
+
+    def rest():
+        for i in (3, 4):
+            other(i)
+        for i in (5, 6):
+            own(i)
+            other(i)
+        for cp in singles:
+            cp.start()
 
     def need(s, i):
         src = x_h.at[s] if i == 0 else items[i]
@@ -342,7 +347,10 @@
             R.ot[s, lo : lo + 64, :] = nn(vt, probs[h].astype(BF)).astype(BF)
             R.pt[s, h] = probs[h]
         need(s, 2)
-        rs_start(R_SA + s, tn(R.ot[s], R.wsa[s, 576:768, :]))
+        value = tn(R.ot[s], R.wsa[s, 576:768, :])
+        if s == 0:
+            enter()
+        rs_start(R_SA + s, value)
 
     def put_norm(slot, spread):
         R.sp[slot] = jnp.broadcast_to(spread, (SH, 128))
@@ -624,6 +632,8 @@
     def dev_c1(k):
         return dev_c
 
+    self_forward(0)
+    rest()
     for j in (10, 11, 12, 13, 14, 15):
         R.vec[j : j + 1, :] = jnp.zeros((1, D), F32)
 
@@ -639,7 +649,6 @@
     R.pos[0] = jnp.broadcast_to(at, (8, KEYS))
     for k in RINGS:
         push(R.pos.at[0], R.pos.at[k], R.m_dps.at[5 + k], R.m_kvr.at[5 + k], dev_q(k))
-    self_forward(0)
     self_finish(0)
     ag_wait(A_Y1)
     need(0, 5)
@@ -758,6 +767,7 @@
     ag_start(A_DR1 + 1, dr)
     R.dres[1] = dr
     vec_put(4, dg, db)
+    g1b("ffd", (0,))
 
     def self_backward(s):
         ag_wait(A_DR1 + s)
@@ -798,7 +808,7 @@
         R.dks[to] = (R.dkf[to] + nt(R.dkr[1], hot)).astype(BF)
         if k:
             push(R.dks.at[to], R.dk2.at[k - 1], R.m_dps.at[2 + k], R.m_dkr.at[2 + k], dev_p(k))
-    g1b("ffd")
+    g1b("ffd", (1,))
     self_backward(1)
     input_part(1)
     self_grads(1, "sad")
@@ -845,9 +855,9 @@
     R.dres[0] = dr
     vec_put(0, dg, db)
     g1("ffi")
-    g2("crx", (1,))
     g4b("ffd")
     g4("crx", (0,))
+    g2("crx", (1,))
     g3("sad")
     g1b("ffo")
     self_backward(0)
@@ -875,11 +885,11 @@
     total = vec_sum(R.vy, y, 4, dev_y, 4)
     vec_send(R.vz, z, total, 7, dev_z, 4)
     g4("ffo")
+    g3("sae")
     g4b("crx", (1,))
-    g3("sae")
+    g4("ffi")
     g4("sae")
     g5("crx")
-    g4("ffi")
     ag_wait(A_IG)
     ag_wait(A_IG + 1)
     push(R.ag.at[A_IG + o], ig_o.at[c], R.m_hs.at[1], R.m_hr.at[1], dev_c)

time: 144 us -> 141 us (0.979)
  Pallas kernels: 143 us -> 140 us
    pallas_call x1, Pallas kernels: 139 us -> 135 us  [body(): pl.pallas_call(run, out_shape=outs, in_specs=[hbm, hbm, vm, vm, hbm, hbm,...]
where the time goes in v7:
time: 141 us
  Pallas kernels  140 us (99%)
    pallas_call x1, Pallas kernels, body(): pl.pallas_call(run, out_shape=outs, in_specs=[hbm, hbm, vm, vm, hbm, hbm,...  135 us
    pallas_call x1, Pallas kernels, body(): pl.pallas_call(widen, out_shape=wide_outs, in_specs=[vm] * 7, out_specs=[...  4.77 us

profile of v7, /device:TPU:0, one launch (start us, length us, event | category | flops | bytes accessed | tf_op | source)
XLA Modules:
  0.0 141.1 jit_solution(12795709609142611551)
XLA Ops:
  0.7 135.5 %layers.1 = (bf16[2,128,768]{2,1,0:T(8,128)(2,1)S(1)}, bf16[2,128,768]{2,1,0:T(8,128)(2,1)S(1)}, bf16[2,2,768,384]{3,2,1,0:T(8,128)(2,1)S(1)}, bf16[2,2,384,384]...) custom-call(bf16[2,128,768]{2,1,0:T(8,128)(2,1)} %bitcast.35, ...), custom_call_target="tpu_custom_call" | custom-call | tf_op jit(solution)/shard_map/layers/pallas_call | solution.py:1002
  136.1 4.8 %widen.1 = (bf16[2,128,768]{2,1,0:T(8,128)(2,1)}, f32[2,128,768]{2,1,0:T(8,128)}, f32[576,768]{1,0:T(8,128)}, f32[192,768]{1,0:T(8,128)}, f32[768,768]{1,0:T(8,1...) custom-call(bf16[2,128,768]{2,1,0:T(8,128)(2,1)S(1)} %get-tuple-elem, ...), custom_call_target="tpu_custom_call" | custom-call | tf_op jit(solution)/shard_map/widen/pallas_call | solution.py:1028

commit v8 on v7

--- a/solution.py
+++ b/solution.py
@@ -77,16 +77,16 @@
         ("dkvct", VMEM((2 * QW, KEYS), BF)),
         ("ptc", VMEM((NH, KEYS, TOK), F32)),
         ("oct", VMEM((QW, TOK), BF)),
-        ("pos", VMEM((4, 8, KEYS), jnp.int32)),
-        ("hot", VMEM((4, 4 * TOK, KEYS), BF)),
-        ("kvt", VMEM((4, 2 * QW, TOK), BF)),
-        ("kvf", VMEM((4, 2 * QW, KEYS), F32)),
-        ("kvs", VMEM((4, 2 * QW, KEYS), BF)),
-        ("kvr", VMEM((3, 2 * QW, KEYS), BF)),
-        ("dkr", VMEM((3, 2 * QW, KEYS), BF)),
-        ("dkf", VMEM((4, 2 * QW, TOK), F32)),
-        ("dks", VMEM((4, 2 * QW, TOK), BF)),
-        ("dk2", VMEM((3, 2 * QW, TOK), BF)),
+        ("pos", VMEM((2, 4, 8, KEYS), jnp.int32)),
+        ("hot", VMEM((2, 4, 4 * TOK, KEYS), BF)),
+        ("kvt", VMEM((2, 4, QW, TOK), BF)),
+        ("kvf", VMEM((2, 4, QW, KEYS), F32)),
+        ("kvs", VMEM((2, 4, QW, KEYS), BF)),
+        ("kvr", VMEM((2, 3, QW, KEYS), BF)),
+        ("dkr", VMEM((2, 3, QW, KEYS), BF)),
+        ("dkf", VMEM((2, 4, QW, TOK), F32)),
+        ("dks", VMEM((2, 4, QW, TOK), BF)),
+        ("dk2", VMEM((2, 3, QW, TOK), BF)),
         ("dkv", VMEM((2 * QW, TOK), BF)),
         ("vec", VMEM((16, D), F32)),
         ("vx", VMEM((4, 16, D), BF)),
@@ -103,9 +103,9 @@
         ("m_agr", DMA((2, 3))),
         ("m_rss", DMA((2, 3))),
         ("m_rsr", DMA((2, 3))),
-        ("m_dps", DMA((10,))),
-        ("m_kvr", DMA((9,))),
-        ("m_dkr", DMA((6,))),
+        ("m_dps", DMA((18,))),
+        ("m_kvr", DMA((18,))),
+        ("m_dkr", DMA((12,))),
         ("m_vr", DMA((10,))),
         ("m_hs", DMA((2,))),
         ("m_hr", DMA((3,))),
@@ -640,15 +640,19 @@
     micro = lax.broadcasted_iota(jnp.int32, (2, 16), 0)
     group = lax.broadcasted_iota(jnp.int32, (2, 16), 1)
     live = (micro == c) & (group <= d) & (dgr[...] > 0)
-    first = jnp.max(jnp.where(live, group, 0), axis=1, keepdims=True)
-    first = jnp.max(first, axis=0, keepdims=True)
-    rows = jnp.where(c == 0, ret[0], ret[1]) + first * TOK
+    start = jnp.max(jnp.where(live, group, 0), axis=1, keepdims=True)
+    start = jnp.max(start, axis=0, keepdims=True)
+    rows = jnp.where(c == 0, ret[0], ret[1]) + start * TOK
     g_at = rows // TOK
     b_at = jnp.where(c == 0, g_at, lax.rem(g_at, 4) * 4 + g_at // 4)
     at = b_at * TOK + lax.rem(rows, TOK)
-    R.pos[0] = jnp.broadcast_to(at, (8, KEYS))
-    for k in RINGS:
-        push(R.pos.at[0], R.pos.at[k], R.m_dps.at[5 + k], R.m_kvr.at[5 + k], dev_q(k))
+    first = (p, q)
+    dev_first, dev_second = (dev_p, dev_q), (dev_q, dev_p)
+    for u in (0, 1):
+        R.pos[u, 0] = jnp.broadcast_to(at, (8, KEYS))
+        for k in RINGS:
+            m = 3 * u + k - 1
+            push(R.pos.at[u, 0], R.pos.at[u, k], R.m_dps.at[m], R.m_kvr.at[m], dev_second[u](k))
     self_finish(0)
     ag_wait(A_Y1)
     need(0, 5)
@@ -657,14 +661,17 @@
 
     for cp in singles:
         cp.wait()
-    for k in (1, 3, 2):
-        landed(R.pos.at[k], R.m_kvr.at[5 + k], dev_q(k))
+    for u in (0, 1):
+        for k in (1, 3, 2):
+            landed(R.pos.at[u, k], R.m_kvr.at[3 * u + k - 1], dev_c)
 
     def build(i, carry):
-        n = lax.broadcasted_iota(jnp.int32, (TOK, KEYS), 0) + (q * 4 + i) * TOK
         rows = pl.ds(pl.multiple_of(i * TOK, TOK), TOK)
-        for k in range(4):
-            R.hot[k, rows, :] = jnp.where(n == R.pos[k, 0:1, :], 1.0, 0.0).astype(BF)
+        for u in (0, 1):
+            block = q * 4 + i if u == 0 else i * 4 + p
+            n = lax.broadcasted_iota(jnp.int32, (TOK, KEYS), 0) + block * TOK
+            for k in range(4):
+                R.hot[u, k, rows, :] = jnp.where(n == R.pos[u, k, 0:1, :], 1.0, 0.0).astype(BF)
         return carry
 
     lax.fori_loop(0, 4, build, 0)
@@ -674,41 +681,51 @@
     R.n2[0] = n
     put_norm(2, spread)
     ag_wait(A_BO)
-    R.kvt[p] = nt(R.wcr[384:768, :], R.ag[A_BO]).astype(BF)
-
-    for k in RINGS:
-        push(R.kvt.at[p], R.kvt.at[p], R.m_dps.at[k - 1], R.m_kvr.at[k - 1], dev_p(k))
-
-    def picked(k, j):
-        return nn(R.kvt[j], R.hot[k, pl.ds(pl.multiple_of(j * TOK, TOK), TOK), :])
-
+
+    def hot(u, k, j):
+        return R.hot[u, k, pl.ds(pl.multiple_of(j * TOK, TOK), TOK), :]
+
+    def picked(u, k, j):
+        return nn(R.kvt[u, j], hot(u, k, j))
+
+    for u in (0, 1):
+        R.kvt[u, first[u]] = nt(R.wcr[384 + u * QW : 384 + u * QW + QW, :], R.ag[A_BO]).astype(BF)
+        for k in RINGS:
+            part, m = R.kvt.at[u, first[u]], 6 + 3 * u + k - 1
+            push(part, part, R.m_dps.at[m], R.m_kvr.at[m], dev_first[u](k))
     self_forward(1)
-    for k in range(4):
-        R.kvf[k] = picked(k, p)
-    for j in (1, 3):
-        landed(R.kvt.at[p], R.m_kvr.at[j - 1], dev_p(j))
+    for u in (0, 1):
         for k in range(4):
-            R.kvf[k] += picked(k, lax.rem(p + 4 - j, 4))
-    landed(R.kvt.at[p], R.m_kvr.at[1], dev_p(2))
-    for k in RINGS + (0,):
-        R.kvs[k] = (R.kvf[k] + picked(k, lax.rem(p + 2, 4))).astype(BF)
-        if k:
-            push(
-                R.kvs.at[k], R.kvr.at[3 - k], R.m_dps.at[6 - k], R.m_kvr.at[6 - k], dev_q(4 - k)
-            )
+            R.kvf[u, k] = picked(u, k, first[u])
+    for u in (0, 1):
+        for j in (1, 3):
+            landed(R.kvt.at[u, 0], R.m_kvr.at[6 + 3 * u + j - 1], dev_c)
+            for k in range(4):
+                R.kvf[u, k] += picked(u, k, lax.rem(first[u] + 4 - j, 4))
+        landed(R.kvt.at[u, 0], R.m_kvr.at[6 + 3 * u + 1], dev_c)
+        for k in RINGS + (0,):
+            R.kvs[u, k] = (R.kvf[u, k] + picked(u, k, lax.rem(first[u] + 2, 4))).astype(BF)
+            if k:
+                m = 12 + 3 * u + 3 - k
+                dst = R.kvr.at[u, 3 - k]
+                push(R.kvs.at[u, k], dst, R.m_dps.at[m], R.m_kvr.at[m], dev_second[u](4 - k))
     self_finish(1)
     ag_wait(A_Y1 + 1)
     R.qct[...] = nt(R.wcr[0:192, :], R.ag[A_Y1 + 1]).astype(BF)
-    for k in (1, 3, 2):
-        landed(R.kvr.at[k - 1], R.m_kvr.at[2 + k], dev_q(k))
-
-    total = R.kvs[0].astype(F32)
-    for k in range(3):
-        total += R.kvr[k].astype(F32)
-    R.kvct[...] = total.astype(BF)
+
+    def chosen(u):
+        for k in (1, 3, 2):
+            landed(R.kvr.at[u, k - 1], R.m_kvr.at[12 + 3 * u + k - 1], dev_c)
+        total = R.kvs[u, 0].astype(F32)
+        for k in range(3):
+            total += R.kvr[u, k].astype(F32)
+        R.kvct[u * QW : u * QW + QW, :] = total.astype(BF)
+
+    chosen(0)
     probs = softmax(
         [tn(R.kvct[lo : lo + 64, :], R.qct[lo : lo + 64, :]) * SCALE for lo in HEADS]
     )
+    chosen(1)
     for h, lo in enumerate(HEADS):
         vt = R.kvct[QW + lo : QW + lo + 64, :]
         R.oct[lo : lo + 64, :] = nn(vt, probs[h].astype(BF)).astype(BF)
@@ -743,21 +760,28 @@
     g1("ffd")
     ag_wait(A_DRC)
 
+    def compact(u):
+        for k in RINGS:
+            m = 3 * u + k - 1
+            part = R.dkvct.at[pl.ds(u * QW, QW)]
+            push(part, R.dkr.at[u, k - 1], R.m_dps.at[m], R.m_dkr.at[m], dev_second[u](k))
+
     doc = nt(R.wcr[192:384, :], R.ag[A_DRC]).astype(BF)
-    dqts, dkts, dvts = attend_backward(
-        [R.qct[lo : lo + 64, :] for lo in HEADS],
-        [R.kvct[lo : lo + 64, :] for lo in HEADS],
-        [R.kvct[QW + lo : QW + lo + 64, :] for lo in HEADS],
-        [R.ptc[h] for h in range(NH)],
-        [doc[lo : lo + 64, :] for lo in HEADS],
-    )
-    for h, lo in enumerate(HEADS):
-        R.dkvct[lo : lo + 64, :] = dkts[h].astype(BF)
-        R.dkvct[QW + lo : QW + lo + 64, :] = dvts[h].astype(BF)
-        R.dqct[lo : lo + 64, :] = dqts[h].astype(BF)
-
-    for k in RINGS:
-        push(R.dkvct, R.dkr.at[k - 1], R.m_dps.at[k - 1], R.m_dkr.at[k - 1], dev_q(k))
+    heads = list(enumerate(HEADS))
+    for h, lo in heads:
+        dvt = nt(doc[lo : lo + 64, :], R.ptc[h].astype(BF))
+        R.dkvct[QW + lo : QW + lo + 64, :] = dvt.astype(BF)
+    compact(1)
+    dpts = [tn(R.kvct[QW + lo : QW + lo + 64, :], doc[lo : lo + 64, :]) for h, lo in heads]
+    sums = [jnp.sum(dpts[h] * R.ptc[h], axis=0, keepdims=True) for h, lo in heads]
+    dsts = [(R.ptc[h] * (dpts[h] - sums[h])).astype(BF) for h, lo in heads]
+    for h, lo in heads:
+        dkt = nt(R.qct[lo : lo + 64, :], dsts[h]) * SCALE
+        R.dkvct[lo : lo + 64, :] = dkt.astype(BF)
+    compact(0)
+    for h, lo in heads:
+        dqt = nn(R.kvct[lo : lo + 64, :], dsts[h]) * SCALE
+        R.dqct[lo : lo + 64, :] = dqt.astype(BF)
     rs_start(R_DQ, tn(R.dqct[...], R.wcr[0:192, :]))
     put(R.g_crx, 0, 0, nn(R.dqct[...], R.ag[A_Y1 + 1]))
     put(R.g_crx, 0, 192, nn(R.oct[...], R.ag[A_DRC]))
@@ -795,30 +819,34 @@
     def input_part(s):
         rs_start(R_DSA + s, tn(R.dpk[s], R.wsa[s, 0:576, :]))
 
-    for j in range(4):
-        R.dkf[j] = nt(R.dkvct[...], R.hot[0, j * TOK : (j + 1) * TOK, :])
-    for k in (1, 3):
-        landed(R.dkr.at[k - 1], R.m_dkr.at[k - 1], dev_q(k))
+    for u in (1, 0):
         for j in range(4):
-            R.dkf[j] += nt(R.dkr[k - 1], R.hot[k, j * TOK : (j + 1) * TOK, :])
-    landed(R.dkr.at[1], R.m_dkr.at[1], dev_q(2))
-    for k in RINGS + (0,):
-        to = lax.rem(p + k, 4)
-        hot = R.hot[2, pl.ds(pl.multiple_of(to * TOK, TOK), TOK), :]
-        R.dks[to] = (R.dkf[to] + nt(R.dkr[1], hot)).astype(BF)
-        if k:
-            push(R.dks.at[to], R.dk2.at[k - 1], R.m_dps.at[2 + k], R.m_dkr.at[2 + k], dev_p(k))
+            R.dkf[u, j] = nt(R.dkvct[u * QW : u * QW + QW, :], hot(u, 0, j))
+    for u in (1, 0):
+        for k in (1, 3):
+            landed(R.dkr.at[u, k - 1], R.m_dkr.at[3 * u + k - 1], dev_c)
+            for j in range(4):
+                R.dkf[u, j] += nt(R.dkr[u, k - 1], hot(u, k, j))
+        landed(R.dkr.at[u, 1], R.m_dkr.at[3 * u + 1], dev_c)
+        for k in RINGS + (0,):
+            to = lax.rem(first[u] + k, 4)
+            R.dks[u, to] = (R.dkf[u, to] + nt(R.dkr[u, 1], hot(u, 2, to))).astype(BF)
+            if k:
+                m = 6 + 3 * u + k - 1
+                dst = R.dk2.at[u, k - 1]
+                push(R.dks.at[u, to], dst, R.m_dps.at[m], R.m_dkr.at[m], dev_first[u](k))
     g1b("ffd", (1,))
     self_backward(1)
     input_part(1)
     self_grads(1, "sad")
     g1("crx", (0,))
-    for k in (1, 3, 2):
-        landed(R.dk2.at[k - 1], R.m_dkr.at[2 + k], dev_p(k))
-    total = R.dks[p].astype(F32)
-    for k in range(3):
-        total += R.dk2[k].astype(F32)
-    R.dkv[...] = total.astype(BF)
+    for u in (1, 0):
+        for k in (1, 3, 2):
+            landed(R.dk2.at[u, k - 1], R.m_dkr.at[6 + 3 * u + k - 1], dev_c)
+        total = R.dks[u, first[u]].astype(F32)
+        for k in range(3):
+            total += R.dk2[u, k].astype(F32)
+        R.dkv[u * QW : u * QW + QW, :] = total.astype(BF)
     rs_start(R_DST, tn(R.dkv[...], R.wcr[384:768, :]))
     put(R.g_crx, 1, 0, nn(R.dkv[...], R.ag[A_BO]))
     g0("crx", (1,))
@@ -880,12 +908,12 @@
     g3("ffo")
     g2("sae")
     g4("crx", (1,))
-    g4b("sad")
     g3("ffi")
     total = vec_sum(R.vy, y, 4, dev_y, 4)
     vec_send(R.vz, z, total, 7, dev_z, 4)
     g4("ffo")
     g3("sae")
+    g4b("sad")
     g4b("crx", (1,))
     g4("ffi")
     g4("sae")

time: 141 us -> 139 us (0.986)
  Pallas kernels: 140 us -> 138 us
    pallas_call x1, Pallas kernels: 135 us -> 133 us  [body(): pl.pallas_call(run, out_shape=outs, in_specs=[hbm, hbm, vm, vm, hbm, hbm,...]
where the time goes in v8:
time: 139 us
  Pallas kernels  138 us (99%)
    pallas_call x1, Pallas kernels, body(): pl.pallas_call(run, out_shape=outs, in_specs=[hbm, hbm, vm, vm, hbm, hbm,...  133 us
    pallas_call x1, Pallas kernels, body(): pl.pallas_call(widen, out_shape=wide_outs, in_specs=[vm] * 7, out_specs=[...  4.77 us

profile of v8, /device:TPU:0, one launch (start us, length us, event | category | flops | bytes accessed | tf_op | source)
XLA Modules:
  0.0 138.7 jit_solution(14234667261219519050)
XLA Ops:
  0.7 133.2 %layers.1 = (bf16[2,128,768]{2,1,0:T(8,128)(2,1)S(1)}, bf16[2,128,768]{2,1,0:T(8,128)(2,1)S(1)}, bf16[2,2,768,384]{3,2,1,0:T(8,128)(2,1)S(1)}, bf16[2,2,384,384]...) custom-call(bf16[2,128,768]{2,1,0:T(8,128)(2,1)} %bitcast.35, ...), custom_call_target="tpu_custom_call" | custom-call | tf_op jit(solution)/shard_map/layers/pallas_call | solution.py:1030
  133.8 4.8 %widen.1 = (bf16[2,128,768]{2,1,0:T(8,128)(2,1)}, f32[2,128,768]{2,1,0:T(8,128)}, f32[576,768]{1,0:T(8,128)}, f32[192,768]{1,0:T(8,128)}, f32[768,768]{1,0:T(8,1...) custom-call(bf16[2,128,768]{2,1,0:T(8,128)(2,1)S(1)} %get-tuple-elem, ...), custom_call_target="tpu_custom_call" | custom-call | tf_op jit(solution)/shard_map/widen/pallas_call | solution.py:1056

commit v9 on v8

--- a/solution.py
+++ b/solution.py
@@ -220,16 +220,6 @@
         ]
 
     items = [x_h.at[c], qkv_h, out_h, ng_h, nb_h, win_h, wfo_h]
-    bar = pltpu.get_barrier_semaphore()
-    peers = [dev_c]
-    for k in (1, 2, 3):
-        for dev in (dev_x(k), dev_y(k), dev_z(k)):
-            peers.append(dev)
-    for k in (1, 2, 3):
-        peers.append((o,) + dev_y(k)[1:])
-        peers.append((o,) + dev_z(k)[1:])
-    for dev in peers:
-        pl.semaphore_signal(bar, inc=1, device_id=dev, device_id_type=MESH)
 
     def own(i):
         pltpu.make_async_copy(items[i], places(c)[i], R.m_w.at[c, i]).start()
@@ -238,7 +228,23 @@
         src = x_h.at[o] if i == 0 else items[i]
         push(src, places(c)[i], R.m_ws.at[i], R.m_w.at[c, i], dev_c)
 
-    for i in range(5):
+    for i in range(3):
+        own(i)
+    bar = pltpu.get_barrier_semaphore()
+    peers = [dev_c] + [dev(k) for k in (1, 2, 3) for dev in (dev_x, dev_y, dev_z)]
+    across = [(o,) + dev(k)[1:] for k in (1, 2, 3) for dev in (dev_y, dev_z)]
+
+    def greet(devices):
+        for dev in devices:
+            pl.semaphore_signal(bar, inc=1, device_id=dev, device_id_type=MESH)
+
+    greet(peers)
+
+    @pl.when(c == 0)
+    def _():
+        greet(across)
+
+    for i in (3, 4):
         own(i)
     singles = [
         pltpu.make_async_copy(cq_h, R.wcr.at[pl.ds(0, 192)], R.m_l.at[0]),
@@ -246,8 +252,9 @@
         pltpu.make_async_copy(ckv_h, R.wcr.at[pl.ds(384, 384)], R.m_l.at[2]),
         pltpu.make_async_copy(cot_h.at[c], R.cot, R.m_l.at[3]),
     ]
+
     def enter():
-        pl.semaphore_wait(bar, len(peers))
+        pl.semaphore_wait(bar, len(peers) + c * len(across))
         for i in range(3):
             other(i)
 
@@ -680,6 +687,7 @@
     ag_start(A_BO, out)
     R.n2[0] = n
     put_norm(2, spread)
+    self_forward(1)
     ag_wait(A_BO)
 
     def hot(u, k, j):
@@ -693,7 +701,7 @@
         for k in RINGS:
             part, m = R.kvt.at[u, first[u]], 6 + 3 * u + k - 1
             push(part, part, R.m_dps.at[m], R.m_kvr.at[m], dev_first[u](k))
-    self_forward(1)
+    self_finish(1)
     for u in (0, 1):
         for k in range(4):
             R.kvf[u, k] = picked(u, k, first[u])
@@ -709,7 +717,6 @@
                 m = 12 + 3 * u + 3 - k
                 dst = R.kvr.at[u, 3 - k]
                 push(R.kvs.at[u, k], dst, R.m_dps.at[m], R.m_kvr.at[m], dev_second[u](4 - k))
-    self_finish(1)
     ag_wait(A_Y1 + 1)
     R.qct[...] = nt(R.wcr[0:192, :], R.ag[A_Y1 + 1]).astype(BF)
 
@@ -750,8 +757,9 @@
     ag_start(A_BO + 1, out)
     flush("")
     put(R.g_ffd, 0, 0, in_grad(1, A_Y2))
+    g0("ffd", (0,))
     put(R.g_ffd, 1, 0, out_grad(1))
-    g0("ffd")
+    g0("ffd", (1,))
     dy = R.dres[1] + rs_sum(R_DFF + 1)
     dr, dg, db = ln_backward(R.nc[...], get_norm(4), cross_gain, dy)
     ag_start(A_DRC, dr)

time: 139 us -> 138 us (level)
  no operation moved by 1% of the time
where the time goes in v9:
time: 138 us
  Pallas kernels  137 us (99%)
    pallas_call x1, Pallas kernels, body(): pl.pallas_call(run, out_shape=outs, in_specs=[hbm, hbm, vm, vm, hbm, hbm,...  132 us
    pallas_call x1, Pallas kernels, body(): pl.pallas_call(widen, out_shape=wide_outs, in_specs=[vm] * 7, out_specs=[...  4.77 us

profile of v9, /device:TPU:0, one launch (start us, length us, event | category | flops | bytes accessed | tf_op | source)
XLA Modules:
  0.0 137.9 jit_solution(5648028116900038224)
XLA Ops:
  0.7 132.3 %layers.1 = (bf16[2,128,768]{2,1,0:T(8,128)(2,1)S(1)}, bf16[2,128,768]{2,1,0:T(8,128)(2,1)S(1)}, bf16[2,2,768,384]{3,2,1,0:T(8,128)(2,1)S(1)}, bf16[2,2,384,384]...) custom-call(bf16[2,128,768]{2,1,0:T(8,128)(2,1)} %bitcast.35, ...), custom_call_target="tpu_custom_call" | custom-call | tf_op jit(solution)/shard_map/layers/pallas_call | solution.py:1038
  133.0 4.8 %widen.1 = (bf16[2,128,768]{2,1,0:T(8,128)(2,1)}, f32[2,128,768]{2,1,0:T(8,128)}, f32[576,768]{1,0:T(8,128)}, f32[192,768]{1,0:T(8,128)}, f32[768,768]{1,0:T(8,1...) custom-call(bf16[2,128,768]{2,1,0:T(8,128)(2,1)S(1)} %get-tuple-elem, ...), custom_call_target="tpu_custom_call" | custom-call | tf_op jit(solution)/shard_map/widen/pallas_call | solution.py:1064

commit v10 on v9

--- a/solution.py
+++ b/solution.py
@@ -105,8 +105,6 @@
         ("m_rsr", DMA((2, 3))),
         ("m_dps", DMA((18,))),
         ("m_kvr", DMA((18,))),
-        ("m_dkr", DMA((12,))),
-        ("m_vr", DMA((10,))),
         ("m_hs", DMA((2,))),
         ("m_hr", DMA((3,))),
         ("m_g0", DMA((len(BLOCKS), 2))),
@@ -126,7 +124,7 @@
         ]
     for group in sorted(set(GROUP.values())):
         out.append(("s_" + group, DMA((2, 4 if group == GROUP["sae"] else 3))))
-        out.append(("r_" + group, DMA((2, 9 if group == GROUP["sae"] else 11))))
+        out.append(("r_" + group, DMA((2, 8 if group == GROUP["sae"] else 10))))
     return out
 
 
@@ -545,7 +543,7 @@
                 part[...] = total.astype(BF)
                 for k in RINGS:
                     gone(b.at[i, k - 1], s.at[i, k - 1])
-                    ship(part, part, s.at[i, k - 1], r.at[i, (3, 4, 8)[k - 1]], devs[i][1](k))
+                    ship(part, part, s.at[i, k - 1], r.at[i, (3, 4, 0)[k - 1]], devs[i][1](k))
 
     def g4(name, pieces=(0, 1)):
         g, x, h, a, b, s, r = blk(name)
@@ -556,7 +554,7 @@
                 mine = quarter(name, place[i][0])
                 part = spot(name, i, mine)
                 for k in () if name in WHOLE else (1, 3, 2):
-                    landed(b.at[i, k - 1], r.at[i, (3, 4, 8)[k - 1]], dev_c)
+                    landed(b.at[i, k - 1], r.at[i, (3, 4, 0)[k - 1]], dev_c)
                     gone(b.at[i, k - 1], s.at[i, k - 1])
                 if name == "sae":
                     dst = result(name, i, mine)
@@ -580,7 +578,7 @@
                     gone(a.at[i, j], s.at[i, j])
                     rows = eighth(name, behind, j)
                     part = spot(name, i, rows)
-                    ship(part, part, s.at[i, j], r.at[i, 9 + j], devs[i][0](k))
+                    ship(part, part, s.at[i, j], r.at[i, 8 + j], devs[i][0](k))
 
     def g5(name):
         g, x, h, a, b, s, r = blk(name)
@@ -589,7 +587,7 @@
         def _():
             for i in (0, 1):
                 for j in (0, 1):
-                    landed(h.at[i, j], r.at[i, 9 + j], dev_c)
+                    landed(h.at[i, j], r.at[i, 8 + j], dev_c)
             if name == "crx":
                 ship(oc_o, oc_o, s.at[0, 2], R.m_hr.at[2], dev_c)
 
@@ -626,11 +624,11 @@
     def vec_send(buf, at, value, base, dev, count):
         buf[at] = value.astype(BF)
         for k in range(1, count):
-            push(buf.at[at], buf.at[at], R.m_dps.at[base + k - 1], R.m_vr.at[base + k - 1], dev(k))
+            push(buf.at[at], buf.at[at], R.m_dps.at[base + k - 1], R.m_kvr.at[base + k - 1], dev(k))
 
     def vec_sum(buf, at, base, dev, count):
         for k in range(1, count):
-            landed(buf.at[at], R.m_vr.at[base + k - 1], dev(k))
+            landed(buf.at[at], R.m_kvr.at[base + k - 1], dev(k))
         total = buf[0].astype(F32)
         for k in range(1, count):
             total += buf[k].astype(F32)
@@ -772,7 +770,7 @@
         for k in RINGS:
             m = 3 * u + k - 1
             part = R.dkvct.at[pl.ds(u * QW, QW)]
-            push(part, R.dkr.at[u, k - 1], R.m_dps.at[m], R.m_dkr.at[m], dev_second[u](k))
+            push(part, R.dkr.at[u, k - 1], R.m_dps.at[m], R.m_kvr.at[m], dev_second[u](k))
 
     doc = nt(R.wcr[192:384, :], R.ag[A_DRC]).astype(BF)
     heads = list(enumerate(HEADS))
@@ -832,17 +830,17 @@
             R.dkf[u, j] = nt(R.dkvct[u * QW : u * QW + QW, :], hot(u, 0, j))
     for u in (1, 0):
         for k in (1, 3):
-            landed(R.dkr.at[u, k - 1], R.m_dkr.at[3 * u + k - 1], dev_c)
+            landed(R.dkr.at[u, k - 1], R.m_kvr.at[3 * u + k - 1], dev_c)
             for j in range(4):
                 R.dkf[u, j] += nt(R.dkr[u, k - 1], hot(u, k, j))
-        landed(R.dkr.at[u, 1], R.m_dkr.at[3 * u + 1], dev_c)
+        landed(R.dkr.at[u, 1], R.m_kvr.at[3 * u + 1], dev_c)
         for k in RINGS + (0,):
             to = lax.rem(first[u] + k, 4)
             R.dks[u, to] = (R.dkf[u, to] + nt(R.dkr[u, 1], hot(u, 2, to))).astype(BF)
             if k:
-                m = 6 + 3 * u + k - 1
+                m = 6 + 3 * (1 - u) + k - 1
                 dst = R.dk2.at[u, k - 1]
-                push(R.dks.at[u, to], dst, R.m_dps.at[m], R.m_dkr.at[m], dev_first[u](k))
+                push(R.dks.at[u, to], dst, R.m_dps.at[m], R.m_kvr.at[m], dev_first[u](k))
     g1b("ffd", (1,))
     self_backward(1)
     input_part(1)
@@ -850,7 +848,7 @@
     g1("crx", (0,))
     for u in (1, 0):
         for k in (1, 3, 2):
-            landed(R.dk2.at[u, k - 1], R.m_dkr.at[6 + 3 * u + k - 1], dev_c)
+            landed(R.dk2.at[u, k - 1], R.m_kvr.at[6 + 3 * (1 - u) + k - 1], dev_c)
         total = R.dks[u, first[u]].astype(F32)
         for k in range(3):
             total += R.dk2[u, k].astype(F32)
@@ -911,14 +909,14 @@
     g4("sad")
     g2("ffi")
     total = vec_sum(R.vc, c, 3, dev_c1, 2)
-    vec_send(R.vy, y, total, 4, dev_y, 4)
+    vec_send(R.vy, y, total, 12, dev_y, 4)
     ag_start(A_IG, R.dres[0] + rs_sum(R_DSA))
     g3("ffo")
     g2("sae")
     g4("crx", (1,))
     g3("ffi")
-    total = vec_sum(R.vy, y, 4, dev_y, 4)
-    vec_send(R.vz, z, total, 7, dev_z, 4)
+    total = vec_sum(R.vy, y, 12, dev_y, 4)
+    vec_send(R.vz, z, total, 15, dev_z, 4)
     g4("ffo")
     g3("sae")
     g4b("sad")
@@ -932,7 +930,7 @@
     outs.append(pltpu.make_async_copy(R.ag.at[A_IG + c], ig_o.at[c], R.m_o.at[1]))
     outs[1].start()
     g4b("ffo")
-    total = vec_sum(R.vz, z, 7, dev_z, 4)
+    total = vec_sum(R.vz, z, 15, dev_z, 4)
     on_o[...] = jnp.where(c == 0, total[0:4, :], total[4:8, :])
     oe_o[...] = total[8:10, :]
     flush("")

time: 138 us -> 138 us (level)
  no operation moved by 1% of the time
where the time goes in v10:
time: 138 us
  Pallas kernels  137 us (99%)
    pallas_call x1, Pallas kernels, body(): pl.pallas_call(run, out_shape=outs, in_specs=[hbm, hbm, vm, vm, hbm, hbm,...  132 us
    pallas_call x1, Pallas kernels, body(): pl.pallas_call(widen, out_shape=wide_outs, in_specs=[vm] * 7, out_specs=[...  4.77 us

profile of v10, /device:TPU:0, one launch (start us, length us, event | category | flops | bytes accessed | tf_op | source)
XLA Modules:
  0.0 137.7 jit_solution(15132666602143144859)
XLA Ops:
  0.7 132.1 %layers.1 = (bf16[2,128,768]{2,1,0:T(8,128)(2,1)S(1)}, bf16[2,128,768]{2,1,0:T(8,128)(2,1)S(1)}, bf16[2,2,768,384]{3,2,1,0:T(8,128)(2,1)S(1)}, bf16[2,2,384,384]...) custom-call(bf16[2,128,768]{2,1,0:T(8,128)(2,1)} %bitcast.35, ...), custom_call_target="tpu_custom_call" | custom-call | tf_op jit(solution)/shard_map/layers/pallas_call | solution.py:1036
  132.7 4.8 %widen.1 = (bf16[2,128,768]{2,1,0:T(8,128)(2,1)}, f32[2,128,768]{2,1,0:T(8,128)}, f32[576,768]{1,0:T(8,128)}, f32[192,768]{1,0:T(8,128)}, f32[768,768]{1,0:T(8,1...) custom-call(bf16[2,128,768]{2,1,0:T(8,128)(2,1)S(1)} %get-tuple-elem, ...), custom_call_target="tpu_custom_call" | custom-call | tf_op jit(solution)/shard_map/widen/pallas_call | solution.py:1062
